TPU v7x, 128 devices: a whole 4x4x4 slice. The times are simulated.
128 devices in a mesh: gx: 16 (over z, y), gy: 8 (over x, core).
Axes of the slice: x: 4, y: 4, z: 4, core: 2. Of those that a mesh axis runs over, the one named last changes fastest.
Arguments:
- tokens: bfloat16 [512, 8192], P('gy', 'gx'), may hold values from -400 to 400
- w_query: bfloat16 [8192, 8192], P('gx', 'gy'), may hold values from -0.0625 to 0.0625
- w_key_value: bfloat16 [8192, 512], P('gx', 'gy'), may hold values from -0.0625 to 0.0625
- w_gate: bfloat16 [8192, 32768], P('gx', 'gy'), may hold values from -0.0625 to 0.0625
- w_up: bfloat16 [8192, 32768], P('gx', 'gy'), may hold values from -0.0625 to 0.0625
- w_attn_out: bfloat16 [8192, 8192], P('gy', 'gx'), may hold values from -0.75 to 0.75
- w_down: bfloat16 [32768, 8192], P('gy', 'gx'), may hold values from -0.03125 to 0.03125
- key_cache: bfloat16 [512, 2048, 256], P(('gx', 'gy')), may hold values from -1000 to 1000
- value_cache: bfloat16 [512, 2048, 256], P(('gx', 'gy')), may hold values from -6 to 6
Outputs:
- layer_out: bfloat16 [512, 8192], P('gy', 'gx')
- new_kv: bfloat16 [512, 512], P(('gx', 'gy'))
All inputs are finite; a program needn't handle non-finite values.
Results may differ from a plain program's by a relative error of at most 0.035.
Values may be sent and summed in bfloat16 or wider, within the bound.
No kernel may reach another device: no remote copies, remote signals or barrier semaphores. Data moves between devices by JAX's collectives and lax.ppermute only.
A program may use at most 128 MiB of HBM per device.

v0:
```python
import jax
import jax.numpy as jnp
from jax import lax
from jax.sharding import PartitionSpec as P

D = 8192
HEADS = 32
HD = 256


def rotate(values, cos_part, sin_part):
    half = values.shape[-1] // 2
    first = values[..., :half]
    second = values[..., half:]
    return jnp.concatenate(
        [first * cos_part - second * sin_part, first * sin_part + second * cos_part], axis=-1
    )


def width_total(values):
    return lax.psum(values, "gx")


def normalize(rows):
    values = rows.astype(jnp.float32)
    mean = width_total(jnp.sum(values, axis=1)) / D
    centered = values - mean[:, None]
    spread = width_total(jnp.sum(centered * centered, axis=1)) / D
    return (centered * lax.rsqrt(spread + 1e-05)[:, None]).astype(jnp.bfloat16)


def local(tokens, w_query, w_key_value, w_gate, w_up, w_attn_out, w_down, key_cache, value_cache):
    count_gx = lax.axis_size("gx")
    count_gy = lax.axis_size("gy")
    source = normalize(tokens)
    gathered = lax.all_gather(source, "gy", axis=0, tiled=True)
    all_rows = gathered.shape[0]
    rows_dev = all_rows // (count_gx * count_gy)
    q_cols = w_query.shape[1]
    att_cols = q_cols + w_key_value.shape[1]
    hid = w_gate.shape[1]
    summed = lax.psum_scatter(
        jnp.concatenate(
            [
                jnp.dot(gathered, w_query, preferred_element_type=jnp.float32),
                jnp.dot(gathered, w_key_value, preferred_element_type=jnp.float32),
                jnp.dot(gathered, w_gate, preferred_element_type=jnp.float32),
                jnp.dot(gathered, w_up, preferred_element_type=jnp.float32),
            ],
            axis=1,
        ).astype(jnp.bfloat16),
        "gx",
        scatter_dimension=0,
        tiled=True,
    ).astype(jnp.float32)
    att_local = summed[:, :att_cols].astype(jnp.bfloat16)
    gate_sum = summed[:, att_cols : att_cols + hid]
    up_sum = summed[:, att_cols + hid :]
    swapped = lax.all_to_all(att_local, "gy", split_axis=0, concat_axis=1, tiled=True)
    per_row = swapped.reshape(rows_dev, count_gy, att_cols)
    hidden = (jax.nn.silu(gate_sum) * up_sum).astype(jnp.bfloat16)
    queries = per_row[:, :, :q_cols].reshape(rows_dev, HEADS, HD)
    keyval = per_row[:, :, q_cols:].reshape(rows_dev, 2 * HD)
    new_value = keyval[:, HD:]
    half = HD // 2
    freqs = 10000.0 ** (-jnp.arange(half, dtype=jnp.float32) / half)
    angles = jnp.float32(key_cache.shape[1]) * freqs
    cos_part = jnp.cos(angles)
    sin_part = jnp.sin(angles)
    qrot = (rotate(queries.astype(jnp.float32), cos_part, sin_part) * HD ** (-0.5)).astype(
        jnp.bfloat16
    )
    krot = rotate(keyval[:, :HD].astype(jnp.float32), cos_part, sin_part).astype(jnp.bfloat16)
    new_kv = jnp.concatenate([krot, new_value], axis=1)
    scores = jnp.einsum("rhd,rtd->rht", qrot, key_cache, preferred_element_type=jnp.float32)
    own = jnp.einsum("rhd,rd->rh", qrot, krot, preferred_element_type=jnp.float32)
    top = jnp.maximum(jnp.max(scores, axis=2), own)
    weights = jnp.exp(scores - top[:, :, None])
    own_w = jnp.exp(own - top)
    total = jnp.sum(weights, axis=2) + own_w
    probs = (weights / total[:, :, None]).astype(jnp.bfloat16)
    own_p = (own_w / total).astype(jnp.bfloat16)
    mixed = jnp.einsum("rht,rtd->rhd", probs, value_cache, preferred_element_type=jnp.float32)
    mixed = (
        mixed + own_p.astype(jnp.float32)[:, :, None] * new_value.astype(jnp.float32)[:, None, :]
    )
    attended = mixed.reshape(rows_dev, HEADS * HD).astype(jnp.bfloat16)
    back = lax.all_to_all(attended, "gy", split_axis=1, concat_axis=0, tiled=True)
    joined = jnp.concatenate([back, hidden], axis=1)
    head_cols = back.shape[1]
    piece = lax.all_gather(joined, "gx", axis=0, tiled=True)
    result = jnp.dot(piece[:, :head_cols], w_attn_out, preferred_element_type=jnp.float32)
    terms = result + jnp.dot(piece[:, head_cols:], w_down, preferred_element_type=jnp.float32)
    branch = lax.psum_scatter(
        terms.astype(jnp.bfloat16), "gy", scatter_dimension=0, tiled=True
    ).astype(jnp.float32)
    layer_out = (tokens.astype(jnp.float32) + branch).astype(jnp.bfloat16)
    return (layer_out, new_kv)


def solution(mesh):
    return jax.shard_map(
        local,
        mesh=mesh,
        in_specs=(
            P("gy", "gx"),
            P("gx", "gy"),
            P("gx", "gy"),
            P("gx", "gy"),
            P("gx", "gy"),
            P("gy", "gx"),
            P("gy", "gx"),
            P(("gx", "gy"), None, None),
            P(("gx", "gy"), None, None),
        ),
        out_specs=(P("gy", "gx"), P(("gx", "gy"), None)),
        check_vma=False,
    )
```

profile of v0, /device:TPU:0, one launch (start us, length us, event | category | flops | bytes accessed | tf_op | source)
XLA Modules:
  0.0 345.3 jit_solution(1699700841087268472)
XLA Ops:
  7.2 1.0 convert_reduce_fusion
  8.3 42.0 %psum.14 = f32[64]{0:T(128)S(1)} all-reduce(f32[64]{0:T(128)S(1)} %convert_reduce_fusion), channel_id=1, replica_groups=mesh['gx'=16,'gy'=8] {'gx'}, use_global_device_ids=true, to_apply=%region_1.0 | all-reduce | flops 64 | bytes 512 | tf_op jit(solution)/shard_map/psum | solution.py:21
  50.3 1.0 fusion.11
  51.3 35.5 %psum.15 = f32[64]{0:T(128)S(1)} all-reduce(f32[64]{0:T(128)S(1)} %fusion.11), channel_id=1, replica_groups=mesh['gx'=16,'gy'=8] {'gx'}, use_global_device_ids=true, to_apply=%region_3.0 | all-reduce | flops 64 | bytes 512 | tf_op jit(solution)/shard_map/psum | solution.py:21
  86.8 0.9 fusion.12
  87.7 13.5 %all_gather.6 = bf16[512,512]{1,0:T(8,128)(2,1)S(1)} all-gather(bf16[64,512]{1,0:T(8,128)(2,1)S(1)} %fusion.12), channel_id=1, replica_groups=mesh['gx'=16,'gy'=8] {'gy'}, dimensions={0}, use_global_device_ids=true | all-gather | bytes 589824 | tf_op jit(solution)/shard_map/all_gather | solution.py:36
  101.2 6.6 %convolution_convert_fusion = bf16[512,4096]{1,0:T(8,128)(2,1)} fusion(bf16[512,512]{1,0:T(8,128)(2,1)S(1)} %all_gather.6, bf16[512,4096]{1,0:T(8,128)(2,1)} %param.13), kind=kOutput, calls=%fused_computation | convolution fusion | flops 2149580800 | bytes 8912896 | tf_op jit(solution)/shard_map/dot_general | solution.py:48
  107.8 4.4 %convolution_convert_fusion.1 = bf16[512,4096]{1,0:T(8,128)(2,1)} fusion(bf16[512,512]{1,0:T(8,128)(2,1)S(1)} %all_gather.6, bf16[512,4096]{1,0:T(8,128)(2,1)S(1)} %copy-done.3), kind=kOutput, calls=%fused_computation.1 | convolution fusion | flops 2149580800 | bytes 8912896 | tf_op jit(solution)/shard_map/dot_general | solution.py:47
  112.2 0.7 convolution_convert_fusion.2
  113.0 0.3 convolution_convert_fusion.3
  113.4 18.3 %concatenate.18 = bf16[512,9280]{1,0:T(8,128)(2,1)} concatenate(bf16[512,1024]{1,0:T(8,128)(2,1)S(1)} %convolution_convert_fusion.2, bf16[512,64]{1,0:T(8,128)(2,1)S(1)} %copy.20, bf16[512,4096]{1,0:T(8,128)(2,1)} %convolution_convert_fusion.1, bf16[512,4096]{1,0:T(8,128)(2,1)} %convolution_convert_fusion), dimensions={1} | concatenate | bytes 19005440 | tf_op jit(solution)/shard_map/concatenate | solution.py:43
  131.7 85.3 %reduce-scatter.3.cloned.1.call-done = bf16[32,9280]{1,0:T(8,128)(2,1)} async-done(((bf16[512,9280]{1,0:T(8,128)(2,1)}), bf16[32,9280]{1,0:T(8,128)(2,1)}) %reduce-scatter.3.cloned.1.call-update) | async-done | bytes 593936 | tf_op jit(solution)/shard_map/reduce_scatter | solution.py:42
  217.0 0.9 slice.53
  217.9 0.6 all_to_all.24
  218.5 4.3 %all-to-all-start = ((bf16[8,4,1088]{2,1,0:T(4,128)(2,1)}), bf16[8,4,1088]{2,1,0:T(4,128)(2,1)S(1)}, u32[]{:S(2)}, u32[]{:S(2)}) async-start(bf16[8,4,1088]{2,1,0:T(4,128)(2,1)} %all_to_all.24), calls=%async_computation.1 | async-start | bytes 147456 | tf_op jit(solution)/shard_map/all_to_all | solution.py:59
  222.8 1.2 convert_element_type.68
  224.0 4.5 %all-to-all-done = bf16[8,4,1088]{2,1,0:T(4,128)(2,1)S(1)} async-done(((bf16[8,4,1088]{2,1,0:T(4,128)(2,1)}), bf16[8,4,1088]{2,1,0:T(4,128)(2,1)S(1)}, u32[]{:S(2)}, u32[]{:S(2)}) %all-to-all-start) | async-done | bytes 69664 | tf_op jit(solution)/shard_map/all_to_all | solution.py:59
  228.7 0.1 fusion.15
  228.8 3.8 %fusion.29 = (f32[4,32]{1,0:T(4,128)S(1)}, f32[4,32,2048]{2,1,0:T(8,128)S(1)}) fusion(bf16[4,2048,256]{2,1,0:T(8,128)(2,1)} %param.16, f32[4,32,128]{2,1,0:T(8,128)S(1)} %get-tuple-element.3, f32[4,32,128]{2,1,0:T(8,128)S(1)} %get-tuple-element.2), kind=kOutput, calls=%fused_computation.56 | convolution fusion | flops 134578048 | bytes 5374464 | tf_op jit(solution)/shard_map/rhd,rtd->rht/dot_general | solution.py:75
  232.6 0.3 fusion.5
  232.9 0.8 fusion.3
  233.8 0.7 copy.22
  234.5 3.4 all-to-all-start.1
  237.9 0.3 fusion.6
  238.3 5.1 %all-to-all-done.1 = bf16[4,8,1024]{2,0,1:T(4,128)(2,1)S(1)} async-done(((bf16[4,8,1024]{2,0,1:T(4,128)(2,1)}), bf16[4,8,1024]{2,0,1:T(4,128)(2,1)S(1)}, u32[]{:S(2)}, u32[]{:S(2)}) %all-to-all-start.1) | async-done | bytes 65568 | tf_op jit(solution)/shard_map/all_to_all | solution.py:88
  243.4 0.7 pad_maximum_fusion
  244.3 53.8 %all-gather.2.cloned.1.call-done = bf16[512,5120]{1,0:T(8,128)(2,1)} async-done(((bf16[32,5120]{1,0:T(8,128)(2,1)}), bf16[512,5120]{1,0:T(8,128)(2,1)}) %all-gather.2.cloned.1.call-update) | async-done | bytes 5242896 | tf_op jit(solution)/shard_map/all_gather | solution.py:91
  298.0 5.8 %fusion = f32[512,512]{1,0:T(8,128)S(1)} fusion(bf16[4096,512]{1,0:T(8,128)(2,1)} %param.15, bf16[512,5120]{1,0:T(8,128)(2,1)} %all-gather.2.cloned.1.call-done), kind=kOutput, calls=%fused_computation.2 | convolution fusion | flops 2147483648 | bytes 9437184 | tf_op jit(solution)/shard_map/dot_general | solution.py:93
  303.9 2.8 fusion.2
  306.7 0.6 pad_maximum_fusion.1
  307.3 30.1 %reduce-scatter.5.cloned.1.call-done = bf16[64,512]{1,0:T(8,128)(2,1)} async-done(((bf16[512,512]{1,0:T(8,128)(2,1)}), bf16[64,512]{1,0:T(8,128)(2,1)}) %reduce-scatter.5.cloned.1.call-update) | async-done | bytes 65552 | tf_op jit(solution)/shard_map/reduce_scatter | solution.py:94
  337.3 1.5 fusion.13
  (35 shorter events, 0.7 us)
Async XLA Ops:
  7.2 105.1 %copy-start = (bf16[512,1024]{1,0:T(8,128)(2,1)S(1)}, bf16[512,1024]{1,0:T(8,128)(2,1)}, u32[]{:S(2)}) copy-start(bf16[512,1024]{1,0:T(8,128)(2,1)} %param.10) | copy-start | bytes 3145732
  7.2 209.8 %reduce-scatter.3.cloned.1.call-start = ((), (), s32[]{:S(2)}) async-start(), calls=%async_computation.4 | async-start | bytes 10166272 | tf_op jit(solution)/shard_map/reduce_scatter | solution.py:42
  101.2 6.6 %copy-start.3 = (bf16[512,4096]{1,0:T(8,128)(2,1)S(1)}, bf16[512,4096]{1,0:T(8,128)(2,1)}, u32[]{:S(2)}) copy-start(bf16[512,4096]{1,0:T(8,128)(2,1)} %param.12) | copy-start | bytes 12582916
  107.8 5.2 %copy-start.2 = (bf16[512,64]{0,1:T(8,128)(2,1)S(1)}, bf16[512,64]{0,1:T(8,128)(2,1)}, u32[]{:S(2)}) copy-start(bf16[512,64]{0,1:T(8,128)(2,1)} %param.11) | copy-start | bytes 196612
  218.5 9.9 %all-to-all-start = ((bf16[8,4,1088]{2,1,0:T(4,128)(2,1)}), bf16[8,4,1088]{2,1,0:T(4,128)(2,1)S(1)}, u32[]{:S(2)}, u32[]{:S(2)}) async-start(bf16[8,4,1088]{2,1,0:T(4,128)(2,1)} %all_to_all.24), calls=%async_computation.1 | async-start | bytes 147456 | tf_op jit(solution)/shard_map/all_to_all | solution.py:59
  228.6 4.3 %copy-start.4 = (bf16[4,2048,256]{2,1,0:T(8,128)(2,1)S(1)}, bf16[4,2048,256]{2,1,0:T(8,128)(2,1)}, u32[]{:S(2)}) copy-start(bf16[4,2048,256]{2,1,0:T(8,128)(2,1)} %param.17) | copy-start | bytes 12582916
  234.5 8.9 %all-to-all-start.1 = ((bf16[4,8,1024]{2,0,1:T(4,128)(2,1)}), bf16[4,8,1024]{2,0,1:T(4,128)(2,1)S(1)}, u32[]{:S(2)}, u32[]{:S(2)}) async-start(bf16[4,8,1024]{2,0,1:T(4,128)(2,1)} %copy.22), calls=%async_computation.2 | async-start | bytes 131072 | tf_op jit(solution)/shard_map/all_to_all | solution.py:88
  237.9 60.2 %all-gather.2.cloned.1.call-start = ((), (), s32[]{:S(2)}) async-start(), calls=%async_computation.5 | async-start | bytes 5570560 | tf_op jit(solution)/shard_map/all_gather | solution.py:91
  244.2 59.6 %copy-start.5 = (bf16[1024,512]{1,0:T(8,128)(2,1)S(1)}, bf16[1024,512]{1,0:T(8,128)(2,1)}, u32[]{:S(2)}) copy-start(bf16[1024,512]{1,0:T(8,128)(2,1)} %param.14) | copy-start | bytes 3145732
  244.2 93.1 %reduce-scatter.5.cloned.1.call-start = ((), (), s32[]{:S(2)}) async-start(), calls=%async_computation.6 | async-start | bytes 589824 | tf_op jit(solution)/shard_map/reduce_scatter | solution.py:94
  303.8 33.5 %copy-start.1 = (bf16[64,512]{1,0:T(8,128)(2,1)S(1)}, bf16[64,512]{1,0:T(8,128)(2,1)}, u32[]{:S(2)}) copy-start(bf16[64,512]{1,0:T(8,128)(2,1)} %param.9) | copy-start | bytes 196612
Sparse Core Ops, SparseCore 0:
  131.8 85.1 reduce-scatter.2
  244.3 53.6 all-gather.1
  306.8 30.4 reduce-scatter.4
where the time goes:
time: 346 us; the launch traced here: 345 us
  waiting for transfers between devices  179 us (52%)
  blocking collectives  90.9 us (26%)
  matrix products  25.3 us (7%)
  local copies, waits for them, and re-layouts  20.8 us (6%)
  between operations  13.9 us (4%)
  starting transfers between devices  7.73 us (2%)
  other arithmetic  7.73 us (2%)
    reduce_scatter x1, waiting for transfers between devices, local(): lax.psum_scatter(jnp.concatenate([jnp.dot(gathered, w_query, preferred_el...  85.3 us
    psum x2, blocking collectives, width_total(): return lax.psum(values, 'gx')  77.5 us
    all_gather x1, waiting for transfers between devices, local(): piece = lax.all_gather(joined, 'gx', axis=0, tiled=True)  53.8 us
    reduce_scatter x1, waiting for transfers between devices, local(): lax.psum_scatter(terms.astype(jnp.bfloat16), 'gy', scatter_dimension=0, t...  30.1 us
    concatenate x1, local copies, waits for them, and re-layouts, local(): jnp.concatenate([jnp.dot(gathered, w_query, preferred_element_type=jnp.fl...  18.3 us
    all_gather x1, blocking collectives, local(): gathered = lax.all_gather(source, 'gy', axis=0, tiled=True)  13.5 us
  transfers between devices with their start and end apart: 5, of which 5 were waited for; matrix products, arithmetic and copies ran while one was open for 1% of the time, Pallas kernels for 0%

commit v1 on v0

v1 whole, which is shorter than its diff:
```python
import functools

import jax
import jax.numpy as jnp
from jax import lax
from jax.experimental import pallas as pl
from jax.experimental.pallas import tpu as pltpu
from jax.sharding import PartitionSpec as P

D = 8192
HEADS = 32
HD = 256
NZ = 4
NY = 4
NX = 4
CHUNK = 32
QUARTER = 128
BLOCK = 512
HID_Z = 2048
F32 = jnp.float32
BF16 = jnp.bfloat16
VMEM = pl.BlockSpec(memory_space=pltpu.VMEM)


def ring_y(shift):
    return [(z * NY + y, z * NY + (y + shift) % NY) for z in range(NZ) for y in range(NY)]


def ring_z(shift):
    return [(z * NY + y, ((z + shift) % NZ) * NY + y) for z in range(NZ) for y in range(NY)]


def ring_x(shift):
    return [(x * 2 + c, ((x + shift) % NX) * 2 + c) for x in range(NX) for c in range(2)]


CORES = [(x * 2 + c, x * 2 + 1 - c) for x in range(NX) for c in range(2)]


def send(value, pairs, axis="gx"):
    return lax.ppermute(value, axis, pairs)


def send_direct(chunks, ring, axis="gx"):
    return (
        send(chunks[1], ring(1), axis),
        send(chunks[3], ring(-1), axis),
        send(chunks[2], ring(2), axis),
    )


def gather_direct(value, ring, axis="gx"):
    left, right, far = send_direct([value] * 4, ring, axis)
    return [value, right, far, left]


def add(*values):
    total = values[0].astype(F32)
    for value in values[1:]:
        total = total + value.astype(F32)
    return total


def dot(a, b):
    return jnp.dot(a, b, preferred_element_type=F32)


def roll(values, axis, shift):
    size = values.shape[axis]
    return lax.dynamic_slice_in_dim(
        jnp.concatenate([values, values], axis=axis), shift, size, axis
    )


def shape(dims, dtype=BF16):
    return jax.ShapeDtypeStruct(dims, dtype)


def params(limit=10):
    return pltpu.CompilerParams(vmem_limit_bytes=limit * 1024 * 1024)


def prepare_kernel(place, strip, other, stats, by_z, by_y):
    z, y, x, core = place[0], place[1], place[2], place[3]
    for k in range(NX):
        chunk_z = lax.rem(x + k, NX)
        for source, owner in ((strip, core), (other, 1 - core)):
            for part in range(2):
                chunk_y = owner * 2 + part
                at = pl.multiple_of((chunk_z * NY + chunk_y) * CHUNK, CHUNK)
                mean = stats[pl.ds(at, CHUNK), 0:1]
                scale = stats[pl.ds(at, CHUNK), 1:2]
                values = source[k, part * CHUNK : (part + 1) * CHUNK, :].astype(F32)
                normed = ((values - mean) * scale).astype(BF16)
                away_z = lax.rem(chunk_z - z + NZ, NZ)
                away_y = lax.rem(chunk_y - y + NY, NY)
                to_z = lax.rem(away_z + 2, NZ) * NY + away_y
                to_y = lax.rem(away_y + 2, NY) * NZ + away_z
                by_z[pl.ds(pl.multiple_of(to_z * CHUNK, CHUNK), CHUNK), :] = normed
                by_y[pl.ds(pl.multiple_of(to_y * CHUNK, CHUNK), CHUNK), :] = normed


def prepare(place, strip, other, stats):
    width = strip.shape[2]
    rows = 2 * strip.shape[0] * strip.shape[1]
    return pl.pallas_call(
        prepare_kernel,
        in_specs=[pl.BlockSpec(memory_space=pltpu.SMEM), VMEM, VMEM, VMEM],
        out_specs=[VMEM] * 2,
        out_shape=[shape((rows, width))] * 2,
        compiler_params=params(),
        name="prepare",
    )(place, strip, other, stats)


def queries_kernel(place, rows, query, keyval, out):
    z, y = place[0], place[1]
    q_cols = query.shape[1]
    for weight, begin in ((query, 0), (keyval, q_cols)):
        part = dot(rows[...], weight[...]).astype(BF16)
        for k in range(NZ):
            for i in range(NY):
                chunk = lax.rem(z + k + 2, NZ) * NY + lax.rem(y + i, NY)
                at = (k * NY + i) * CHUNK
                values = part[at : at + CHUNK].reshape(CHUNK // 4, 4, weight.shape[1])
                out[pl.ds(chunk * (CHUNK // 4), CHUNK // 4), :, begin : begin + weight.shape[1]] = (
                    values
                )


def queries(place, rows, query, keyval):
    cols = query.shape[1] + keyval.shape[1]
    return pl.pallas_call(
        queries_kernel,
        in_specs=[pl.BlockSpec(memory_space=pltpu.SMEM), VMEM, VMEM, VMEM],
        out_specs=VMEM,
        out_shape=shape((rows.shape[0] // 4, 4, cols)),
        compiler_params=params(),
        name="queries",
    )(place, rows, query, keyval)


def products_kernel(rows, gate, up, later, left, right, ahead, own, behind):
    for i, weight in enumerate((gate, up)):
        out = dot(rows[...], weight[...]).astype(BF16)
        (left, right)[i][...] = out[:QUARTER]
        behind[i] = out[QUARTER : 2 * QUARTER]
        own[i] = out[2 * QUARTER : 3 * QUARTER]
        ahead[i] = out[3 * QUARTER :]


def products(rows, gate, up, begin, cols, later):
    width = rows.shape[1]
    skip = begin // BLOCK
    column = pl.BlockSpec((width, BLOCK), lambda j: (0, skip + j))
    flat = pl.BlockSpec((QUARTER, BLOCK), lambda j: (0, j))
    both = pl.BlockSpec((2, QUARTER, BLOCK), lambda j: (0, 0, j))
    return pl.pallas_call(
        products_kernel,
        grid=(cols // BLOCK,),
        in_specs=[pl.BlockSpec(rows.shape, lambda j: (0, 0)), column, column]
        + [pl.BlockSpec(memory_space=pl.ANY)],
        out_specs=[flat] * 2 + [both] * 3,
        out_shape=[shape((QUARTER, cols))] * 2 + [shape((2, QUARTER, cols))] * 3,
        compiler_params=params(56),
        name="products",
    )(rows, gate, up, later)


def second_kernel(left, right, ahead_in, behind_in, later, ahead, behind):
    ahead[0] = add(ahead_in[0], left[...]).astype(BF16)
    behind[0] = add(behind_in[0], right[...]).astype(BF16)


def second(left, right, ahead, behind, later):
    quarter, cols = left.shape
    steps = 4
    whole = pl.BlockSpec((quarter, cols // steps), lambda j: (0, j))
    first = pl.BlockSpec((1, quarter, cols // steps), lambda j: (0, 0, j))
    last = pl.BlockSpec((1, quarter, cols // steps), lambda j: (1, 0, j))
    return pl.pallas_call(
        second_kernel,
        grid=(steps,),
        in_specs=[whole, whole, first, last, pl.BlockSpec(memory_space=pl.ANY)],
        out_specs=[first, last],
        out_shape=[shape(ahead.shape)] * 2,
        input_output_aliases={2: 0, 3: 1},
        compiler_params=params(56),
        name="second",
    )(left, right, ahead, behind, later)


def total_kernel(own, left, right, later, *outs):
    for k, out in enumerate(outs):
        at = slice(k * CHUNK, (k + 1) * CHUNK)
        for i in range(2):
            out[i] = add(own[i, at, :], left[i, at, :], right[i, at, :]).astype(BF16)


def total(own, left, right, later):
    cols = own.shape[2]
    return pl.pallas_call(
        total_kernel,
        in_specs=[VMEM] * 3 + [pl.BlockSpec(memory_space=pl.ANY)],
        out_specs=[VMEM] * 4,
        out_shape=[shape((2, CHUNK, cols))] * 4,
        compiler_params=params(),
        name="total",
    )(own, left, right, later)


def hidden_kernel(own, left, right, far, *refs):
    out = refs[-1]
    gate, up = [add(own[i], left[i], right[i], far[i]) for i in range(2)]
    joined = [(gate / (1.0 + jnp.exp(-gate)) * up).astype(BF16)]
    joined = jnp.concatenate(joined + [ref[...] for ref in refs[:-1]], axis=1)
    half = out.shape[2]
    out[0] = joined[:, :half]
    out[1] = joined[:, half:]


def hidden(own, left, right, far, *att):
    cols = own.shape[2] + sum(v.shape[1] for v in att)
    return pl.pallas_call(
        hidden_kernel,
        in_specs=[VMEM] * (4 + len(att)),
        out_specs=VMEM,
        out_shape=shape((2, CHUNK, cols // 2)),
        compiler_params=params(),
        name="hidden",
    )(own, left, right, far, *att)


def attend_kernel(att, turn, keys, values, later, attended, new_kv):
    q_cols = attended.shape[3]
    count = attended.shape[0]
    heads = q_cols // HD
    half = HD // 2
    cos_part, sin_part = turn[0:1, :], turn[1:2, :]

    def rotated(v):
        first, second = v[:, :half], v[:, half:]
        return jnp.concatenate(
            [first * cos_part - second * sin_part, first * sin_part + second * cos_part], axis=1
        )

    mine = att[0].astype(F32)
    queries = jnp.concatenate([mine[:, h * HD : (h + 1) * HD] for h in range(heads)], axis=0)
    queries = (rotated(queries) * HD ** (-0.5)).astype(BF16)
    key = jnp.concatenate([mine[j : j + 1, q_cols:] for j in range(4)], axis=1)
    key = rotated(key).astype(BF16)
    value = jnp.concatenate([mine[j : j + 1, q_cols:] for j in range(4, 8)], axis=1)
    new_kv[0, :, :HD] = key
    new_kv[0, :, HD:] = value.astype(BF16)
    scores = lax.dot_general(
        queries, keys[0], (((1,), (1,)), ((), ())), preferred_element_type=F32
    )
    own = jnp.sum(queries.astype(F32) * key.astype(F32), axis=1, keepdims=True)
    top = jnp.maximum(jnp.max(scores, axis=1, keepdims=True), own)
    weights = jnp.exp(scores - top)
    own_w = jnp.exp(own - top)
    sums = jnp.sum(weights, axis=1, keepdims=True) + own_w
    probs = (weights / sums).astype(BF16)
    mixed = dot(probs, values[0]) + (own_w / sums).astype(BF16).astype(F32) * value
    for h in range(heads):
        attended[:, 0, 0, h * HD : (h + 1) * HD] = mixed[h * count : (h + 1) * count].astype(BF16)


def attend(att, q_cols, key_cache, value_cache, later):
    half = HD // 2
    freqs = 10000.0 ** (-jnp.arange(half, dtype=F32) / half)
    angles = F32(key_cache.shape[1]) * freqs
    turn = jnp.stack([jnp.cos(angles), jnp.sin(angles)])
    rows, count, cols = att.shape
    cache = pl.BlockSpec((1,) + key_cache.shape[1:], lambda r: (r, 0, 0))
    return pl.pallas_call(
        attend_kernel,
        grid=(rows,),
        in_specs=[
            pl.BlockSpec((1, count, cols), lambda r: (r, 0, 0)),
            pl.BlockSpec(turn.shape, lambda r: (0, 0)),
            cache,
            cache,
            pl.BlockSpec(memory_space=pl.ANY),
        ],
        out_specs=[
            pl.BlockSpec((count, 1, 1, q_cols), lambda r: (0, r, 0, 0)),
            pl.BlockSpec((1, 1, 2 * HD), lambda r: (r, 0, 0)),
        ],
        out_shape=[shape((count, rows, 1, q_cols)), shape((rows, 1, 2 * HD))],
        compiler_params=params(56),
        name="attend",
    )(att, turn, key_cache, value_cache, later)


def local(tokens, w_query, w_key_value, w_gate, w_up, w_attn_out, w_down, key_cache, value_cache):
    count_gx = lax.axis_size("gx")
    count_gy = lax.axis_size("gy")
    mine = lax.axis_index("gx")
    place = lax.axis_index("gy")
    z, y = mine // NY, mine % NY
    x, core = place // 2, place % 2
    width = tokens.shape[1]
    q_cols = w_query.shape[1]
    att_cols = q_cols + w_key_value.shape[1]
    hid = w_gate.shape[1]
    hid_y = hid - HID_Z
    rows_dev = CHUNK // count_gy

    values = tokens.astype(F32)
    block_mean = jnp.mean(values, axis=1)
    centered = values - block_mean[:, None]
    stats = jnp.concatenate([block_mean, jnp.sum(centered * centered, axis=1)])
    count = count_gx * count_gy
    stats = lax.all_to_all(
        jnp.broadcast_to(stats, (count, 1, stats.shape[0])), ("gx", "gy"), 0, 0
    ).reshape(count_gx, count_gy, 2, -1)
    mean = jnp.mean(stats[:, :, 0], axis=0)
    offsets = stats[:, :, 0] - mean
    spread = jnp.sum(stats[:, :, 1] + width * offsets * offsets, axis=0) / D
    stats = jnp.stack([mean.reshape(-1), lax.rsqrt(spread + 1e-05).reshape(-1)], axis=1)

    position = jnp.stack([z, y, x, core]).astype(jnp.int32)
    strip = jnp.stack(gather_direct(tokens, ring_x, "gy"))
    other = send(strip, CORES, "gy")
    by_z, by_y = prepare(position, strip, other, stats)

    att = queries(position, by_z, w_query, w_key_value)
    later = att
    att = lax.all_to_all(att, ("gx", "gy"), 0, 0)

    left_z, right_z, ahead_z, own_z, behind_z = products(by_z, w_gate, w_up, 0, HID_Z, later)
    left_y, right_y, ahead_y, own_y, behind_y = products(by_y, w_gate, w_up, HID_Z, hid_y, own_z)
    left_z = send(left_z, ring_z(1))
    right_z = send(right_z, ring_z(-1))
    left_y = send(left_y, ring_y(1))
    right_y = send(right_y, ring_y(-1))

    ahead_z, behind_z = second(left_z, right_z, ahead_z, behind_z, att)
    ahead_y, behind_y = second(left_y, right_y, ahead_y, behind_y, ahead_z)

    att = jnp.sum(att.reshape(count_gx, count_gy, rows_dev, att_cols).astype(F32), axis=0)
    att = att.astype(BF16).transpose(1, 0, 2)
    attended, new_kv = attend(att, q_cols, key_cache, value_cache, ahead_y)
    new_kv = new_kv.reshape(rows_dev, 2 * HD)
    total_z = total(own_z, send(ahead_z, ring_z(1)), send(behind_z, ring_z(-1)), attended)
    attended = lax.all_to_all(attended, "gy", 0, 0)
    total_y = total(own_y, send(ahead_y, ring_y(1)), send(behind_y, ring_y(-1)), attended)
    attended = attended.reshape(CHUNK, q_cols)

    att_z = q_cols // 2
    hidden_z = hidden(total_z[0], *send_direct(total_z, ring_y), attended[:, :att_z])
    hidden_y = hidden(total_y[0], *send_direct(total_y, ring_z), attended[:, att_z:])

    def down(part, first, second, hid, att):
        inner = jnp.concatenate(gather_direct(part, first), axis=1)
        left = send(inner, second(1))
        right = send(inner, second(-1))
        low = send(left[0], second(1))
        high = send(right[1], second(-1))
        half = part.shape[2]

        def product(low, high):
            middle = hid.stop - hid.start - half
            out = dot(low, w_down[hid.start : hid.start + half])
            out = out + dot(high[:, :middle], w_down[hid.start + half : hid.stop])
            return out + dot(high[:, middle:], w_attn_out[att])

        return jnp.concatenate(
            [
                product(inner[0], inner[1]),
                product(right[0], right[1]),
                product(low, high),
                product(left[0], left[1]),
            ],
            axis=0,
        )

    down_z = down(hidden_z, ring_y, ring_z, slice(0, HID_Z), slice(0, att_z))
    down_y = down(hidden_y, ring_z, ring_y, slice(HID_Z, hid), slice(att_z, q_cols))
    d_out = w_down.shape[1]
    terms = down_z.reshape(NZ, NY, CHUNK, d_out)
    terms = terms + down_y.reshape(NY, NZ, CHUNK, d_out).transpose(1, 0, 2, 3)
    terms = roll(roll(terms.astype(BF16), 0, (NZ - z) % NZ), 1, (NY - y) % NY)

    terms = terms.reshape(NX, 2, -1, d_out)
    theirs = lax.dynamic_index_in_dim(terms, 1 - core, 1, keepdims=False)
    ours = lax.dynamic_index_in_dim(terms, core, 1, keepdims=False)
    ours = add(ours, send(theirs, CORES, "gy")).astype(BF16)
    ours = roll(ours, 0, x)
    branch = add(ours[0], *send_direct([ours[k] for k in range(NX)], ring_x, "gy"))
    layer_out = (tokens.astype(F32) + branch).astype(BF16)
    return (layer_out, new_kv)


def solution(mesh):
    return jax.shard_map(
        local,
        mesh=mesh,
        in_specs=(
            P("gy", "gx"),
            P("gx", "gy"),
            P("gx", "gy"),
            P("gx", "gy"),
            P("gx", "gy"),
            P("gy", "gx"),
            P("gy", "gx"),
            P(("gx", "gy"), None, None),
            P(("gx", "gy"), None, None),
        ),
        out_specs=(P("gy", "gx"), P(("gx", "gy"), None)),
        check_vma=False,
    )
```

time: 346 us -> 190 us (0.55)
  waiting for transfers between devices: 179 us -> 52.1 us
  blocking collectives: 90.9 us -> 9.28 us
  starting transfers between devices: 7.73 us -> 66.9 us
  Pallas kernels: 0 us -> 33.8 us
  matrix products: 25.3 us -> 6.72 us
  between operations: 13.9 us -> 1.3 us
  local copies, waits for them, and re-layouts: 20.8 us -> 10.8 us
    reduce_scatter x2 -> x0, waiting for transfers between devices: 115 us -> none  [the longest x1 85.3 us: local(): lax.psum_scatter(jnp.concatenate([jnp.dot(gathered, w_query, preferred_el...]
    psum x2 -> x0, blocking collectives: 77.5 us -> none  [width_total(): return lax.psum(values, 'gx')]
    all_gather x1 -> x0, waiting for transfers between devices: 53.8 us -> none  [local(): piece = lax.all_gather(joined, 'gx', axis=0, tiled=True)]
    ppermute x0 -> x36, starting transfers between devices: none -> 52.6 us  [send(): return lax.ppermute(value, axis, pairs)]
    ppermute x0 -> x36, waiting for transfers between devices: none -> 44 us  [send(): return lax.ppermute(value, axis, pairs)]
    pallas_call x0 -> x11, Pallas kernels: none -> 33.8 us  [the longest x2 12.2 us: products(): pl.pallas_call(products_kernel, grid=(cols // BLOCK,), in_specs=[pl.Block...]
    dot_general x9 -> x24, matrix products: 25.3 us -> 6.72 us  [dot(): return jnp.dot(a, b, preferred_element_type=F32)]
    concatenate x1 -> x0, local copies, waits for them, and re-layouts: 18.3 us -> none  [local(): jnp.concatenate([jnp.dot(gathered, w_query, preferred_element_type=jnp.fl...]
  transfers between devices with their start and end apart: 5 -> 38, of which waited for: 5 -> 17; matrix products, arithmetic and copies ran while one was open for 1% -> 9% of each run, Pallas kernels for 0% -> 16%
where the time goes in v1:
time: 190 us; the launch traced here: 189 us
  starting transfers between devices  66.9 us (35%)
  waiting for transfers between devices  52.1 us (27%)
  Pallas kernels  33.8 us (18%)
  local copies, waits for them, and re-layouts  10.8 us (6%)
  blocking collectives  9.28 us (5%)
  other arithmetic  8.1 us (4%)
  matrix products  6.72 us (4%)
    ppermute x36, starting transfers between devices, send(): return lax.ppermute(value, axis, pairs)  52.6 us
    ppermute x36, waiting for transfers between devices, send(): return lax.ppermute(value, axis, pairs)  44 us
    pallas_call x2, Pallas kernels, products(): pl.pallas_call(products_kernel, grid=(cols // BLOCK,), in_specs=[pl.Block...  12.2 us
    all_to_all x1, blocking collectives, local(): attended = lax.all_to_all(attended, 'gy', 0, 0)  9.28 us
    all_to_all x1, starting transfers between devices, local(): lax.all_to_all(jnp.broadcast_to(stats, (count, 1, stats.shape[0])), ('gx'...  8.63 us
    all_to_all x1, waiting for transfers between devices, local(): lax.all_to_all(jnp.broadcast_to(stats, (count, 1, stats.shape[0])), ('gx'...  8.11 us
    unnamed x34, local copies, waits for them, and re-layouts  8.02 us
    pallas_call x1, Pallas kernels, attend(): pl.pallas_call(attend_kernel, grid=(rows,), in_specs=[pl.BlockSpec((1, co...  7.37 us
  transfers between devices with their start and end apart: 38, of which 17 were waited for; matrix products, arithmetic and copies ran while one was open for 9% of the time, Pallas kernels for 16%

profile of v1, /device:TPU:0, one launch (start us, length us, event | category | flops | bytes accessed | tf_op | source)
XLA Modules:
  0.0 189.0 jit_solution(8993406623488336978)
XLA Ops:
  2.3 2.7 %collective-permute-start.1 = (bf16[64,512]{1,0:T(8,128)(2,1)}, bf16[64,512]{1,0:T(8,128)(2,1)S(1)}, u32[]{:S(2)}, u32[]{:S(2)}) collective-permute-start(bf16[64,512]{1,0:T(8,128)(2,1)} %param.9), channel_id=1, source_target_pairs={{0,4},{1,5},{2,6},{3,7},{4,0},{5,1},{6,2},{7,3},{8,12},{9,13},{10,... | collective-permute-start | bytes 196616 | tf_op jit(solution)/shard_map/ppermute | solution.py:41
  9.2 8.6 %all-to-all-start = ((f32[128,1,128]{2,1,0:T(1,128)}), f32[128,1,128]{2,1,0:T(1,128)S(1)}, u32[]{:S(2)}, u32[]{:S(2)}) async-start(f32[128,1,128]{2,1,0:T(1,128)} %broadcast_in_dim.2), calls=%async_computation | async-start | bytes 131072 | tf_op jit(solution)/shard_map/all_to_all | solution.py:315
  19.0 8.1 %all-to-all-done = f32[128,1,128]{2,1,0:T(1,128)S(1)} async-done(((f32[128,1,128]{2,1,0:T(1,128)}), f32[128,1,128]{2,1,0:T(1,128)S(1)}, u32[]{:S(2)}, u32[]{:S(2)}) %all-to-all-start) | async-done | bytes 65568 | tf_op jit(solution)/shard_map/all_to_all | solution.py:315
  34.4 2.5 %queries.1.later = bf16[128,4,1088]{2,1,0:T(4,128)(2,1)} custom-call(s32[4]{0:T(128)S(1)} %pad_add_fusion.place, bf16[512,512]{1,0:T(8,128)(2,1)S(1)} %get-tuple-element.28.rows, bf16[512,1024]{1,0:T(8,128)(2,1)S(1)} %copy-done.2, bf16[512,64]{1,0:T(8,128)(2,1)S(1)} %copy.45.keyval), custom_call_target="tpu_custom_call" | custom-call | tf_op jit(solution)/shard_map/queries/pallas_call | solution.py:133
  36.8 5.7 %all-to-all-start.1 = ((bf16[128,4,1088]{2,1,0:T(4,128)(2,1)}), bf16[128,4,1088]{2,1,0:T(4,128)(2,1)}, u32[]{:S(2)}, u32[]{:S(2)}) async-start(bf16[128,4,1088]{2,1,0:T(4,128)(2,1)} %queries.1.later), calls=%async_computation.1 | async-start | bytes 2359296 | tf_op jit(solution)/shard_map/all_to_all | solution.py:330
  42.5 6.0 %products.2 = (bf16[128,2048]{1,0:T(8,128)(2,1)}, bf16[128,2048]{1,0:T(8,128)(2,1)}, bf16[2,128,2048]{2,1,0:T(8,128)(2,1)}, bf16[2,128,2048]{2,1,0:T(8,128)(2,1)}, bf16[2,128,2048]{2,1,0:T(8,128)(2,1)}) custom-call(bf16[512,512]{1,0:T(8,128)(2,1)} %copy-done.1, bf16[512,4096]{1,0:T(8,128)(2,1)} %gate.3, bf16[512,4096]{1,0:T(8,128)(2,1)} %up.3, ...), custom_call_target="tpu_custom_call" | custom-call | tf_op jit(solution)/shard_map/products/pallas_call | solution.py:158
  49.6 2.2 %collective-permute-start.5 = (bf16[128,2048]{1,0:T(8,128)(2,1)}, bf16[128,2048]{1,0:T(8,128)(2,1)S(1)}, u32[]{:S(2)}, u32[]{:S(2)}) collective-permute-start(bf16[128,2048]{1,0:T(8,128)(2,1)} %get-tuple-element.31), channel_id=1, source_target_pairs={{0,96},{8,104},{16,112},{24,120},{32,0},{40,8},{48,16},{56,24},{64... | collective-permute-start | bytes 1572872 | tf_op jit(solution)/shard_map/ppermute | solution.py:41
  51.8 6.1 %products.3 = (bf16[128,2048]{1,0:T(8,128)(2,1)}, bf16[128,2048]{1,0:T(8,128)(2,1)}, bf16[2,128,2048]{2,1,0:T(8,128)(2,1)}, bf16[2,128,2048]{2,1,0:T(8,128)(2,1)}, bf16[2,128,2048]{2,1,0:T(8,128)(2,1)}) custom-call(bf16[512,512]{1,0:T(8,128)(2,1)} %copy-done.4, bf16[512,4096]{1,0:T(8,128)(2,1)} %gate.3, bf16[512,4096]{1,0:T(8,128)(2,1)} %up.3, ...), custom_call_target="tpu_custom_call" | custom-call | tf_op jit(solution)/shard_map/products/pallas_call | solution.py:158
  59.1 2.1 %collective-permute-start.9 = (bf16[128,2048]{1,0:T(8,128)(2,1)}, bf16[128,2048]{1,0:T(8,128)(2,1)S(1)}, u32[]{:S(2)}, u32[]{:S(2)}) collective-permute-start(bf16[128,2048]{1,0:T(8,128)(2,1)} %get-tuple-element.38), channel_id=1, source_target_pairs={{0,24},{8,0},{16,8},{24,16},{32,56},{40,32},{48,40},{56,48},{64,88... | collective-permute-start | bytes 1572872 | tf_op jit(solution)/shard_map/ppermute | solution.py:41
  61.2 9.5 %collective-permute-done.4.left = bf16[128,2048]{1,0:T(8,128)(2,1)S(1)} collective-permute-done((bf16[128,2048]{1,0:T(8,128)(2,1)}, bf16[128,2048]{1,0:T(8,128)(2,1)S(1)}, u32[]{:S(2)}, u32[]{:S(2)}) %collective-permute-start.4) | collective-permute-done | bytes 524320 | tf_op jit(solution)/shard_map/ppermute | solution.py:41
  71.7 3.7 %second.2 = (bf16[2,128,2048]{2,1,0:T(8,128)(2,1)}, bf16[2,128,2048]{2,1,0:T(8,128)(2,1)}) custom-call(bf16[128,2048]{1,0:T(8,128)(2,1)} %copy-done.11, bf16[128,2048]{1,0:T(8,128)(2,1)} %copy-done.12, bf16[2,128,2048]{2,1,0:T(8,128)(2,1)} %get-tuple-element.32.ahead_in, ...), custom_call_target="tpu_custom_call", output_to_operand_aliasing={{0}: (2, {}), {1}: (3, {})} | custom-call | tf_op jit(solution)/shard_map/second/pallas_call | solution.py:181
  75.7 2.9 %collective-permute-start.7 = (bf16[2,128,2048]{2,1,0:T(8,128)(2,1)}, bf16[2,128,2048]{2,1,0:T(8,128)(2,1)}, u32[]{:S(2)}, u32[]{:S(2)}) collective-permute-start(bf16[2,128,2048]{2,1,0:T(8,128)(2,1)} %get-tuple-element.35), channel_id=1, source_target_pairs={{0,96},{8,104},{16,112},{24,120},{32,0},{40,8},{48,16},{56,24},{64... | collective-permute-start | bytes 3145736 | tf_op jit(solution)/shard_map/ppermute | solution.py:41
  79.6 3.7 %second.3 = (bf16[2,128,2048]{2,1,0:T(8,128)(2,1)}, bf16[2,128,2048]{2,1,0:T(8,128)(2,1)}) custom-call(bf16[128,2048]{1,0:T(8,128)(2,1)} %copy-done.13, bf16[128,2048]{1,0:T(8,128)(2,1)} %copy-done.14, bf16[2,128,2048]{2,1,0:T(8,128)(2,1)} %get-tuple-element.39.ahead_in, ...), custom_call_target="tpu_custom_call", output_to_operand_aliasing={{0}: (2, {}), {1}: (3, {})} | custom-call | tf_op jit(solution)/shard_map/second/pallas_call | solution.py:181
  83.8 2.7 %collective-permute-start.21 = (bf16[2,128,2048]{2,1,0:T(8,128)(2,1)}, bf16[2,128,2048]{2,1,0:T(8,128)(2,1)S(1)}, u32[]{:S(2)}, u32[]{:S(2)}) collective-permute-start(bf16[2,128,2048]{2,1,0:T(8,128)(2,1)} %get-tuple-element.48), channel_id=1, source_target_pairs={{0,24},{8,0},{16,8},{24,16},{32,56},{40,32},{48,40},{56,48},{64,88... | collective-permute-start | bytes 3145736 | tf_op jit(solution)/shard_map/ppermute | solution.py:41
  89.6 7.4 %attend.1 = (bf16[8,4,1,1024]{3,2,1,0:T(2,128)(2,1)}, bf16[4,1,512]{2,1,0:T(2,128)(2,1)}) custom-call(bf16[4,8,1088]{2,1,0:T(8,128)(2,1)} %bitcast.83, f32[2,128]{1,0:T(2,128)} %pad_maximum_fusion.6.turn, bf16[4,2048,256]{2,1,0:T(8,128)(2,1)} %keys.1, bf16[4,2048,256]{2,1,0:T(8,128)(2,1)} %values.1, bf16[2,128,2048]{2,1,0:T(8,128)(2,1)} %get-tuple-element.41.later), custom_call_target="tpu_custom_call" | custom-call | tf_op jit(solution)/shard_map/attend/pallas_call | solution.py:276
  96.9 4.9 %collective-permute-done.6.left = bf16[2,128,2048]{2,1,0:T(8,128)(2,1)S(1)} collective-permute-done((bf16[2,128,2048]{2,1,0:T(8,128)(2,1)}, bf16[2,128,2048]{2,1,0:T(8,128)(2,1)S(1)}, u32[]{:S(2)}, u32[]{:S(2)}) %collective-permute-start.6) | collective-permute-done | bytes 1048608 | tf_op jit(solution)/shard_map/ppermute | solution.py:41
  102.7 2.2 %total.2 = (bf16[2,32,2048]{2,1,0:T(8,128)(2,1)S(1)}, bf16[2,32,2048]{2,1,0:T(8,128)(2,1)}, bf16[2,32,2048]{2,1,0:T(8,128)(2,1)}, bf16[2,32,2048]{2,1,0:T(8,128)(2,1)}) custom-call(bf16[2,128,2048]{2,1,0:T(8,128)(2,1)S(1)} %copy-done, bf16[2,128,2048]{2,1,0:T(8,128)(2,1)S(1)} %collective-permute-done.6.left, ...), custom_call_target="tpu_custom_call" | custom-call | tf_op jit(solution)/shard_map/total/pallas_call | solution.py:202
  105.7 9.3 %all_to_all.15 = bf16[8,4,1,1024]{3,1,2,0:T(4,128)(2,1)S(1)} all-to-all(bf16[8,4,1,1024]{3,1,2,0:T(4,128)(2,1)S(1)} %copy.47), channel_id=1, replica_groups=mesh['gx'=16,'gy'=8] {'gy'}, dimensions={0} | all-to-all | bytes 131072 | tf_op jit(solution)/shard_map/all_to_all | solution.py:347
  115.1 2.6 %collective-permute-start.11 = (bf16[2,32,2048]{2,1,0:T(8,128)(2,1)}, bf16[2,32,2048]{2,1,0:T(8,128)(2,1)S(1)}, u32[]{:S(2)}, u32[]{:S(2)}) collective-permute-start(bf16[2,32,2048]{2,1,0:T(8,128)(2,1)} %get-tuple-element.45), channel_id=1, source_target_pairs={{0,24},{8,0},{16,8},{24,16},{32,56},{40,32},{48,40},{56,48},{64,88... | collective-permute-start | bytes 786440 | tf_op jit(solution)/shard_map/ppermute | solution.py:41
  121.1 3.3 %collective-permute-start.23 = (bf16[2,32,2048]{2,1,0:T(8,128)(2,1)}, bf16[2,32,2048]{2,1,0:T(8,128)(2,1)S(1)}, u32[]{:S(2)}, u32[]{:S(2)}) collective-permute-start(bf16[2,32,2048]{2,1,0:T(8,128)(2,1)} %copy-done.7), channel_id=1, source_target_pairs={{0,96},{8,104},{16,112},{24,120},{32,0},{40,8},{48,16},{56,24},{64... | collective-permute-start | bytes 786440 | tf_op jit(solution)/shard_map/ppermute | solution.py:41
  125.8 3.3 %collective-permute-done.11.right = bf16[2,32,2048]{2,1,0:T(8,128)(2,1)S(1)} collective-permute-done((bf16[2,32,2048]{2,1,0:T(8,128)(2,1)}, bf16[2,32,2048]{2,1,0:T(8,128)(2,1)S(1)}, u32[]{:S(2)}, u32[]{:S(2)}) %collective-permute-start.11) | collective-permute-done | bytes 262176 | tf_op jit(solution)/shard_map/ppermute | solution.py:41
  131.1 3.3 %collective-permute-start.14 = (bf16[2,32,1280]{2,1,0:T(8,128)(2,1)S(1)}, bf16[2,32,1280]{2,1,0:T(8,128)(2,1)S(1)}, u32[]{:S(2)}, u32[]{:S(2)}) collective-permute-start(bf16[2,32,1280]{2,1,0:T(8,128)(2,1)S(1)} %hidden.2), channel_id=1, source_target_pairs={{0,16},{8,24},{16,0},{24,8},{32,48},{40,56},{48,32},{56,40},{64,80... | collective-permute-start | bytes 491528 | tf_op jit(solution)/shard_map/ppermute | solution.py:41
  138.3 2.1 %collective-permute-start.26 = (bf16[2,32,1280]{2,1,0:T(8,128)(2,1)S(1)}, bf16[2,32,1280]{2,1,0:T(8,128)(2,1)S(1)}, u32[]{:S(2)}, u32[]{:S(2)}) collective-permute-start(bf16[2,32,1280]{2,1,0:T(8,128)(2,1)S(1)} %hidden.3), channel_id=1, source_target_pairs={{0,64},{8,72},{16,80},{24,88},{32,96},{40,104},{48,112},{56,120},{... | collective-permute-start | bytes 491528 | tf_op jit(solution)/shard_map/ppermute | solution.py:41
  142.6 1.9 collective-permute-start.16
  145.5 3.5 %collective-permute-done.26 = bf16[2,32,1280]{2,1,0:T(8,128)(2,1)S(1)} collective-permute-done((bf16[2,32,1280]{2,1,0:T(8,128)(2,1)S(1)}, bf16[2,32,1280]{2,1,0:T(8,128)(2,1)S(1)}, u32[]{:S(2)}, u32[]{:S(2)}) %collective-permute-start.26) | collective-permute-done | bytes 163872 | tf_op jit(solution)/shard_map/ppermute | solution.py:41
  150.3 2.8 %collective-permute-start.28 = (bf16[2,128,1280]{2,1,0:T(8,128)(2,1)S(1)}, bf16[2,128,1280]{2,1,0:T(8,128)(2,1)S(1)}, u32[]{:S(2)}, u32[]{:S(2)}) collective-permute-start(bf16[2,128,1280]{2,1,0:T(8,128)(2,1)S(1)} %pad_maximum_fusion.3), channel_id=1, source_target_pairs={{0,24},{8,0},{16,8},{24,16},{32,56},{40,32},{48,40},{56,48},{64,88... | collective-permute-start | bytes 1966088 | tf_op jit(solution)/shard_map/ppermute | solution.py:41
  154.9 5.9 %collective-permute-done.16 = bf16[2,128,1280]{2,1,0:T(8,128)(2,1)S(1)} collective-permute-done((bf16[2,128,1280]{2,1,0:T(8,128)(2,1)S(1)}, bf16[2,128,1280]{2,1,0:T(8,128)(2,1)S(1)}, u32[]{:S(2)}, u32[]{:S(2)}) %collective-permute-start.16) | collective-permute-done | bytes 655392 | tf_op jit(solution)/shard_map/ppermute | solution.py:41
  160.8 2.7 %collective-permute-start.19 = (bf16[128,1280]{1,0:T(8,128)(2,1)S(1)}, bf16[128,1280]{1,0:T(8,128)(2,1)S(1)}, u32[]{:S(2)}, u32[]{:S(2)}) collective-permute-start(bf16[128,1280]{1,0:T(8,128)(2,1)S(1)} %slice_bitcast_fusion.10), channel_id=1, source_target_pairs={{0,96},{8,104},{16,112},{24,120},{32,0},{40,8},{48,16},{56,24},{64... | collective-permute-start | bytes 983048 | tf_op jit(solution)/shard_map/ppermute | solution.py:41
  169.6 3.5 %collective-permute-done.31 = bf16[128,1280]{1,0:T(8,128)(2,1)S(1)} collective-permute-done((bf16[128,1280]{1,0:T(8,128)(2,1)S(1)}, bf16[128,1280]{1,0:T(8,128)(2,1)S(1)}, u32[]{:S(2)}, u32[]{:S(2)}) %collective-permute-start.31) | collective-permute-done | bytes 327712 | tf_op jit(solution)/shard_map/ppermute | solution.py:41
  173.7 2.0 %collective-permute-done.18 = bf16[128,1280]{1,0:T(8,128)(2,1)S(1)} collective-permute-done((bf16[128,1280]{1,0:T(8,128)(2,1)S(1)}, bf16[128,1280]{1,0:T(8,128)(2,1)S(1)}, u32[]{:S(2)}, u32[]{:S(2)}) %collective-permute-start.18) | collective-permute-done | bytes 327712 | tf_op jit(solution)/shard_map/ppermute | solution.py:41
  179.4 1.9 %collective-permute-start.35 = (bf16[64,512]{1,0:T(8,128)(2,1)S(1)}, bf16[64,512]{1,0:T(8,128)(2,1)S(1)}, u32[]{:S(2)}, u32[]{:S(2)}) collective-permute-start(bf16[64,512]{1,0:T(8,128)(2,1)S(1)} %get-tuple-element.60), channel_id=1, source_target_pairs={{0,4},{1,5},{2,6},{3,7},{4,0},{5,1},{6,2},{7,3},{8,12},{9,13},{10,... | collective-permute-start | bytes 196616 | tf_op jit(solution)/shard_map/ppermute | solution.py:41
  185.6 2.8 %collective-permute-done.33 = bf16[64,512]{1,0:T(8,128)(2,1)S(1)} collective-permute-done((bf16[64,512]{1,0:T(8,128)(2,1)S(1)}, bf16[64,512]{1,0:T(8,128)(2,1)S(1)}, u32[]{:S(2)}, u32[]{:S(2)}) %collective-permute-start.33) | collective-permute-done | bytes 65568 | tf_op jit(solution)/shard_map/ppermute | solution.py:41
  (159 shorter events, 55.8 us)
Async XLA Ops:
  0.6 28.1 %collective-permute-start.2 = (bf16[64,512]{1,0:T(8,128)(2,1)}, bf16[64,512]{1,0:T(8,128)(2,1)S(1)}, u32[]{:S(2)}, u32[]{:S(2)}) collective-permute-start(bf16[64,512]{1,0:T(8,128)(2,1)} %param.9), channel_id=1, source_target_pairs={{0,2},{1,3},{2,4},{3,5},{4,6},{5,7},{6,0},{7,1},{8,10},{9,11},{10,... | collective-permute-start | bytes 196616 | tf_op jit(solution)/shard_map/ppermute | solution.py:41
  2.3 26.5 %collective-permute-start.1 = (bf16[64,512]{1,0:T(8,128)(2,1)}, bf16[64,512]{1,0:T(8,128)(2,1)S(1)}, u32[]{:S(2)}, u32[]{:S(2)}) collective-permute-start(bf16[64,512]{1,0:T(8,128)(2,1)} %param.9), channel_id=1, source_target_pairs={{0,4},{1,5},{2,6},{3,7},{4,0},{5,1},{6,2},{7,3},{8,12},{9,13},{10,... | collective-permute-start | bytes 196616 | tf_op jit(solution)/shard_map/ppermute | solution.py:41
  5.0 23.8 %collective-permute-start = (bf16[64,512]{1,0:T(8,128)(2,1)}, bf16[64,512]{1,0:T(8,128)(2,1)S(1)}, u32[]{:S(2)}, u32[]{:S(2)}) collective-permute-start(bf16[64,512]{1,0:T(8,128)(2,1)} %param.9), channel_id=1, source_target_pairs={{0,6},{1,7},{2,0},{3,1},{4,2},{5,3},{6,4},{7,5},{8,14},{9,15},{10,... | collective-permute-start | bytes 196616 | tf_op jit(solution)/shard_map/ppermute | solution.py:41
  9.2 17.9 %all-to-all-start = ((f32[128,1,128]{2,1,0:T(1,128)}), f32[128,1,128]{2,1,0:T(1,128)S(1)}, u32[]{:S(2)}, u32[]{:S(2)}) async-start(f32[128,1,128]{2,1,0:T(1,128)} %broadcast_in_dim.2), calls=%async_computation | async-start | bytes 131072 | tf_op jit(solution)/shard_map/all_to_all | solution.py:315
  36.8 33.9 %all-to-all-start.1 = ((bf16[128,4,1088]{2,1,0:T(4,128)(2,1)}), bf16[128,4,1088]{2,1,0:T(4,128)(2,1)}, u32[]{:S(2)}, u32[]{:S(2)}) async-start(bf16[128,4,1088]{2,1,0:T(4,128)(2,1)} %queries.1.later), calls=%async_computation.1 | async-start | bytes 2359296 | tf_op jit(solution)/shard_map/all_to_all | solution.py:330
  48.6 22.1 %collective-permute-start.4 = (bf16[128,2048]{1,0:T(8,128)(2,1)}, bf16[128,2048]{1,0:T(8,128)(2,1)S(1)}, u32[]{:S(2)}, u32[]{:S(2)}) collective-permute-start(bf16[128,2048]{1,0:T(8,128)(2,1)} %get-tuple-element.30), channel_id=1, source_target_pairs={{0,32},{8,40},{16,48},{24,56},{32,64},{40,72},{48,80},{56,88},{64,... | collective-permute-start | bytes 1572872 | tf_op jit(solution)/shard_map/ppermute | solution.py:41
  49.6 21.1 %collective-permute-start.5 = (bf16[128,2048]{1,0:T(8,128)(2,1)}, bf16[128,2048]{1,0:T(8,128)(2,1)S(1)}, u32[]{:S(2)}, u32[]{:S(2)}) collective-permute-start(bf16[128,2048]{1,0:T(8,128)(2,1)} %get-tuple-element.31), channel_id=1, source_target_pairs={{0,96},{8,104},{16,112},{24,120},{32,0},{40,8},{48,16},{56,24},{64... | collective-permute-start | bytes 1572872 | tf_op jit(solution)/shard_map/ppermute | solution.py:41
  57.9 20.7 %collective-permute-start.8 = (bf16[128,2048]{1,0:T(8,128)(2,1)}, bf16[128,2048]{1,0:T(8,128)(2,1)S(1)}, u32[]{:S(2)}, u32[]{:S(2)}) collective-permute-start(bf16[128,2048]{1,0:T(8,128)(2,1)} %get-tuple-element.37), channel_id=1, source_target_pairs={{0,8},{8,16},{16,24},{24,0},{32,40},{40,48},{48,56},{56,32},{64,72... | collective-permute-start | bytes 1572872 | tf_op jit(solution)/shard_map/ppermute | solution.py:41
  59.1 19.5 %collective-permute-start.9 = (bf16[128,2048]{1,0:T(8,128)(2,1)}, bf16[128,2048]{1,0:T(8,128)(2,1)S(1)}, u32[]{:S(2)}, u32[]{:S(2)}) collective-permute-start(bf16[128,2048]{1,0:T(8,128)(2,1)} %get-tuple-element.38), channel_id=1, source_target_pairs={{0,24},{8,0},{16,8},{24,16},{32,56},{40,32},{48,40},{56,48},{64,88... | collective-permute-start | bytes 1572872 | tf_op jit(solution)/shard_map/ppermute | solution.py:41
  75.4 26.4 %collective-permute-start.6 = (bf16[2,128,2048]{2,1,0:T(8,128)(2,1)}, bf16[2,128,2048]{2,1,0:T(8,128)(2,1)S(1)}, u32[]{:S(2)}, u32[]{:S(2)}) collective-permute-start(bf16[2,128,2048]{2,1,0:T(8,128)(2,1)} %get-tuple-element.34.later), channel_id=1, source_target_pairs={{0,32},{8,40},{16,48},{24,56},{32,64},{40,72},{48,80},{56,88},{64,... | collective-permute-start | bytes 3145736 | tf_op jit(solution)/shard_map/ppermute | solution.py:41
  75.7 26.1 %collective-permute-start.7 = (bf16[2,128,2048]{2,1,0:T(8,128)(2,1)}, bf16[2,128,2048]{2,1,0:T(8,128)(2,1)}, u32[]{:S(2)}, u32[]{:S(2)}) collective-permute-start(bf16[2,128,2048]{2,1,0:T(8,128)(2,1)} %get-tuple-element.35), channel_id=1, source_target_pairs={{0,96},{8,104},{16,112},{24,120},{32,0},{40,8},{48,16},{56,24},{64... | collective-permute-start | bytes 3145736 | tf_op jit(solution)/shard_map/ppermute | solution.py:41
  83.2 35.4 %collective-permute-start.20 = (bf16[2,128,2048]{2,1,0:T(8,128)(2,1)}, bf16[2,128,2048]{2,1,0:T(8,128)(2,1)S(1)}, u32[]{:S(2)}, u32[]{:S(2)}) collective-permute-start(bf16[2,128,2048]{2,1,0:T(8,128)(2,1)} %get-tuple-element.41.later), channel_id=1, source_target_pairs={{0,8},{8,16},{16,24},{24,0},{32,40},{40,48},{48,56},{56,32},{64,72... | collective-permute-start | bytes 3145736 | tf_op jit(solution)/shard_map/ppermute | solution.py:41
  83.8 34.9 %collective-permute-start.21 = (bf16[2,128,2048]{2,1,0:T(8,128)(2,1)}, bf16[2,128,2048]{2,1,0:T(8,128)(2,1)S(1)}, u32[]{:S(2)}, u32[]{:S(2)}) collective-permute-start(bf16[2,128,2048]{2,1,0:T(8,128)(2,1)} %get-tuple-element.48), channel_id=1, source_target_pairs={{0,24},{8,0},{16,8},{24,16},{32,56},{40,32},{48,40},{56,48},{64,88... | collective-permute-start | bytes 3145736 | tf_op jit(solution)/shard_map/ppermute | solution.py:41
  104.9 19.5 %collective-permute-start.10 = (bf16[2,32,2048]{2,1,0:T(8,128)(2,1)}, bf16[2,32,2048]{2,1,0:T(8,128)(2,1)S(1)}, u32[]{:S(2)}, u32[]{:S(2)}) collective-permute-start(bf16[2,32,2048]{2,1,0:T(8,128)(2,1)} %get-tuple-element.44), channel_id=1, source_target_pairs={{0,8},{8,16},{16,24},{24,0},{32,40},{40,48},{48,56},{56,32},{64,72... | collective-permute-start | bytes 786440 | tf_op jit(solution)/shard_map/ppermute | solution.py:41
  115.1 14.0 %collective-permute-start.11 = (bf16[2,32,2048]{2,1,0:T(8,128)(2,1)}, bf16[2,32,2048]{2,1,0:T(8,128)(2,1)S(1)}, u32[]{:S(2)}, u32[]{:S(2)}) collective-permute-start(bf16[2,32,2048]{2,1,0:T(8,128)(2,1)} %get-tuple-element.45), channel_id=1, source_target_pairs={{0,24},{8,0},{16,8},{24,16},{32,56},{40,32},{48,40},{56,48},{64,88... | collective-permute-start | bytes 786440 | tf_op jit(solution)/shard_map/ppermute | solution.py:41
  117.7 11.4 %collective-permute-start.12 = (bf16[2,32,2048]{2,1,0:T(8,128)(2,1)}, bf16[2,32,2048]{2,1,0:T(8,128)(2,1)S(1)}, u32[]{:S(2)}, u32[]{:S(2)}) collective-permute-start(bf16[2,32,2048]{2,1,0:T(8,128)(2,1)} %get-tuple-element.46), channel_id=1, source_target_pairs={{0,16},{8,24},{16,0},{24,8},{32,48},{40,56},{48,32},{56,40},{64,80... | collective-permute-start | bytes 786440 | tf_op jit(solution)/shard_map/ppermute | solution.py:41
  121.1 13.3 %collective-permute-start.22 = (bf16[2,32,2048]{2,1,0:T(8,128)(2,1)}, bf16[2,32,2048]{2,1,0:T(8,128)(2,1)S(1)}, u32[]{:S(2)}, u32[]{:S(2)}) collective-permute-start(bf16[2,32,2048]{2,1,0:T(8,128)(2,1)} %get-tuple-element.50), channel_id=1, source_target_pairs={{0,32},{8,40},{16,48},{24,56},{32,64},{40,72},{48,80},{56,88},{64,... | collective-permute-start | bytes 786440 | tf_op jit(solution)/shard_map/ppermute | solution.py:41
  121.1 14.0 %collective-permute-start.23 = (bf16[2,32,2048]{2,1,0:T(8,128)(2,1)}, bf16[2,32,2048]{2,1,0:T(8,128)(2,1)S(1)}, u32[]{:S(2)}, u32[]{:S(2)}) collective-permute-start(bf16[2,32,2048]{2,1,0:T(8,128)(2,1)} %copy-done.7), channel_id=1, source_target_pairs={{0,96},{8,104},{16,112},{24,120},{32,0},{40,8},{48,16},{56,24},{64... | collective-permute-start | bytes 786440 | tf_op jit(solution)/shard_map/ppermute | solution.py:41
  124.4 12.4 %collective-permute-start.24 = (bf16[2,32,2048]{2,1,0:T(8,128)(2,1)}, bf16[2,32,2048]{2,1,0:T(8,128)(2,1)S(1)}, u32[]{:S(2)}, u32[]{:S(2)}) collective-permute-start(bf16[2,32,2048]{2,1,0:T(8,128)(2,1)} %copy-done.6), channel_id=1, source_target_pairs={{0,64},{8,72},{16,80},{24,88},{32,96},{40,104},{48,112},{56,120},{... | collective-permute-start | bytes 786440 | tf_op jit(solution)/shard_map/ppermute | solution.py:41
  129.3 11.1 %collective-permute-start.15 = (bf16[2,32,1280]{2,1,0:T(8,128)(2,1)S(1)}, bf16[2,32,1280]{2,1,0:T(8,128)(2,1)S(1)}, u32[]{:S(2)}, u32[]{:S(2)}) collective-permute-start(bf16[2,32,1280]{2,1,0:T(8,128)(2,1)S(1)} %hidden.2), channel_id=1, source_target_pairs={{0,8},{8,16},{16,24},{24,0},{32,40},{40,48},{48,56},{56,32},{64,72... | collective-permute-start | bytes 491528 | tf_op jit(solution)/shard_map/ppermute | solution.py:41
  131.1 10.0 %collective-permute-start.14 = (bf16[2,32,1280]{2,1,0:T(8,128)(2,1)S(1)}, bf16[2,32,1280]{2,1,0:T(8,128)(2,1)S(1)}, u32[]{:S(2)}, u32[]{:S(2)}) collective-permute-start(bf16[2,32,1280]{2,1,0:T(8,128)(2,1)S(1)} %hidden.2), channel_id=1, source_target_pairs={{0,16},{8,24},{16,0},{24,8},{32,48},{40,56},{48,32},{56,40},{64,80... | collective-permute-start | bytes 491528 | tf_op jit(solution)/shard_map/ppermute | solution.py:41
  137.0 8.5 %collective-permute-start.27 = (bf16[2,32,1280]{2,1,0:T(8,128)(2,1)S(1)}, bf16[2,32,1280]{2,1,0:T(8,128)(2,1)S(1)}, u32[]{:S(2)}, u32[]{:S(2)}) collective-permute-start(bf16[2,32,1280]{2,1,0:T(8,128)(2,1)S(1)} %hidden.3), channel_id=1, source_target_pairs={{0,32},{8,40},{16,48},{24,56},{32,64},{40,72},{48,80},{56,88},{64,... | collective-permute-start | bytes 491528 | tf_op jit(solution)/shard_map/ppermute | solution.py:41
  138.3 10.7 %collective-permute-start.26 = (bf16[2,32,1280]{2,1,0:T(8,128)(2,1)S(1)}, bf16[2,32,1280]{2,1,0:T(8,128)(2,1)S(1)}, u32[]{:S(2)}, u32[]{:S(2)}) collective-permute-start(bf16[2,32,1280]{2,1,0:T(8,128)(2,1)S(1)} %hidden.3), channel_id=1, source_target_pairs={{0,64},{8,72},{16,80},{24,88},{32,96},{40,104},{48,112},{56,120},{... | collective-permute-start | bytes 491528 | tf_op jit(solution)/shard_map/ppermute | solution.py:41
  140.4 9.4 %collective-permute-start.25 = (bf16[2,32,1280]{2,1,0:T(8,128)(2,1)S(1)}, bf16[2,32,1280]{2,1,0:T(8,128)(2,1)S(1)}, u32[]{:S(2)}, u32[]{:S(2)}) collective-permute-start(bf16[2,32,1280]{2,1,0:T(8,128)(2,1)S(1)} %hidden.3), channel_id=1, source_target_pairs={{0,96},{8,104},{16,112},{24,120},{32,0},{40,8},{48,16},{56,24},{64... | collective-permute-start | bytes 491528 | tf_op jit(solution)/shard_map/ppermute | solution.py:41
  141.1 22.4 %collective-permute-start.17 = (bf16[2,128,1280]{2,1,0:T(8,128)(2,1)S(1)}, bf16[2,128,1280]{2,1,0:T(8,128)(2,1)S(1)}, u32[]{:S(2)}, u32[]{:S(2)}) collective-permute-start(bf16[2,128,1280]{2,1,0:T(8,128)(2,1)S(1)} %pad_maximum_fusion.2), channel_id=1, source_target_pairs={{0,32},{8,40},{16,48},{24,56},{32,64},{40,72},{48,80},{56,88},{64,... | collective-permute-start | bytes 1966088 | tf_op jit(solution)/shard_map/ppermute | solution.py:41
  142.6 18.2 %collective-permute-start.16 = (bf16[2,128,1280]{2,1,0:T(8,128)(2,1)S(1)}, bf16[2,128,1280]{2,1,0:T(8,128)(2,1)S(1)}, u32[]{:S(2)}, u32[]{:S(2)}) collective-permute-start(bf16[2,128,1280]{2,1,0:T(8,128)(2,1)S(1)} %pad_maximum_fusion.2), channel_id=1, source_target_pairs={{0,96},{8,104},{16,112},{24,120},{32,0},{40,8},{48,16},{56,24},{64... | collective-permute-start | bytes 1966088 | tf_op jit(solution)/shard_map/ppermute | solution.py:41
  149.8 14.5 %collective-permute-start.29 = (bf16[2,128,1280]{2,1,0:T(8,128)(2,1)S(1)}, bf16[2,128,1280]{2,1,0:T(8,128)(2,1)S(1)}, u32[]{:S(2)}, u32[]{:S(2)}) collective-permute-start(bf16[2,128,1280]{2,1,0:T(8,128)(2,1)S(1)} %pad_maximum_fusion.3), channel_id=1, source_target_pairs={{0,8},{8,16},{16,24},{24,0},{32,40},{40,48},{48,56},{56,32},{64,72... | collective-permute-start | bytes 1966088 | tf_op jit(solution)/shard_map/ppermute | solution.py:41
  150.3 14.8 %collective-permute-start.28 = (bf16[2,128,1280]{2,1,0:T(8,128)(2,1)S(1)}, bf16[2,128,1280]{2,1,0:T(8,128)(2,1)S(1)}, u32[]{:S(2)}, u32[]{:S(2)}) collective-permute-start(bf16[2,128,1280]{2,1,0:T(8,128)(2,1)S(1)} %pad_maximum_fusion.3), channel_id=1, source_target_pairs={{0,24},{8,0},{16,8},{24,16},{32,56},{40,32},{48,40},{56,48},{64,88... | collective-permute-start | bytes 1966088 | tf_op jit(solution)/shard_map/ppermute | solution.py:41
  160.8 8.6 %collective-permute-start.19 = (bf16[128,1280]{1,0:T(8,128)(2,1)S(1)}, bf16[128,1280]{1,0:T(8,128)(2,1)S(1)}, u32[]{:S(2)}, u32[]{:S(2)}) collective-permute-start(bf16[128,1280]{1,0:T(8,128)(2,1)S(1)} %slice_bitcast_fusion.10), channel_id=1, source_target_pairs={{0,96},{8,104},{16,112},{24,120},{32,0},{40,8},{48,16},{56,24},{64... | collective-permute-start | bytes 983048 | tf_op jit(solution)/shard_map/ppermute | solution.py:41
  165.2 7.9 %collective-permute-start.31 = (bf16[128,1280]{1,0:T(8,128)(2,1)S(1)}, bf16[128,1280]{1,0:T(8,128)(2,1)S(1)}, u32[]{:S(2)}, u32[]{:S(2)}) collective-permute-start(bf16[128,1280]{1,0:T(8,128)(2,1)S(1)} %slice_bitcast_fusion.2), channel_id=1, source_target_pairs={{0,24},{8,0},{16,8},{24,16},{32,56},{40,32},{48,40},{56,48},{64,88... | collective-permute-start | bytes 983048 | tf_op jit(solution)/shard_map/ppermute | solution.py:41
  166.7 8.9 %collective-permute-start.18 = (bf16[128,1280]{1,0:T(8,128)(2,1)S(1)}, bf16[128,1280]{1,0:T(8,128)(2,1)S(1)}, u32[]{:S(2)}, u32[]{:S(2)}) collective-permute-start(bf16[128,1280]{1,0:T(8,128)(2,1)S(1)} %get-tuple-element.56), channel_id=1, source_target_pairs={{0,32},{8,40},{16,48},{24,56},{32,64},{40,72},{48,80},{56,88},{64,... | collective-permute-start | bytes 983048 | tf_op jit(solution)/shard_map/ppermute | solution.py:41
  166.8 9.5 %collective-permute-start.30 = (bf16[128,1280]{1,0:T(8,128)(2,1)S(1)}, bf16[128,1280]{1,0:T(8,128)(2,1)S(1)}, u32[]{:S(2)}, u32[]{:S(2)}) collective-permute-start(bf16[128,1280]{1,0:T(8,128)(2,1)S(1)} %get-tuple-element.54), channel_id=1, source_target_pairs={{0,8},{8,16},{16,24},{24,0},{32,40},{40,48},{48,56},{56,32},{64,72... | collective-permute-start | bytes 983048 | tf_op jit(solution)/shard_map/ppermute | solution.py:41
  (22 other events, 131.4 us)

commit v2 on v1

--- a/solution.py
+++ b/solution.py
@@ -17,6 +17,9 @@
 QUARTER = 128
 BLOCK = 512
 HID_Z = 2048
+ATT = 1152
+RIDE = 640
+FIRST_STAT = 16
 F32 = jnp.float32
 BF16 = jnp.bfloat16
 VMEM = pl.BlockSpec(memory_space=pltpu.VMEM)
@@ -80,42 +83,55 @@
     return pltpu.CompilerParams(vmem_limit_bytes=limit * 1024 * 1024)
 
 
-def prepare_kernel(place, strip, other, stats, by_z, by_y):
+def prepare_kernel(place, strip, other, by_z, by_y, stats):
     z, y, x, core = place[0], place[1], place[2], place[3]
+    stats[...] = jnp.zeros(stats.shape, BF16)
     for k in range(NX):
         chunk_z = lax.rem(x + k, NX)
         for source, owner in ((strip, core), (other, 1 - core)):
             for part in range(2):
                 chunk_y = owner * 2 + part
-                at = pl.multiple_of((chunk_z * NY + chunk_y) * CHUNK, CHUNK)
-                mean = stats[pl.ds(at, CHUNK), 0:1]
-                scale = stats[pl.ds(at, CHUNK), 1:2]
                 values = source[k, part * CHUNK : (part + 1) * CHUNK, :].astype(F32)
-                normed = ((values - mean) * scale).astype(BF16)
+                mean = jnp.mean(values, axis=1, keepdims=True)
+                centered = values - mean
+                spread = jnp.sum(centered * centered, axis=1, keepdims=True)
+                centered = centered.astype(BF16)
                 away_z = lax.rem(chunk_z - z + NZ, NZ)
                 away_y = lax.rem(chunk_y - y + NY, NY)
                 to_z = lax.rem(away_z + 2, NZ) * NY + away_y
                 to_y = lax.rem(away_y + 2, NY) * NZ + away_z
-                by_z[pl.ds(pl.multiple_of(to_z * CHUNK, CHUNK), CHUNK), :] = normed
-                by_y[pl.ds(pl.multiple_of(to_y * CHUNK, CHUNK), CHUNK), :] = normed
-
-
-def prepare(place, strip, other, stats):
+                by_z[pl.ds(pl.multiple_of(to_z * CHUNK, CHUNK), CHUNK), :] = centered
+                by_y[pl.ds(pl.multiple_of(to_y * CHUNK, CHUNK), CHUNK), :] = centered
+                lane = lax.broadcasted_iota(jnp.int32, (CHUNK, 128), 1)
+                parts = jnp.zeros((CHUNK, 128), F32)
+                for i, value in enumerate((mean, spread)):
+                    for n in range(3):
+                        piece = value.astype(BF16).astype(F32)
+                        parts = jnp.where(lane == FIRST_STAT + 3 * i + n, piece, parts)
+                        value = value - piece
+                at = (chunk_z * NY + chunk_y) * (CHUNK // 4)
+                stats[pl.ds(at, CHUNK // 4), :, RIDE - 128 :] = parts.astype(BF16).reshape(
+                    CHUNK // 4, 4, 128
+                )
+
+
+def prepare(place, strip, other):
     width = strip.shape[2]
     rows = 2 * strip.shape[0] * strip.shape[1]
     return pl.pallas_call(
         prepare_kernel,
-        in_specs=[pl.BlockSpec(memory_space=pltpu.SMEM), VMEM, VMEM, VMEM],
-        out_specs=[VMEM] * 2,
-        out_shape=[shape((rows, width))] * 2,
+        in_specs=[pl.BlockSpec(memory_space=pltpu.SMEM), VMEM, VMEM],
+        out_specs=[VMEM] * 3,
+        out_shape=[shape((rows, width))] * 2 + [shape((rows // 4, 4, RIDE))],
         compiler_params=params(),
         name="prepare",
-    )(place, strip, other, stats)
-
-
-def queries_kernel(place, rows, query, keyval, out):
+    )(place, strip, other)
+
+
+def queries_kernel(place, rows, query, keyval, riders, stats, out):
     z, y = place[0], place[1]
     q_cols = query.shape[1]
+    out[:, :, q_cols:ATT] = jnp.zeros((out.shape[0], 4, ATT - q_cols), BF16)
     for weight, begin in ((query, 0), (keyval, q_cols)):
         part = dot(rows[...], weight[...]).astype(BF16)
         for k in range(NZ):
@@ -126,18 +142,20 @@
                 out[pl.ds(chunk * (CHUNK // 4), CHUNK // 4), :, begin : begin + weight.shape[1]] = (
                     values
                 )
-
-
-def queries(place, rows, query, keyval):
-    cols = query.shape[1] + keyval.shape[1]
+    for n in range(0, out.shape[0], riders.shape[0]):
+        at = slice(n, n + riders.shape[0])
+        out[at, :, ATT:] = riders[...] + stats[at]
+
+
+def queries(place, rows, query, keyval, riders, stats):
     return pl.pallas_call(
         queries_kernel,
-        in_specs=[pl.BlockSpec(memory_space=pltpu.SMEM), VMEM, VMEM, VMEM],
+        in_specs=[pl.BlockSpec(memory_space=pltpu.SMEM)] + [VMEM] * 5,
         out_specs=VMEM,
-        out_shape=shape((rows.shape[0] // 4, 4, cols)),
-        compiler_params=params(),
+        out_shape=shape((rows.shape[0] // 4, 4, ATT + RIDE)),
+        compiler_params=params(16),
         name="queries",
-    )(place, rows, query, keyval)
+    )(place, rows, query, keyval, riders, stats)
 
 
 def products_kernel(rows, gate, up, later, left, right, ahead, own, behind):
@@ -173,14 +191,12 @@
 
 
 def second(left, right, ahead, behind, later):
-    quarter, cols = left.shape
-    steps = 4
-    whole = pl.BlockSpec((quarter, cols // steps), lambda j: (0, j))
-    first = pl.BlockSpec((1, quarter, cols // steps), lambda j: (0, 0, j))
-    last = pl.BlockSpec((1, quarter, cols // steps), lambda j: (1, 0, j))
+    whole = pl.BlockSpec(left.shape, lambda j: (0, 0))
+    first = pl.BlockSpec((1,) + left.shape, lambda j: (0, 0, 0))
+    last = pl.BlockSpec((1,) + left.shape, lambda j: (1, 0, 0))
     return pl.pallas_call(
         second_kernel,
-        grid=(steps,),
+        grid=(1,),
         in_specs=[whole, whole, first, last, pl.BlockSpec(memory_space=pl.ANY)],
         out_specs=[first, last],
         out_shape=[shape(ahead.shape)] * 2,
@@ -209,9 +225,13 @@
     )(own, left, right, later)
 
 
-def hidden_kernel(own, left, right, far, *refs):
+def hidden_kernel(own, left, right, far, offsets, sums, scale, *refs):
     out = refs[-1]
-    gate, up = [add(own[i], left[i], right[i], far[i]) for i in range(2)]
+    both = []
+    for i in range(2):
+        value = add(own[i], left[i], right[i], far[i]) + dot(offsets[...], sums[i])
+        both.append(value * scale[...])
+    gate, up = both
     joined = [(gate / (1.0 + jnp.exp(-gate)) * up).astype(BF16)]
     joined = jnp.concatenate(joined + [ref[...] for ref in refs[:-1]], axis=1)
     half = out.shape[2]
@@ -219,16 +239,16 @@
     out[1] = joined[:, half:]
 
 
-def hidden(own, left, right, far, *att):
+def hidden(own, left, right, far, offsets, sums, scale, *att):
     cols = own.shape[2] + sum(v.shape[1] for v in att)
     return pl.pallas_call(
         hidden_kernel,
-        in_specs=[VMEM] * (4 + len(att)),
+        in_specs=[VMEM] * (7 + len(att)),
         out_specs=VMEM,
         out_shape=shape((2, CHUNK, cols // 2)),
         compiler_params=params(),
         name="hidden",
-    )(own, left, right, far, *att)
+    )(own, left, right, far, offsets, sums, scale, *att)
 
 
 def attend_kernel(att, turn, keys, values, later, attended, new_kv):
@@ -307,25 +327,21 @@
     hid_y = hid - HID_Z
     rows_dev = CHUNK // count_gy
 
-    values = tokens.astype(F32)
-    block_mean = jnp.mean(values, axis=1)
-    centered = values - block_mean[:, None]
-    stats = jnp.concatenate([block_mean, jnp.sum(centered * centered, axis=1)])
-    count = count_gx * count_gy
-    stats = lax.all_to_all(
-        jnp.broadcast_to(stats, (count, 1, stats.shape[0])), ("gx", "gy"), 0, 0
-    ).reshape(count_gx, count_gy, 2, -1)
-    mean = jnp.mean(stats[:, :, 0], axis=0)
-    offsets = stats[:, :, 0] - mean
-    spread = jnp.sum(stats[:, :, 1] + width * offsets * offsets, axis=0) / D
-    stats = jnp.stack([mean.reshape(-1), lax.rsqrt(spread + 1e-05).reshape(-1)], axis=1)
+    ones = jnp.ones((8, width), BF16)
+    sums = [dot(ones, w)[:1].astype(BF16) for w in (w_query, w_key_value, w_gate, w_up)]
+    sums_att = jnp.concatenate(sums[:2], axis=1).reshape(1, 4, -1)
+    sums_hid = jnp.concatenate(sums[2:], axis=1).reshape(count_gy, 4, -1)
+    sums_att = jnp.broadcast_to(sums_att, (count_gy,) + sums_att.shape[1:])
+    riders = jnp.concatenate([sums_att, sums_hid], axis=2)
+    ride = riders.shape[2]
+    riders = jnp.pad(riders, ((0, 0), (0, 0), (0, RIDE - ride)))
 
     position = jnp.stack([z, y, x, core]).astype(jnp.int32)
     strip = jnp.stack(gather_direct(tokens, ring_x, "gy"))
     other = send(strip, CORES, "gy")
-    by_z, by_y = prepare(position, strip, other, stats)
-
-    att = queries(position, by_z, w_query, w_key_value)
+    by_z, by_y, stats = prepare(position, strip, other)
+
+    att = queries(position, by_z, w_query, w_key_value, riders, stats)
     later = att
     att = lax.all_to_all(att, ("gx", "gy"), 0, 0)
 
@@ -339,18 +355,61 @@
     ahead_z, behind_z = second(left_z, right_z, ahead_z, behind_z, att)
     ahead_y, behind_y = second(left_y, right_y, ahead_y, behind_y, ahead_z)
 
-    att = jnp.sum(att.reshape(count_gx, count_gy, rows_dev, att_cols).astype(F32), axis=0)
-    att = att.astype(BF16).transpose(1, 0, 2)
-    attended, new_kv = attend(att, q_cols, key_cache, value_cache, ahead_y)
+    att = att.reshape(count_gx, count_gy, rows_dev, ATT + RIDE)
+    quarter = att_cols // 4
+    stats = att[:, 0, :, ATT + ride : ATT + ride + 6].astype(F32)
+    means = stats[:, :, 0] + stats[:, :, 1] + stats[:, :, 2]
+    spread = stats[:, :, 3] + stats[:, :, 4] + stats[:, :, 5]
+    offsets = means - jnp.mean(means, axis=0)
+    spread = jnp.sum(spread + width * offsets * offsets, axis=0) / D
+    scale = lax.rsqrt(spread + 1e-05)
+    offsets = offsets.astype(BF16)
+    sums_att = att[:, :, :, ATT : ATT + quarter].reshape(count_gx, count_gy, att_cols)
+    sums_hid = att[:, :, :, ATT + quarter : ATT + ride].reshape(count_gx, count_gy, q_cols)
+    high = scale.astype(BF16)
+    rest = scale - high.astype(F32)
+    middle = rest.astype(BF16)
+    low = (rest - middle.astype(F32)).astype(BF16)
+    extra = jnp.concatenate([offsets.reshape(-1), high, middle, low])
+    n_off = offsets.size
+    extra = jnp.pad(extra, (0, q_cols - extra.size)).reshape(1, 1, q_cols)
+    extra = jnp.broadcast_to(extra, (count_gy, 8 - rows_dev, q_cols))
+
+    att = jnp.sum(att[:, :, :, :att_cols].astype(F32), axis=0) + jnp.einsum(
+        "br,bjc->jrc", offsets, sums_att, preferred_element_type=F32
+    )
+    att = (att * scale[:, None]).astype(BF16).transpose(1, 0, 2)
+    ahead_y = send(ahead_y, ring_y(1))
+    behind_y = send(behind_y, ring_y(-1))
+    attended, new_kv = attend(att, q_cols, key_cache, value_cache, later)
     new_kv = new_kv.reshape(rows_dev, 2 * HD)
-    total_z = total(own_z, send(ahead_z, ring_z(1)), send(behind_z, ring_z(-1)), attended)
-    attended = lax.all_to_all(attended, "gy", 0, 0)
-    total_y = total(own_y, send(ahead_y, ring_y(1)), send(behind_y, ring_y(-1)), attended)
-    attended = attended.reshape(CHUNK, q_cols)
+    back = jnp.concatenate(
+        [attended.reshape(count_gy, rows_dev, q_cols), extra, sums_hid.transpose(1, 0, 2)], axis=1
+    )
+    back = lax.all_to_all(back, "gy", 0, 0)
+    total_z = total(own_z, send(ahead_z, ring_z(1)), send(behind_z, ring_z(-1)), back)
+    total_y = total(own_y, ahead_y, behind_y, back)
+    attended = back[:, :rows_dev].reshape(CHUNK, q_cols)
+    extra = back[:, rows_dev]
+    sums_hid = back[:, 8:].transpose(1, 0, 2).reshape(count_gx, -1)
+    offsets = extra[:, :n_off].reshape(count_gy, count_gx, rows_dev).transpose(0, 2, 1)
+    offsets = offsets.reshape(CHUNK, count_gx)
+    scale = extra[:, n_off : n_off + 3 * rows_dev].reshape(count_gy, 3, rows_dev)
+    scale = add(scale[:, 0], scale[:, 1], scale[:, 2]).reshape(CHUNK, 1)
 
     att_z = q_cols // 2
-    hidden_z = hidden(total_z[0], *send_direct(total_z, ring_y), attended[:, :att_z])
-    hidden_y = hidden(total_y[0], *send_direct(total_y, ring_z), attended[:, att_z:])
+
+    def column_sums(begin, end):
+        return jnp.stack([sums_hid[:, begin:end], sums_hid[:, hid + begin : hid + end]])
+
+    hidden_z = hidden(
+        total_z[0], *send_direct(total_z, ring_y), offsets, column_sums(0, HID_Z), scale,
+        attended[:, :att_z],
+    )
+    hidden_y = hidden(
+        total_y[0], *send_direct(total_y, ring_z), offsets, column_sums(HID_Z, hid), scale,
+        attended[:, att_z:],
+    )
 
     def down(part, first, second, hid, att):
         inner = jnp.concatenate(gather_direct(part, first), axis=1)

time: 190 us -> 179 us (0.942)
  blocking collectives: 9.28 us -> 0 us
  matrix products: 6.72 us -> 10.8 us
  other arithmetic: 8.1 us -> 6.02 us
  starting transfers between devices: 66.9 us -> 64.9 us
    all_to_all x1 -> x0, blocking collectives: 9.28 us -> none  [local(): attended = lax.all_to_all(attended, 'gy', 0, 0)]
    all_to_all x1, waiting for transfers between devices: 0.01 us -> 8.35 us  [local(): att = lax.all_to_all(att, ('gx', 'gy'), 0, 0)]
    all_to_all x1, waiting for transfers between devices: 8.11 us -> 2.67 us  [local(): back = lax.all_to_all(back, 'gy', 0, 0)]
    all_to_all x1, starting transfers between devices: 5.69 us -> 10.8 us  [local(): att = lax.all_to_all(att, ('gx', 'gy'), 0, 0)]
    all_to_all x1, starting transfers between devices: 8.63 us -> 3.63 us  [local(): back = lax.all_to_all(back, 'gy', 0, 0)]
    dot_general x24 -> x28, matrix products: 6.72 us -> 10.6 us  [dot(): return jnp.dot(a, b, preferred_element_type=F32)]
    unnamed x34 -> x43, local copies, waits for them, and re-layouts: 8.02 us -> 4.68 us
    reduce_sum x5 -> x3, other arithmetic: 3.85 us -> 0.71 us  [the longest x1 0.51 us: local(): jnp.sum(att[:, :, :, :att_cols].astype(F32), axis=0)]
  transfers between devices with their start and end apart: 38 -> 38, of which waited for: 17 -> 19; matrix products, arithmetic and copies ran while one was open for 9% -> 12% of each run, Pallas kernels for 16% -> 17%
where the time goes in v2:
time: 179 us
  starting transfers between devices  64.9 us (36%)
  waiting for transfers between devices  52.3 us (29%)
  Pallas kernels  33.7 us (19%)
  matrix products  10.8 us (6%)
  local copies, waits for them, and re-layouts  9.53 us (5%)
  other arithmetic  6.02 us (3%)
    ppermute x36, starting transfers between devices, send(): return lax.ppermute(value, axis, pairs)  50.4 us
    ppermute x36, waiting for transfers between devices, send(): return lax.ppermute(value, axis, pairs)  41.3 us
    pallas_call x2, Pallas kernels, products(): pl.pallas_call(products_kernel, grid=(cols // BLOCK,), in_specs=[pl.Block...  12.1 us
    all_to_all x1, starting transfers between devices, local(): att = lax.all_to_all(att, ('gx', 'gy'), 0, 0)  10.8 us
    dot_general x28, matrix products, dot(): return jnp.dot(a, b, preferred_element_type=F32)  10.6 us
    all_to_all x1, waiting for transfers between devices, local(): att = lax.all_to_all(att, ('gx', 'gy'), 0, 0)  8.35 us
    pallas_call x1, Pallas kernels, attend(): pl.pallas_call(attend_kernel, grid=(rows,), in_specs=[pl.BlockSpec((1, co...  7.28 us
    pallas_call x2, Pallas kernels, second(): pl.pallas_call(second_kernel, grid=(1,), in_specs=[whole, whole, first, l...  5.39 us
  transfers between devices with their start and end apart: 38, of which 19 were waited for; matrix products, arithmetic and copies ran while one was open for 12% of the time, Pallas kernels for 17%

profile of v2, /device:TPU:0, one launch (start us, length us, event | category | flops | bytes accessed | tf_op | source)
XLA Modules:
  0.0 178.6 jit_solution(18254652891197804369)
XLA Ops:
  0.7 2.9 %collective-permute-start = (bf16[64,512]{1,0:T(8,128)(2,1)}, bf16[64,512]{1,0:T(8,128)(2,1)S(1)}, u32[]{:S(2)}, u32[]{:S(2)}) collective-permute-start(bf16[64,512]{1,0:T(8,128)(2,1)} %param.9), channel_id=1, source_target_pairs={{0,6},{1,7},{2,0},{3,1},{4,2},{5,3},{6,4},{7,5},{8,14},{9,15},{10,... | collective-permute-start | bytes 196616 | tf_op jit(solution)/shard_map/ppermute | solution.py:44
  3.6 2.3 %collective-permute-start.1 = (bf16[64,512]{1,0:T(8,128)(2,1)}, bf16[64,512]{1,0:T(8,128)(2,1)S(1)}, u32[]{:S(2)}, u32[]{:S(2)}) collective-permute-start(bf16[64,512]{1,0:T(8,128)(2,1)} %param.9), channel_id=1, source_target_pairs={{0,4},{1,5},{2,6},{3,7},{4,0},{5,1},{6,2},{7,3},{8,12},{9,13},{10,... | collective-permute-start | bytes 196616 | tf_op jit(solution)/shard_map/ppermute | solution.py:44
  5.9 2.8 %fusion.83 = bf16[8,4096]{1,0:T(8,128)(2,1)S(1)} fusion(bf16[512,4096]{1,0:T(8,128)(2,1)} %gate.3), kind=kOutput, calls=%fused_computation.152 | convolution fusion | flops 33554432 | bytes 4259840 | tf_op jit(solution)/shard_map/dot_general | solution.py:68
  13.6 2.9 %queries.1.later = bf16[128,4,1792]{2,1,0:T(4,128)(2,1)} custom-call(s32[4]{0:T(128)S(1)} %pad_add_fusion.place, bf16[512,512]{1,0:T(8,128)(2,1)S(1)} %get-tuple-element.29.rows, bf16[512,1024]{1,0:T(8,128)(2,1)S(1)} %copy-done.1, bf16[512,64]{1,0:T(8,128)(2,1)S(1)} %copy.50.keyval, bf16[8,4,640]{2,1,0:T(4,128)(2,1)S(1)} %fusion.75.riders, ...), custom_call_target="tpu_custom_call" | custom-call | tf_op jit(solution)/shard_map/queries/pallas_call | solution.py:151
  16.4 10.8 %all-to-all-start = ((bf16[128,4,1792]{2,1,0:T(4,128)(2,1)}), bf16[128,4,1792]{2,1,0:T(4,128)(2,1)S(1)}, u32[]{:S(2)}, u32[]{:S(2)}) async-start(bf16[128,4,1792]{2,1,0:T(4,128)(2,1)} %queries.1.later), calls=%async_computation | async-start | bytes 3670016 | tf_op jit(solution)/shard_map/all_to_all | solution.py:346
  27.9 6.0 %products.2 = (bf16[128,2048]{1,0:T(8,128)(2,1)}, bf16[128,2048]{1,0:T(8,128)(2,1)}, bf16[2,128,2048]{2,1,0:T(8,128)(2,1)}, bf16[2,128,2048]{2,1,0:T(8,128)(2,1)}, bf16[2,128,2048]{2,1,0:T(8,128)(2,1)}) custom-call(bf16[512,512]{1,0:T(8,128)(2,1)} %copy-done.2, bf16[512,4096]{1,0:T(8,128)(2,1)} %gate.3, bf16[512,4096]{1,0:T(8,128)(2,1)} %up.3, ...), custom_call_target="tpu_custom_call" | custom-call | tf_op jit(solution)/shard_map/products/pallas_call | solution.py:176
  35.0 2.2 %collective-permute-start.5 = (bf16[128,2048]{1,0:T(8,128)(2,1)}, bf16[128,2048]{1,0:T(8,128)(2,1)}, u32[]{:S(2)}, u32[]{:S(2)}) collective-permute-start(bf16[128,2048]{1,0:T(8,128)(2,1)} %get-tuple-element.33), channel_id=1, source_target_pairs={{0,96},{8,104},{16,112},{24,120},{32,0},{40,8},{48,16},{56,24},{64... | collective-permute-start | bytes 1572872 | tf_op jit(solution)/shard_map/ppermute | solution.py:44
  37.1 6.1 %products.3 = (bf16[128,2048]{1,0:T(8,128)(2,1)}, bf16[128,2048]{1,0:T(8,128)(2,1)}, bf16[2,128,2048]{2,1,0:T(8,128)(2,1)}, bf16[2,128,2048]{2,1,0:T(8,128)(2,1)}, bf16[2,128,2048]{2,1,0:T(8,128)(2,1)}) custom-call(bf16[512,512]{1,0:T(8,128)(2,1)} %copy-done.4, bf16[512,4096]{1,0:T(8,128)(2,1)} %gate.3, bf16[512,4096]{1,0:T(8,128)(2,1)} %up.3, ...), custom_call_target="tpu_custom_call" | custom-call | tf_op jit(solution)/shard_map/products/pallas_call | solution.py:176
  44.5 2.0 %collective-permute-start.19 = (bf16[128,2048]{1,0:T(8,128)(2,1)}, bf16[128,2048]{1,0:T(8,128)(2,1)}, u32[]{:S(2)}, u32[]{:S(2)}) collective-permute-start(bf16[128,2048]{1,0:T(8,128)(2,1)} %get-tuple-element.46), channel_id=1, source_target_pairs={{0,24},{8,0},{16,8},{24,16},{32,56},{40,32},{48,40},{56,48},{64,88... | collective-permute-start | bytes 1572872 | tf_op jit(solution)/shard_map/ppermute | solution.py:44
  46.5 8.3 %all-to-all-done.later = bf16[128,4,1792]{2,1,0:T(4,128)(2,1)S(1)} async-done(((bf16[128,4,1792]{2,1,0:T(4,128)(2,1)}), bf16[128,4,1792]{2,1,0:T(4,128)(2,1)S(1)}, u32[]{:S(2)}, u32[]{:S(2)}) %all-to-all-start) | async-done | bytes 1835040 | tf_op jit(solution)/shard_map/all_to_all | solution.py:346
  58.9 7.3 %attend.1 = (bf16[8,4,1,1024]{3,2,1,0:T(2,128)(2,1)}, bf16[4,1,512]{2,1,0:T(2,128)(2,1)}) custom-call(bf16[4,8,1088]{2,1,0:T(8,128)(2,1)} %fusion.60.att, f32[2,128]{1,0:T(2,128)} %pad_maximum_fusion.8.turn, bf16[4,2048,256]{2,1,0:T(8,128)(2,1)} %keys.1, bf16[4,2048,256]{2,1,0:T(8,128)(2,1)} %values.1, bf16[128,4,1792]{2,1,0:T(4,128)(2,1)} %queries.1.later), custom_call_target="tpu_custom_call" | custom-call | tf_op jit(solution)/shard_map/attend/pallas_call | solution.py:296
  67.3 2.7 %second.2 = (bf16[2,128,2048]{2,1,0:T(8,128)(2,1)}, bf16[2,128,2048]{2,1,0:T(8,128)(2,1)}) custom-call(bf16[128,2048]{1,0:T(8,128)(2,1)} %collective-permute-done.4.left, bf16[128,2048]{1,0:T(8,128)(2,1)} %collective-permute-done.5.right, bf16[2,128,2048]{2,1,0:T(8,128)(2,1)} %get-tuple-element.34.ahead_in, ...), custom_call_target="tpu_custom_call", output_to_operand_aliasing={{0}: (2, {}), {1}: (3, {})} | custom-call | tf_op jit(solution)/shard_map/second/pallas_call | solution.py:197
  73.0 3.6 %all-to-all-start.1 = ((bf16[8,24,1024]{2,1,0:T(8,128)(2,1)}), bf16[8,24,1024]{2,1,0:T(8,128)(2,1)S(1)}, u32[]{:S(2)}, u32[]{:S(2)}) async-start(bf16[8,24,1024]{2,1,0:T(8,128)(2,1)} %pad_maximum_fusion.4), calls=%async_computation.1 | async-start | bytes 786432 | tf_op jit(solution)/shard_map/all_to_all | solution.py:389
  76.6 2.7 %second.3 = (bf16[2,128,2048]{2,1,0:T(8,128)(2,1)}, bf16[2,128,2048]{2,1,0:T(8,128)(2,1)}) custom-call(bf16[128,2048]{1,0:T(8,128)(2,1)} %collective-permute-done.18.left, bf16[128,2048]{1,0:T(8,128)(2,1)} %collective-permute-done.19.right, bf16[2,128,2048]{2,1,0:T(8,128)(2,1)} %get-tuple-element.47.ahead_in, ...), custom_call_target="tpu_custom_call", output_to_operand_aliasing={{0}: (2, {}), {1}: (3, {})} | custom-call | tf_op jit(solution)/shard_map/second/pallas_call | solution.py:197
  79.5 3.1 %collective-permute-start.21 = (bf16[2,128,2048]{2,1,0:T(8,128)(2,1)}, bf16[2,128,2048]{2,1,0:T(8,128)(2,1)}, u32[]{:S(2)}, u32[]{:S(2)}) collective-permute-start(bf16[2,128,2048]{2,1,0:T(8,128)(2,1)} %get-tuple-element.50), channel_id=1, source_target_pairs={{0,24},{8,0},{16,8},{24,16},{32,56},{40,32},{48,40},{56,48},{64,88... | collective-permute-start | bytes 3145736 | tf_op jit(solution)/shard_map/ppermute | solution.py:44
  82.6 2.7 %all-to-all-done.1.later = bf16[8,24,1024]{2,1,0:T(8,128)(2,1)S(1)} async-done(((bf16[8,24,1024]{2,1,0:T(8,128)(2,1)}), bf16[8,24,1024]{2,1,0:T(8,128)(2,1)S(1)}, u32[]{:S(2)}, u32[]{:S(2)}) %all-to-all-start.1) | async-done | bytes 393248 | tf_op jit(solution)/shard_map/all_to_all | solution.py:389
  86.0 8.9 %collective-permute-done.7.right = bf16[2,128,2048]{2,1,0:T(8,128)(2,1)S(1)} collective-permute-done((bf16[2,128,2048]{2,1,0:T(8,128)(2,1)}, bf16[2,128,2048]{2,1,0:T(8,128)(2,1)S(1)}, u32[]{:S(2)}, u32[]{:S(2)}) %collective-permute-start.7) | collective-permute-done | bytes 1048608 | tf_op jit(solution)/shard_map/ppermute | solution.py:44
  100.7 3.3 %collective-permute-start.9 = (bf16[2,32,2048]{2,1,0:T(8,128)(2,1)}, bf16[2,32,2048]{2,1,0:T(8,128)(2,1)S(1)}, u32[]{:S(2)}, u32[]{:S(2)}) collective-permute-start(bf16[2,32,2048]{2,1,0:T(8,128)(2,1)} %copy-done.9), channel_id=1, source_target_pairs={{0,24},{8,0},{16,8},{24,16},{32,56},{40,32},{48,40},{56,48},{64,88... | collective-permute-start | bytes 786440 | tf_op jit(solution)/shard_map/ppermute | solution.py:44
  104.0 2.9 %collective-permute-done.20.left = bf16[2,128,2048]{2,1,0:T(8,128)(2,1)} collective-permute-done((bf16[2,128,2048]{2,1,0:T(8,128)(2,1)}, bf16[2,128,2048]{2,1,0:T(8,128)(2,1)}, u32[]{:S(2)}, u32[]{:S(2)}) %collective-permute-start.20) | collective-permute-done | bytes 1048608 | tf_op jit(solution)/shard_map/ppermute | solution.py:44
  106.9 2.3 %total.3 = (bf16[2,32,2048]{2,1,0:T(8,128)(2,1)S(1)}, bf16[2,32,2048]{2,1,0:T(8,128)(2,1)}, bf16[2,32,2048]{2,1,0:T(8,128)(2,1)S(1)}, bf16[2,32,2048]{2,1,0:T(8,128)(2,1)S(1)}) custom-call(bf16[2,128,2048]{2,1,0:T(8,128)(2,1)S(1)} %copy-done.3, bf16[2,128,2048]{2,1,0:T(8,128)(2,1)} %collective-permute-done.20.left, ...), custom_call_target="tpu_custom_call" | custom-call | tf_op jit(solution)/shard_map/total/pallas_call | solution.py:218
  110.6 2.9 %collective-permute-start.23 = (bf16[2,32,2048]{2,1,0:T(8,128)(2,1)}, bf16[2,32,2048]{2,1,0:T(8,128)(2,1)S(1)}, u32[]{:S(2)}, u32[]{:S(2)}) collective-permute-start(bf16[2,32,2048]{2,1,0:T(8,128)(2,1)} %copy-done.8), channel_id=1, source_target_pairs={{0,96},{8,104},{16,112},{24,120},{32,0},{40,8},{48,16},{56,24},{64... | collective-permute-start | bytes 786440 | tf_op jit(solution)/shard_map/ppermute | solution.py:44
  113.5 3.8 %collective-permute-done.8.left = bf16[2,32,2048]{2,1,0:T(8,128)(2,1)S(1)} collective-permute-done((bf16[2,32,2048]{2,1,0:T(8,128)(2,1)}, bf16[2,32,2048]{2,1,0:T(8,128)(2,1)S(1)}, u32[]{:S(2)}, u32[]{:S(2)}) %collective-permute-start.8) | collective-permute-done | bytes 262176 | tf_op jit(solution)/shard_map/ppermute | solution.py:44
  118.5 3.6 %collective-permute-start.12 = (bf16[2,32,1280]{2,1,0:T(8,128)(2,1)S(1)}, bf16[2,32,1280]{2,1,0:T(8,128)(2,1)S(1)}, u32[]{:S(2)}, u32[]{:S(2)}) collective-permute-start(bf16[2,32,1280]{2,1,0:T(8,128)(2,1)S(1)} %hidden.2), channel_id=1, source_target_pairs={{0,16},{8,24},{16,0},{24,8},{32,48},{40,56},{48,32},{56,40},{64,80... | collective-permute-start | bytes 491528 | tf_op jit(solution)/shard_map/ppermute | solution.py:44
  127.2 2.9 %collective-permute-start.26 = (bf16[2,32,1280]{2,1,0:T(8,128)(2,1)S(1)}, bf16[2,32,1280]{2,1,0:T(8,128)(2,1)S(1)}, u32[]{:S(2)}, u32[]{:S(2)}) collective-permute-start(bf16[2,32,1280]{2,1,0:T(8,128)(2,1)S(1)} %hidden.3), channel_id=1, source_target_pairs={{0,64},{8,72},{16,80},{24,88},{32,96},{40,104},{48,112},{56,120},{... | collective-permute-start | bytes 491528 | tf_op jit(solution)/shard_map/ppermute | solution.py:44
  132.2 2.2 %collective-permute-start.14 = (bf16[2,128,1280]{2,1,0:T(8,128)(2,1)S(1)}, bf16[2,128,1280]{2,1,0:T(8,128)(2,1)S(1)}, u32[]{:S(2)}, u32[]{:S(2)}) collective-permute-start(bf16[2,128,1280]{2,1,0:T(8,128)(2,1)S(1)} %pad_maximum_fusion.2), channel_id=1, source_target_pairs={{0,96},{8,104},{16,112},{24,120},{32,0},{40,8},{48,16},{56,24},{64... | collective-permute-start | bytes 1966088 | tf_op jit(solution)/shard_map/ppermute | solution.py:44
  134.5 2.3 %collective-permute-done.27 = bf16[2,32,1280]{2,1,0:T(8,128)(2,1)S(1)} collective-permute-done((bf16[2,32,1280]{2,1,0:T(8,128)(2,1)S(1)}, bf16[2,32,1280]{2,1,0:T(8,128)(2,1)S(1)}, u32[]{:S(2)}, u32[]{:S(2)}) %collective-permute-start.27) | collective-permute-done | bytes 163872 | tf_op jit(solution)/shard_map/ppermute | solution.py:44
  139.7 3.2 %collective-permute-start.28 = (bf16[2,128,1280]{2,1,0:T(8,128)(2,1)S(1)}, bf16[2,128,1280]{2,1,0:T(8,128)(2,1)S(1)}, u32[]{:S(2)}, u32[]{:S(2)}) collective-permute-start(bf16[2,128,1280]{2,1,0:T(8,128)(2,1)S(1)} %pad_maximum_fusion.3), channel_id=1, source_target_pairs={{0,24},{8,0},{16,8},{24,16},{32,56},{40,32},{48,40},{56,48},{64,88... | collective-permute-start | bytes 1966088 | tf_op jit(solution)/shard_map/ppermute | solution.py:44
  144.6 6.1 %collective-permute-done.14 = bf16[2,128,1280]{2,1,0:T(8,128)(2,1)S(1)} collective-permute-done((bf16[2,128,1280]{2,1,0:T(8,128)(2,1)S(1)}, bf16[2,128,1280]{2,1,0:T(8,128)(2,1)S(1)}, u32[]{:S(2)}, u32[]{:S(2)}) %collective-permute-start.14) | collective-permute-done | bytes 655392 | tf_op jit(solution)/shard_map/ppermute | solution.py:44
  150.8 2.4 %collective-permute-start.17 = (bf16[128,1280]{1,0:T(8,128)(2,1)S(1)}, bf16[128,1280]{1,0:T(8,128)(2,1)S(1)}, u32[]{:S(2)}, u32[]{:S(2)}) collective-permute-start(bf16[128,1280]{1,0:T(8,128)(2,1)S(1)} %slice_bitcast_fusion.10), channel_id=1, source_target_pairs={{0,96},{8,104},{16,112},{24,120},{32,0},{40,8},{48,16},{56,24},{64... | collective-permute-start | bytes 983048 | tf_op jit(solution)/shard_map/ppermute | solution.py:44
  155.3 2.2 %collective-permute-start.16 = (bf16[128,1280]{1,0:T(8,128)(2,1)S(1)}, bf16[128,1280]{1,0:T(8,128)(2,1)S(1)}, u32[]{:S(2)}, u32[]{:S(2)}) collective-permute-start(bf16[128,1280]{1,0:T(8,128)(2,1)S(1)} %get-tuple-element.62), channel_id=1, source_target_pairs={{0,32},{8,40},{16,48},{24,56},{32,64},{40,72},{48,80},{56,88},{64,... | collective-permute-start | bytes 983048 | tf_op jit(solution)/shard_map/ppermute | solution.py:44
  159.5 3.4 %collective-permute-done.31 = bf16[128,1280]{1,0:T(8,128)(2,1)S(1)} collective-permute-done((bf16[128,1280]{1,0:T(8,128)(2,1)S(1)}, bf16[128,1280]{1,0:T(8,128)(2,1)S(1)}, u32[]{:S(2)}, u32[]{:S(2)}) %collective-permute-start.31) | collective-permute-done | bytes 327712 | tf_op jit(solution)/shard_map/ppermute | solution.py:44
  174.8 3.2 %collective-permute-done.35 = bf16[64,512]{1,0:T(8,128)(2,1)S(1)} collective-permute-done((bf16[64,512]{1,0:T(8,128)(2,1)S(1)}, bf16[64,512]{1,0:T(8,128)(2,1)S(1)}, u32[]{:S(2)}, u32[]{:S(2)}) %collective-permute-start.35) | collective-permute-done | bytes 65568 | tf_op jit(solution)/shard_map/ppermute | solution.py:44
  (201 shorter events, 53.1 us)
Async XLA Ops:
  0.7 9.0 %collective-permute-start = (bf16[64,512]{1,0:T(8,128)(2,1)}, bf16[64,512]{1,0:T(8,128)(2,1)S(1)}, u32[]{:S(2)}, u32[]{:S(2)}) collective-permute-start(bf16[64,512]{1,0:T(8,128)(2,1)} %param.9), channel_id=1, source_target_pairs={{0,6},{1,7},{2,0},{3,1},{4,2},{5,3},{6,4},{7,5},{8,14},{9,15},{10,... | collective-permute-start | bytes 196616 | tf_op jit(solution)/shard_map/ppermute | solution.py:44
  3.6 6.4 %collective-permute-start.2 = (bf16[64,512]{1,0:T(8,128)(2,1)}, bf16[64,512]{1,0:T(8,128)(2,1)S(1)}, u32[]{:S(2)}, u32[]{:S(2)}) collective-permute-start(bf16[64,512]{1,0:T(8,128)(2,1)} %param.9), channel_id=1, source_target_pairs={{0,2},{1,3},{2,4},{3,5},{4,6},{5,7},{6,0},{7,1},{8,10},{9,11},{10,... | collective-permute-start | bytes 196616 | tf_op jit(solution)/shard_map/ppermute | solution.py:44
  16.4 38.4 %all-to-all-start = ((bf16[128,4,1792]{2,1,0:T(4,128)(2,1)}), bf16[128,4,1792]{2,1,0:T(4,128)(2,1)S(1)}, u32[]{:S(2)}, u32[]{:S(2)}) async-start(bf16[128,4,1792]{2,1,0:T(4,128)(2,1)} %queries.1.later), calls=%async_computation | async-start | bytes 3670016 | tf_op jit(solution)/shard_map/all_to_all | solution.py:346
  33.9 33.4 %collective-permute-start.4 = (bf16[128,2048]{1,0:T(8,128)(2,1)}, bf16[128,2048]{1,0:T(8,128)(2,1)}, u32[]{:S(2)}, u32[]{:S(2)}) collective-permute-start(bf16[128,2048]{1,0:T(8,128)(2,1)} %get-tuple-element.32), channel_id=1, source_target_pairs={{0,32},{8,40},{16,48},{24,56},{32,64},{40,72},{48,80},{56,88},{64,... | collective-permute-start | bytes 1572872 | tf_op jit(solution)/shard_map/ppermute | solution.py:44
  35.0 32.3 %collective-permute-start.5 = (bf16[128,2048]{1,0:T(8,128)(2,1)}, bf16[128,2048]{1,0:T(8,128)(2,1)}, u32[]{:S(2)}, u32[]{:S(2)}) collective-permute-start(bf16[128,2048]{1,0:T(8,128)(2,1)} %get-tuple-element.33), channel_id=1, source_target_pairs={{0,96},{8,104},{16,112},{24,120},{32,0},{40,8},{48,16},{56,24},{64... | collective-permute-start | bytes 1572872 | tf_op jit(solution)/shard_map/ppermute | solution.py:44
  43.3 33.3 %collective-permute-start.18 = (bf16[128,2048]{1,0:T(8,128)(2,1)}, bf16[128,2048]{1,0:T(8,128)(2,1)}, u32[]{:S(2)}, u32[]{:S(2)}) collective-permute-start(bf16[128,2048]{1,0:T(8,128)(2,1)} %get-tuple-element.45), channel_id=1, source_target_pairs={{0,8},{8,16},{16,24},{24,0},{32,40},{40,48},{48,56},{56,32},{64,72... | collective-permute-start | bytes 1572872 | tf_op jit(solution)/shard_map/ppermute | solution.py:44
  44.5 32.2 %collective-permute-start.19 = (bf16[128,2048]{1,0:T(8,128)(2,1)}, bf16[128,2048]{1,0:T(8,128)(2,1)}, u32[]{:S(2)}, u32[]{:S(2)}) collective-permute-start(bf16[128,2048]{1,0:T(8,128)(2,1)} %get-tuple-element.46), channel_id=1, source_target_pairs={{0,24},{8,0},{16,8},{24,16},{32,56},{40,32},{48,40},{56,48},{64,88... | collective-permute-start | bytes 1572872 | tf_op jit(solution)/shard_map/ppermute | solution.py:44
  70.0 24.9 %collective-permute-start.7 = (bf16[2,128,2048]{2,1,0:T(8,128)(2,1)}, bf16[2,128,2048]{2,1,0:T(8,128)(2,1)S(1)}, u32[]{:S(2)}, u32[]{:S(2)}) collective-permute-start(bf16[2,128,2048]{2,1,0:T(8,128)(2,1)} %get-tuple-element.37), channel_id=1, source_target_pairs={{0,96},{8,104},{16,112},{24,120},{32,0},{40,8},{48,16},{56,24},{64... | collective-permute-start | bytes 3145736 | tf_op jit(solution)/shard_map/ppermute | solution.py:44
  70.5 25.9 %collective-permute-start.6 = (bf16[2,128,2048]{2,1,0:T(8,128)(2,1)}, bf16[2,128,2048]{2,1,0:T(8,128)(2,1)}, u32[]{:S(2)}, u32[]{:S(2)}) collective-permute-start(bf16[2,128,2048]{2,1,0:T(8,128)(2,1)} %get-tuple-element.36.later), channel_id=1, source_target_pairs={{0,32},{8,40},{16,48},{24,56},{32,64},{40,72},{48,80},{56,88},{64,... | collective-permute-start | bytes 3145736 | tf_op jit(solution)/shard_map/ppermute | solution.py:44
  73.0 12.3 %all-to-all-start.1 = ((bf16[8,24,1024]{2,1,0:T(8,128)(2,1)}), bf16[8,24,1024]{2,1,0:T(8,128)(2,1)S(1)}, u32[]{:S(2)}, u32[]{:S(2)}) async-start(bf16[8,24,1024]{2,1,0:T(8,128)(2,1)} %pad_maximum_fusion.4), calls=%async_computation.1 | async-start | bytes 786432 | tf_op jit(solution)/shard_map/all_to_all | solution.py:389
  79.4 27.5 %collective-permute-start.20 = (bf16[2,128,2048]{2,1,0:T(8,128)(2,1)}, bf16[2,128,2048]{2,1,0:T(8,128)(2,1)}, u32[]{:S(2)}, u32[]{:S(2)}) collective-permute-start(bf16[2,128,2048]{2,1,0:T(8,128)(2,1)} %get-tuple-element.49), channel_id=1, source_target_pairs={{0,8},{8,16},{16,24},{24,0},{32,40},{40,48},{48,56},{56,32},{64,72... | collective-permute-start | bytes 3145736 | tf_op jit(solution)/shard_map/ppermute | solution.py:44
  79.5 27.3 %collective-permute-start.21 = (bf16[2,128,2048]{2,1,0:T(8,128)(2,1)}, bf16[2,128,2048]{2,1,0:T(8,128)(2,1)}, u32[]{:S(2)}, u32[]{:S(2)}) collective-permute-start(bf16[2,128,2048]{2,1,0:T(8,128)(2,1)} %get-tuple-element.50), channel_id=1, source_target_pairs={{0,24},{8,0},{16,8},{24,16},{32,56},{40,32},{48,40},{56,48},{64,88... | collective-permute-start | bytes 3145736 | tf_op jit(solution)/shard_map/ppermute | solution.py:44
  100.6 16.7 %collective-permute-start.8 = (bf16[2,32,2048]{2,1,0:T(8,128)(2,1)}, bf16[2,32,2048]{2,1,0:T(8,128)(2,1)S(1)}, u32[]{:S(2)}, u32[]{:S(2)}) collective-permute-start(bf16[2,32,2048]{2,1,0:T(8,128)(2,1)} %get-tuple-element.40), channel_id=1, source_target_pairs={{0,8},{8,16},{16,24},{24,0},{32,40},{40,48},{48,56},{56,32},{64,72... | collective-permute-start | bytes 786440 | tf_op jit(solution)/shard_map/ppermute | solution.py:44
  100.7 17.4 %collective-permute-start.9 = (bf16[2,32,2048]{2,1,0:T(8,128)(2,1)}, bf16[2,32,2048]{2,1,0:T(8,128)(2,1)S(1)}, u32[]{:S(2)}, u32[]{:S(2)}) collective-permute-start(bf16[2,32,2048]{2,1,0:T(8,128)(2,1)} %copy-done.9), channel_id=1, source_target_pairs={{0,24},{8,0},{16,8},{24,16},{32,56},{40,32},{48,40},{56,48},{64,88... | collective-permute-start | bytes 786440 | tf_op jit(solution)/shard_map/ppermute | solution.py:44
  104.0 14.1 %collective-permute-start.10 = (bf16[2,32,2048]{2,1,0:T(8,128)(2,1)}, bf16[2,32,2048]{2,1,0:T(8,128)(2,1)S(1)}, u32[]{:S(2)}, u32[]{:S(2)}) collective-permute-start(bf16[2,32,2048]{2,1,0:T(8,128)(2,1)} %copy-done.7), channel_id=1, source_target_pairs={{0,16},{8,24},{16,0},{24,8},{32,48},{40,56},{48,32},{56,40},{64,80... | collective-permute-start | bytes 786440 | tf_op jit(solution)/shard_map/ppermute | solution.py:44
  110.0 12.1 %collective-permute-start.22 = (bf16[2,32,2048]{2,1,0:T(8,128)(2,1)}, bf16[2,32,2048]{2,1,0:T(8,128)(2,1)S(1)}, u32[]{:S(2)}, u32[]{:S(2)}) collective-permute-start(bf16[2,32,2048]{2,1,0:T(8,128)(2,1)} %get-tuple-element.52), channel_id=1, source_target_pairs={{0,32},{8,40},{16,48},{24,56},{32,64},{40,72},{48,80},{56,88},{64,... | collective-permute-start | bytes 786440 | tf_op jit(solution)/shard_map/ppermute | solution.py:44
  110.6 14.0 %collective-permute-start.23 = (bf16[2,32,2048]{2,1,0:T(8,128)(2,1)}, bf16[2,32,2048]{2,1,0:T(8,128)(2,1)S(1)}, u32[]{:S(2)}, u32[]{:S(2)}) collective-permute-start(bf16[2,32,2048]{2,1,0:T(8,128)(2,1)} %copy-done.8), channel_id=1, source_target_pairs={{0,96},{8,104},{16,112},{24,120},{32,0},{40,8},{48,16},{56,24},{64... | collective-permute-start | bytes 786440 | tf_op jit(solution)/shard_map/ppermute | solution.py:44
  117.3 9.1 %collective-permute-start.24 = (bf16[2,32,2048]{2,1,0:T(8,128)(2,1)S(1)}, bf16[2,32,2048]{2,1,0:T(8,128)(2,1)S(1)}, u32[]{:S(2)}, u32[]{:S(2)}) collective-permute-start(bf16[2,32,2048]{2,1,0:T(8,128)(2,1)S(1)} %get-tuple-element.54), channel_id=1, source_target_pairs={{0,64},{8,72},{16,80},{24,88},{32,96},{40,104},{48,112},{56,120},{... | collective-permute-start | bytes 786440 | tf_op jit(solution)/shard_map/ppermute | solution.py:44
  118.4 11.6 %collective-permute-start.13 = (bf16[2,32,1280]{2,1,0:T(8,128)(2,1)S(1)}, bf16[2,32,1280]{2,1,0:T(8,128)(2,1)S(1)}, u32[]{:S(2)}, u32[]{:S(2)}) collective-permute-start(bf16[2,32,1280]{2,1,0:T(8,128)(2,1)S(1)} %hidden.2), channel_id=1, source_target_pairs={{0,8},{8,16},{16,24},{24,0},{32,40},{40,48},{48,56},{56,32},{64,72... | collective-permute-start | bytes 491528 | tf_op jit(solution)/shard_map/ppermute | solution.py:44
  118.5 12.5 %collective-permute-start.12 = (bf16[2,32,1280]{2,1,0:T(8,128)(2,1)S(1)}, bf16[2,32,1280]{2,1,0:T(8,128)(2,1)S(1)}, u32[]{:S(2)}, u32[]{:S(2)}) collective-permute-start(bf16[2,32,1280]{2,1,0:T(8,128)(2,1)S(1)} %hidden.2), channel_id=1, source_target_pairs={{0,16},{8,24},{16,0},{24,8},{32,48},{40,56},{48,32},{56,40},{64,80... | collective-permute-start | bytes 491528 | tf_op jit(solution)/shard_map/ppermute | solution.py:44
  122.1 9.0 %collective-permute-start.11 = (bf16[2,32,1280]{2,1,0:T(8,128)(2,1)S(1)}, bf16[2,32,1280]{2,1,0:T(8,128)(2,1)S(1)}, u32[]{:S(2)}, u32[]{:S(2)}) collective-permute-start(bf16[2,32,1280]{2,1,0:T(8,128)(2,1)S(1)} %hidden.2), channel_id=1, source_target_pairs={{0,24},{8,0},{16,8},{24,16},{32,56},{40,32},{48,40},{56,48},{64,88... | collective-permute-start | bytes 491528 | tf_op jit(solution)/shard_map/ppermute | solution.py:44
  126.7 10.0 %collective-permute-start.27 = (bf16[2,32,1280]{2,1,0:T(8,128)(2,1)S(1)}, bf16[2,32,1280]{2,1,0:T(8,128)(2,1)S(1)}, u32[]{:S(2)}, u32[]{:S(2)}) collective-permute-start(bf16[2,32,1280]{2,1,0:T(8,128)(2,1)S(1)} %hidden.3), channel_id=1, source_target_pairs={{0,32},{8,40},{16,48},{24,56},{32,64},{40,72},{48,80},{56,88},{64,... | collective-permute-start | bytes 491528 | tf_op jit(solution)/shard_map/ppermute | solution.py:44
  127.2 11.5 %collective-permute-start.26 = (bf16[2,32,1280]{2,1,0:T(8,128)(2,1)S(1)}, bf16[2,32,1280]{2,1,0:T(8,128)(2,1)S(1)}, u32[]{:S(2)}, u32[]{:S(2)}) collective-permute-start(bf16[2,32,1280]{2,1,0:T(8,128)(2,1)S(1)} %hidden.3), channel_id=1, source_target_pairs={{0,64},{8,72},{16,80},{24,88},{32,96},{40,104},{48,112},{56,120},{... | collective-permute-start | bytes 491528 | tf_op jit(solution)/shard_map/ppermute | solution.py:44
  130.1 9.4 %collective-permute-start.25 = (bf16[2,32,1280]{2,1,0:T(8,128)(2,1)S(1)}, bf16[2,32,1280]{2,1,0:T(8,128)(2,1)S(1)}, u32[]{:S(2)}, u32[]{:S(2)}) collective-permute-start(bf16[2,32,1280]{2,1,0:T(8,128)(2,1)S(1)} %hidden.3), channel_id=1, source_target_pairs={{0,96},{8,104},{16,112},{24,120},{32,0},{40,8},{48,16},{56,24},{64... | collective-permute-start | bytes 491528 | tf_op jit(solution)/shard_map/ppermute | solution.py:44
  131.2 22.1 %collective-permute-start.15 = (bf16[2,128,1280]{2,1,0:T(8,128)(2,1)S(1)}, bf16[2,128,1280]{2,1,0:T(8,128)(2,1)S(1)}, u32[]{:S(2)}, u32[]{:S(2)}) collective-permute-start(bf16[2,128,1280]{2,1,0:T(8,128)(2,1)S(1)} %pad_maximum_fusion.2), channel_id=1, source_target_pairs={{0,32},{8,40},{16,48},{24,56},{32,64},{40,72},{48,80},{56,88},{64,... | collective-permute-start | bytes 1966088 | tf_op jit(solution)/shard_map/ppermute | solution.py:44
  132.2 18.5 %collective-permute-start.14 = (bf16[2,128,1280]{2,1,0:T(8,128)(2,1)S(1)}, bf16[2,128,1280]{2,1,0:T(8,128)(2,1)S(1)}, u32[]{:S(2)}, u32[]{:S(2)}) collective-permute-start(bf16[2,128,1280]{2,1,0:T(8,128)(2,1)S(1)} %pad_maximum_fusion.2), channel_id=1, source_target_pairs={{0,96},{8,104},{16,112},{24,120},{32,0},{40,8},{48,16},{56,24},{64... | collective-permute-start | bytes 1966088 | tf_op jit(solution)/shard_map/ppermute | solution.py:44
  139.6 14.4 %collective-permute-start.29 = (bf16[2,128,1280]{2,1,0:T(8,128)(2,1)S(1)}, bf16[2,128,1280]{2,1,0:T(8,128)(2,1)S(1)}, u32[]{:S(2)}, u32[]{:S(2)}) collective-permute-start(bf16[2,128,1280]{2,1,0:T(8,128)(2,1)S(1)} %pad_maximum_fusion.3), channel_id=1, source_target_pairs={{0,8},{8,16},{16,24},{24,0},{32,40},{40,48},{48,56},{56,32},{64,72... | collective-permute-start | bytes 1966088 | tf_op jit(solution)/shard_map/ppermute | solution.py:44
  139.7 15.2 %collective-permute-start.28 = (bf16[2,128,1280]{2,1,0:T(8,128)(2,1)S(1)}, bf16[2,128,1280]{2,1,0:T(8,128)(2,1)S(1)}, u32[]{:S(2)}, u32[]{:S(2)}) collective-permute-start(bf16[2,128,1280]{2,1,0:T(8,128)(2,1)S(1)} %pad_maximum_fusion.3), channel_id=1, source_target_pairs={{0,24},{8,0},{16,8},{24,16},{32,56},{40,32},{48,40},{56,48},{64,88... | collective-permute-start | bytes 1966088 | tf_op jit(solution)/shard_map/ppermute | solution.py:44
  150.8 8.5 %collective-permute-start.17 = (bf16[128,1280]{1,0:T(8,128)(2,1)S(1)}, bf16[128,1280]{1,0:T(8,128)(2,1)S(1)}, u32[]{:S(2)}, u32[]{:S(2)}) collective-permute-start(bf16[128,1280]{1,0:T(8,128)(2,1)S(1)} %slice_bitcast_fusion.10), channel_id=1, source_target_pairs={{0,96},{8,104},{16,112},{24,120},{32,0},{40,8},{48,16},{56,24},{64... | collective-permute-start | bytes 983048 | tf_op jit(solution)/shard_map/ppermute | solution.py:44
  155.2 7.8 %collective-permute-start.31 = (bf16[128,1280]{1,0:T(8,128)(2,1)S(1)}, bf16[128,1280]{1,0:T(8,128)(2,1)S(1)}, u32[]{:S(2)}, u32[]{:S(2)}) collective-permute-start(bf16[128,1280]{1,0:T(8,128)(2,1)S(1)} %slice_bitcast_fusion.2), channel_id=1, source_target_pairs={{0,24},{8,0},{16,8},{24,16},{32,56},{40,32},{48,40},{56,48},{64,88... | collective-permute-start | bytes 983048 | tf_op jit(solution)/shard_map/ppermute | solution.py:44
  155.3 9.0 %collective-permute-start.16 = (bf16[128,1280]{1,0:T(8,128)(2,1)S(1)}, bf16[128,1280]{1,0:T(8,128)(2,1)S(1)}, u32[]{:S(2)}, u32[]{:S(2)}) collective-permute-start(bf16[128,1280]{1,0:T(8,128)(2,1)S(1)} %get-tuple-element.62), channel_id=1, source_target_pairs={{0,32},{8,40},{16,48},{24,56},{32,64},{40,72},{48,80},{56,88},{64,... | collective-permute-start | bytes 983048 | tf_op jit(solution)/shard_map/ppermute | solution.py:44
  157.6 8.3 %collective-permute-start.30 = (bf16[128,1280]{1,0:T(8,128)(2,1)S(1)}, bf16[128,1280]{1,0:T(8,128)(2,1)S(1)}, u32[]{:S(2)}, u32[]{:S(2)}) collective-permute-start(bf16[128,1280]{1,0:T(8,128)(2,1)S(1)} %get-tuple-element.60), channel_id=1, source_target_pairs={{0,8},{8,16},{16,24},{24,0},{32,40},{40,48},{48,56},{56,32},{64,72... | collective-permute-start | bytes 983048 | tf_op jit(solution)/shard_map/ppermute | solution.py:44
  (25 other events, 232.2 us)

commit v3 on v2

--- a/solution.py
+++ b/solution.py
@@ -18,8 +18,10 @@
 BLOCK = 512
 HID_Z = 2048
 ATT = 1152
-RIDE = 640
-FIRST_STAT = 16
+FIRST_STAT = 64
+SUMS_ATT = 384
+SUMS_HID = 256
+RIDE = SUMS_ATT + SUMS_HID
 F32 = jnp.float32
 BF16 = jnp.bfloat16
 VMEM = pl.BlockSpec(memory_space=pltpu.VMEM)
@@ -85,7 +87,6 @@
 
 def prepare_kernel(place, strip, other, by_z, by_y, stats):
     z, y, x, core = place[0], place[1], place[2], place[3]
-    stats[...] = jnp.zeros(stats.shape, BF16)
     for k in range(NX):
         chunk_z = lax.rem(x + k, NX)
         for source, owner in ((strip, core), (other, 1 - core)):
@@ -110,7 +111,7 @@
                         parts = jnp.where(lane == FIRST_STAT + 3 * i + n, piece, parts)
                         value = value - piece
                 at = (chunk_z * NY + chunk_y) * (CHUNK // 4)
-                stats[pl.ds(at, CHUNK // 4), :, RIDE - 128 :] = parts.astype(BF16).reshape(
+                stats[pl.ds(at, CHUNK // 4), :, :] = parts.astype(BF16).reshape(
                     CHUNK // 4, 4, 128
                 )
 
@@ -122,7 +123,7 @@
         prepare_kernel,
         in_specs=[pl.BlockSpec(memory_space=pltpu.SMEM), VMEM, VMEM],
         out_specs=[VMEM] * 3,
-        out_shape=[shape((rows, width))] * 2 + [shape((rows // 4, 4, RIDE))],
+        out_shape=[shape((rows, width))] * 2 + [shape((rows // 4, 4, 128))],
         compiler_params=params(),
         name="prepare",
     )(place, strip, other)
@@ -131,7 +132,7 @@
 def queries_kernel(place, rows, query, keyval, riders, stats, out):
     z, y = place[0], place[1]
     q_cols = query.shape[1]
-    out[:, :, q_cols:ATT] = jnp.zeros((out.shape[0], 4, ATT - q_cols), BF16)
+    out[:, :, ATT - 128 : ATT] = stats[...]
     for weight, begin in ((query, 0), (keyval, q_cols)):
         part = dot(rows[...], weight[...]).astype(BF16)
         for k in range(NZ):
@@ -144,7 +145,7 @@
                 )
     for n in range(0, out.shape[0], riders.shape[0]):
         at = slice(n, n + riders.shape[0])
-        out[at, :, ATT:] = riders[...] + stats[at]
+        out[at, :, ATT:] = riders[...]
 
 
 def queries(place, rows, query, keyval, riders, stats):
@@ -158,13 +159,17 @@
     )(place, rows, query, keyval, riders, stats)
 
 
-def products_kernel(rows, gate, up, later, left, right, ahead, own, behind):
+def products_kernel(rows, gate, up, later, ahead, behind, gate_on, up_on, own):
     for i, weight in enumerate((gate, up)):
         out = dot(rows[...], weight[...]).astype(BF16)
-        (left, right)[i][...] = out[:QUARTER]
-        behind[i] = out[QUARTER : 2 * QUARTER]
+        (ahead, behind)[i][i] = out[:QUARTER]
         own[i] = out[2 * QUARTER : 3 * QUARTER]
-        ahead[i] = out[3 * QUARTER :]
+        if i == 0:
+            behind[0] = out[QUARTER : 2 * QUARTER]
+            gate_on[...] = out[3 * QUARTER :]
+        else:
+            up_on[...] = out[QUARTER : 2 * QUARTER]
+            ahead[1] = out[3 * QUARTER :]
 
 
 def products(rows, gate, up, begin, cols, later):
@@ -178,51 +183,60 @@
         grid=(cols // BLOCK,),
         in_specs=[pl.BlockSpec(rows.shape, lambda j: (0, 0)), column, column]
         + [pl.BlockSpec(memory_space=pl.ANY)],
-        out_specs=[flat] * 2 + [both] * 3,
-        out_shape=[shape((QUARTER, cols))] * 2 + [shape((2, QUARTER, cols))] * 3,
+        out_specs=[both] * 2 + [flat] * 2 + [both],
+        out_shape=[shape((2, QUARTER, cols))] * 2
+        + [shape((QUARTER, cols))] * 2
+        + [shape((2, QUARTER, cols))],
         compiler_params=params(56),
         name="products",
     )(rows, gate, up, later)
 
 
-def second_kernel(left, right, ahead_in, behind_in, later, ahead, behind):
-    ahead[0] = add(ahead_in[0], left[...]).astype(BF16)
-    behind[0] = add(behind_in[0], right[...]).astype(BF16)
-
-
-def second(left, right, ahead, behind, later):
-    whole = pl.BlockSpec(left.shape, lambda j: (0, 0))
-    first = pl.BlockSpec((1,) + left.shape, lambda j: (0, 0, 0))
-    last = pl.BlockSpec((1,) + left.shape, lambda j: (1, 0, 0))
+def second_kernel(left, right, gate_in, up_in, later, gate, up):
+    gate[...] = add(gate_in[...], left[0]).astype(BF16)
+    up[...] = add(up_in[...], right[0]).astype(BF16)
+
+
+def half(values, i):
+    return pl.BlockSpec((1,) + values.shape[1:], lambda j: (i, 0, 0))
+
+
+def whole(values):
+    return pl.BlockSpec(values.shape, lambda j: (0,) * values.ndim)
+
+
+def second(left, right, gate, up, later):
     return pl.pallas_call(
         second_kernel,
         grid=(1,),
-        in_specs=[whole, whole, first, last, pl.BlockSpec(memory_space=pl.ANY)],
-        out_specs=[first, last],
-        out_shape=[shape(ahead.shape)] * 2,
-        input_output_aliases={2: 0, 3: 1},
-        compiler_params=params(56),
+        in_specs=[half(left, 0), half(right, 1), whole(gate), whole(up)]
+        + [pl.BlockSpec(memory_space=pl.ANY)],
+        out_specs=[whole(gate), whole(up)],
+        out_shape=[shape(gate.shape)] * 2,
+        compiler_params=params(10),
         name="second",
-    )(left, right, ahead, behind, later)
-
-
-def total_kernel(own, left, right, later, *outs):
+    )(left, right, gate, up, later)
+
+
+def total_kernel(own, left, right, gate, up, later, *outs):
     for k, out in enumerate(outs):
         at = slice(k * CHUNK, (k + 1) * CHUNK)
-        for i in range(2):
-            out[i] = add(own[i, at, :], left[i, at, :], right[i, at, :]).astype(BF16)
-
-
-def total(own, left, right, later):
-    cols = own.shape[2]
+        out[0] = add(own[0, at, :], gate[at, :], right[0, at, :]).astype(BF16)
+        out[1] = add(own[1, at, :], left[0, at, :], up[at, :]).astype(BF16)
+
+
+def total(own, left, right, gate, up, later):
+    outs = [shape((2, CHUNK, own.shape[2]))] * 4
     return pl.pallas_call(
         total_kernel,
-        in_specs=[VMEM] * 3 + [pl.BlockSpec(memory_space=pl.ANY)],
-        out_specs=[VMEM] * 4,
-        out_shape=[shape((2, CHUNK, cols))] * 4,
+        grid=(1,),
+        in_specs=[whole(own), half(left, 1), half(right, 0), whole(gate), whole(up)]
+        + [pl.BlockSpec(memory_space=pl.ANY)],
+        out_specs=[whole(out) for out in outs],
+        out_shape=outs,
         compiler_params=params(),
         name="total",
-    )(own, left, right, later)
+    )(own, left, right, gate, up, later)
 
 
 def hidden_kernel(own, left, right, far, offsets, sums, scale, *refs):
@@ -251,11 +265,52 @@
     )(own, left, right, far, offsets, sums, scale, *att)
 
 
-def attend_kernel(att, turn, keys, values, later, attended, new_kv):
-    q_cols = attended.shape[3]
-    count = attended.shape[0]
+def attend_kernel(come, turn, keys, values, later, back, new_kv, att, attended, *, width, q_cols):
+    row = pl.program_id(0)
+    blocks = come.shape[0] // back.shape[0]
+    count = back.shape[0]
+    rows = att.shape[0]
     heads = q_cols // HD
     half = HD // 2
+
+    @pl.when(row == 0)
+    def _():
+        means, spreads = [], []
+        for b in range(blocks):
+            stats = come[b * count, :, ATT - 128 : ATT].astype(F32)
+            at = [stats[:, FIRST_STAT + i : FIRST_STAT + i + 1] for i in range(6)]
+            means.append(at[0] + at[1] + at[2])
+            spreads.append(at[3] + at[4] + at[5])
+        mean = sum(means[1:], means[0]) / blocks
+        offsets = [value - mean for value in means]
+        spread = sum(v + width * o * o for v, o in zip(spreads, offsets)) / D
+        scale = lax.rsqrt(spread + 1e-05)
+        total = jnp.zeros((count, rows, ATT), F32)
+        for b in range(blocks):
+            at = slice(b * count, (b + 1) * count)
+            sums = jnp.concatenate(
+                [come[at, i : i + 1, ATT : ATT + SUMS_ATT] for i in range(ATT // SUMS_ATT)], axis=2
+            )
+            total = total + come[at, :, :ATT].astype(F32) + offsets[b][None] * sums.astype(F32)
+            back[:, 8 + b : 9 + b, :] = jnp.concatenate(
+                [come[at, i : i + 1, ATT + SUMS_ATT :] for i in range(rows)], axis=2
+            )
+        total = (total * scale[None]).astype(BF16)
+        for r in range(rows):
+            att[r] = total[:, r, :]
+        lane = lax.broadcasted_iota(jnp.int32, (rows, back.shape[2]), 1)
+        line = lax.broadcasted_iota(jnp.int32, (rows, back.shape[2]), 0)
+        pieces = list(offsets)
+        rest = scale
+        for _ in range(3):
+            pieces.append(rest.astype(BF16).astype(F32))
+            rest = rest - pieces[-1]
+        extra = jnp.zeros(lane.shape, F32)
+        for i, piece in enumerate(pieces):
+            extra = extra + jnp.where(lane == i * rows + line, piece, 0.0)
+        extra = jnp.sum(extra, axis=0, keepdims=True).astype(BF16)
+        back[:, rows:8, :] = jnp.broadcast_to(extra[None], (count, 8 - rows, back.shape[2]))
+
     cos_part, sin_part = turn[0:1, :], turn[1:2, :]
 
     def rotated(v):
@@ -264,12 +319,13 @@
             [first * cos_part - second * sin_part, first * sin_part + second * cos_part], axis=1
         )
 
-    mine = att[0].astype(F32)
+    mine = att[row].astype(F32)
     queries = jnp.concatenate([mine[:, h * HD : (h + 1) * HD] for h in range(heads)], axis=0)
     queries = (rotated(queries) * HD ** (-0.5)).astype(BF16)
-    key = jnp.concatenate([mine[j : j + 1, q_cols:] for j in range(4)], axis=1)
+    part = 2 * HD // count
+    key = jnp.concatenate([mine[j : j + 1, q_cols : q_cols + part] for j in range(4)], axis=1)
     key = rotated(key).astype(BF16)
-    value = jnp.concatenate([mine[j : j + 1, q_cols:] for j in range(4, 8)], axis=1)
+    value = jnp.concatenate([mine[j : j + 1, q_cols : q_cols + part] for j in range(4, 8)], axis=1)
     new_kv[0, :, :HD] = key
     new_kv[0, :, HD:] = value.astype(BF16)
     scores = lax.dot_general(
@@ -283,34 +339,36 @@
     probs = (weights / sums).astype(BF16)
     mixed = dot(probs, values[0]) + (own_w / sums).astype(BF16).astype(F32) * value
     for h in range(heads):
-        attended[:, 0, 0, h * HD : (h + 1) * HD] = mixed[h * count : (h + 1) * count].astype(BF16)
-
-
-def attend(att, q_cols, key_cache, value_cache, later):
+        attended[row, :, h * HD : (h + 1) * HD] = mixed[h * count : (h + 1) * count].astype(BF16)
+
+    @pl.when(row == rows - 1)
+    def _():
+        for r in range(rows):
+            back[:, r, :] = attended[r]
+
+
+def attend(come, count, width, q_cols, key_cache, value_cache, later):
     half = HD // 2
     freqs = 10000.0 ** (-jnp.arange(half, dtype=F32) / half)
     angles = F32(key_cache.shape[1]) * freqs
     turn = jnp.stack([jnp.cos(angles), jnp.sin(angles)])
-    rows, count, cols = att.shape
+    rows = come.shape[1]
+    blocks = come.shape[0] // count
     cache = pl.BlockSpec((1,) + key_cache.shape[1:], lambda r: (r, 0, 0))
-    return pl.pallas_call(
-        attend_kernel,
+    back = shape((count, 8 + blocks, q_cols))
+    return pl.pallas_call(
+        functools.partial(attend_kernel, width=width, q_cols=q_cols),
         grid=(rows,),
-        in_specs=[
-            pl.BlockSpec((1, count, cols), lambda r: (r, 0, 0)),
-            pl.BlockSpec(turn.shape, lambda r: (0, 0)),
-            cache,
-            cache,
-            pl.BlockSpec(memory_space=pl.ANY),
+        in_specs=[whole(come), whole(turn), cache, cache, pl.BlockSpec(memory_space=pl.ANY)],
+        out_specs=[whole(back), pl.BlockSpec((1, 1, 2 * HD), lambda r: (r, 0, 0))],
+        out_shape=[back, shape((rows, 1, 2 * HD))],
+        scratch_shapes=[
+            pltpu.VMEM((rows, count, ATT), BF16),
+            pltpu.VMEM((rows, count, q_cols), BF16),
         ],
-        out_specs=[
-            pl.BlockSpec((count, 1, 1, q_cols), lambda r: (0, r, 0, 0)),
-            pl.BlockSpec((1, 1, 2 * HD), lambda r: (r, 0, 0)),
-        ],
-        out_shape=[shape((count, rows, 1, q_cols)), shape((rows, 1, 2 * HD))],
-        compiler_params=params(56),
+        compiler_params=params(16),
         name="attend",
-    )(att, turn, key_cache, value_cache, later)
+    )(come, turn, key_cache, value_cache, later)
 
 
 def local(tokens, w_query, w_key_value, w_gate, w_up, w_attn_out, w_down, key_cache, value_cache):
@@ -329,12 +387,10 @@
 
     ones = jnp.ones((8, width), BF16)
     sums = [dot(ones, w)[:1].astype(BF16) for w in (w_query, w_key_value, w_gate, w_up)]
-    sums_att = jnp.concatenate(sums[:2], axis=1).reshape(1, 4, -1)
-    sums_hid = jnp.concatenate(sums[2:], axis=1).reshape(count_gy, 4, -1)
-    sums_att = jnp.broadcast_to(sums_att, (count_gy,) + sums_att.shape[1:])
+    sums_att = jnp.pad(jnp.concatenate(sums[:2], axis=1), ((0, 0), (0, 4 * SUMS_ATT - att_cols)))
+    sums_att = jnp.broadcast_to(sums_att.reshape(1, 4, SUMS_ATT), (count_gy, 4, SUMS_ATT))
+    sums_hid = jnp.concatenate(sums[2:], axis=1).reshape(count_gy, 4, SUMS_HID)
     riders = jnp.concatenate([sums_att, sums_hid], axis=2)
-    ride = riders.shape[2]
-    riders = jnp.pad(riders, ((0, 0), (0, 0), (0, RIDE - ride)))
 
     position = jnp.stack([z, y, x, core]).astype(jnp.int32)
     strip = jnp.stack(gather_direct(tokens, ring_x, "gy"))
@@ -345,52 +401,28 @@
     later = att
     att = lax.all_to_all(att, ("gx", "gy"), 0, 0)
 
-    left_z, right_z, ahead_z, own_z, behind_z = products(by_z, w_gate, w_up, 0, HID_Z, later)
-    left_y, right_y, ahead_y, own_y, behind_y = products(by_y, w_gate, w_up, HID_Z, hid_y, own_z)
-    left_z = send(left_z, ring_z(1))
-    right_z = send(right_z, ring_z(-1))
-    left_y = send(left_y, ring_y(1))
-    right_y = send(right_y, ring_y(-1))
-
-    ahead_z, behind_z = second(left_z, right_z, ahead_z, behind_z, att)
-    ahead_y, behind_y = second(left_y, right_y, ahead_y, behind_y, ahead_z)
-
-    att = att.reshape(count_gx, count_gy, rows_dev, ATT + RIDE)
-    quarter = att_cols // 4
-    stats = att[:, 0, :, ATT + ride : ATT + ride + 6].astype(F32)
-    means = stats[:, :, 0] + stats[:, :, 1] + stats[:, :, 2]
-    spread = stats[:, :, 3] + stats[:, :, 4] + stats[:, :, 5]
-    offsets = means - jnp.mean(means, axis=0)
-    spread = jnp.sum(spread + width * offsets * offsets, axis=0) / D
-    scale = lax.rsqrt(spread + 1e-05)
-    offsets = offsets.astype(BF16)
-    sums_att = att[:, :, :, ATT : ATT + quarter].reshape(count_gx, count_gy, att_cols)
-    sums_hid = att[:, :, :, ATT + quarter : ATT + ride].reshape(count_gx, count_gy, q_cols)
-    high = scale.astype(BF16)
-    rest = scale - high.astype(F32)
-    middle = rest.astype(BF16)
-    low = (rest - middle.astype(F32)).astype(BF16)
-    extra = jnp.concatenate([offsets.reshape(-1), high, middle, low])
-    n_off = offsets.size
-    extra = jnp.pad(extra, (0, q_cols - extra.size)).reshape(1, 1, q_cols)
-    extra = jnp.broadcast_to(extra, (count_gy, 8 - rows_dev, q_cols))
-
-    att = jnp.sum(att[:, :, :, :att_cols].astype(F32), axis=0) + jnp.einsum(
-        "br,bjc->jrc", offsets, sums_att, preferred_element_type=F32
-    )
-    att = (att * scale[:, None]).astype(BF16).transpose(1, 0, 2)
-    ahead_y = send(ahead_y, ring_y(1))
-    behind_y = send(behind_y, ring_y(-1))
-    attended, new_kv = attend(att, q_cols, key_cache, value_cache, later)
+    ahead_z, behind_z, gate_z, up_z, own_z = products(by_z, w_gate, w_up, 0, HID_Z, later)
+    ahead_y, behind_y, gate_y, up_y, own_y = products(by_y, w_gate, w_up, HID_Z, hid_y, own_z)
+    left_z = send(ahead_z, ring_z(1))
+    right_z = send(behind_z, ring_z(-1))
+    left_y = send(ahead_y, ring_y(1))
+    right_y = send(behind_y, ring_y(-1))
+
+    back, new_kv = attend(att, count_gy, width, q_cols, key_cache, value_cache, own_y)
     new_kv = new_kv.reshape(rows_dev, 2 * HD)
-    back = jnp.concatenate(
-        [attended.reshape(count_gy, rows_dev, q_cols), extra, sums_hid.transpose(1, 0, 2)], axis=1
-    )
+    attended = back
     back = lax.all_to_all(back, "gy", 0, 0)
-    total_z = total(own_z, send(ahead_z, ring_z(1)), send(behind_z, ring_z(-1)), back)
-    total_y = total(own_y, ahead_y, behind_y, back)
+
+    gate_z, up_z = second(left_z, right_z, gate_z, up_z, attended)
+    gate_y, up_y = second(left_y, right_y, gate_y, up_y, gate_z)
+    gate_z, up_z = send(gate_z, ring_z(1)), send(up_z, ring_z(-1))
+    gate_y, up_y = send(gate_y, ring_y(1)), send(up_y, ring_y(-1))
+    total_z = total(own_z, left_z, right_z, gate_z, up_z, back)
+    total_y = total(own_y, left_y, right_y, gate_y, up_y, back)
+
     attended = back[:, :rows_dev].reshape(CHUNK, q_cols)
     extra = back[:, rows_dev]
+    n_off = count_gx * rows_dev
     sums_hid = back[:, 8:].transpose(1, 0, 2).reshape(count_gx, -1)
     offsets = extra[:, :n_off].reshape(count_gy, count_gx, rows_dev).transpose(0, 2, 1)
     offsets = offsets.reshape(CHUNK, count_gx)

time: 179 us -> 174 us (0.972)
  waiting for transfers between devices: 52.3 us -> 40.8 us
  local copies, waits for them, and re-layouts: 9.53 us -> 14.8 us
  starting transfers between devices: 64.9 us -> 68.2 us
  other arithmetic: 6.02 us -> 3 us
    ppermute x36, waiting for transfers between devices: 41.3 us -> 32.2 us  [send(): return lax.ppermute(value, axis, pairs)]
    unnamed x43 -> x50, local copies, waits for them, and re-layouts: 4.68 us -> 13.2 us
    ppermute x36, starting transfers between devices: 50.4 us -> 54.7 us  [send(): return lax.ppermute(value, axis, pairs)]
    all_to_all x1, waiting for transfers between devices: 2.67 us -> 0.01 us  [local(): back = lax.all_to_all(back, 'gy', 0, 0)]
  transfers between devices with their start and end apart: 38 -> 38, of which waited for: 19 -> 15; matrix products, arithmetic and copies ran while one was open for 12% -> 8% of each run, Pallas kernels for 17% -> 17%
where the time goes in v3:
time: 174 us; the launch traced here: 173 us
  starting transfers between devices  68.2 us (39%)
  waiting for transfers between devices  40.8 us (23%)
  Pallas kernels  33.7 us (19%)
  local copies, waits for them, and re-layouts  14.8 us (9%)
  matrix products  10.6 us (6%)
  other arithmetic  3 us (2%)
    ppermute x36, starting transfers between devices, send(): return lax.ppermute(value, axis, pairs)  54.7 us
    ppermute x36, waiting for transfers between devices, send(): return lax.ppermute(value, axis, pairs)  32.2 us
    unnamed x50, local copies, waits for them, and re-layouts  13.2 us
    pallas_call x2, Pallas kernels, products(): pl.pallas_call(products_kernel, grid=(cols // BLOCK,), in_specs=[pl.Block...  12.3 us
    dot_general x28, matrix products, dot(): return jnp.dot(a, b, preferred_element_type=F32)  10.6 us
    all_to_all x1, starting transfers between devices, local(): att = lax.all_to_all(att, ('gx', 'gy'), 0, 0)  9.93 us
    all_to_all x1, waiting for transfers between devices, local(): att = lax.all_to_all(att, ('gx', 'gy'), 0, 0)  8.59 us
    pallas_call x1, Pallas kernels, attend(): pl.pallas_call(functools.partial(attend_kernel, width=width, q_cols=q_col...  7.03 us
  transfers between devices with their start and end apart: 38, of which 15 were waited for; matrix products, arithmetic and copies ran while one was open for 8% of the time, Pallas kernels for 17%

profile of v3, /device:TPU:0, one launch (start us, length us, event | category | flops | bytes accessed | tf_op | source)
XLA Modules:
  0.0 172.5 jit_solution(1017838626046119091)
XLA Ops:
  2.3 2.7 %collective-permute-start.1 = (bf16[64,512]{1,0:T(8,128)(2,1)}, bf16[64,512]{1,0:T(8,128)(2,1)S(1)}, u32[]{:S(2)}, u32[]{:S(2)}) collective-permute-start(bf16[64,512]{1,0:T(8,128)(2,1)} %param.9), channel_id=1, source_target_pairs={{0,4},{1,5},{2,6},{3,7},{4,0},{5,1},{6,2},{7,3},{8,12},{9,13},{10,... | collective-permute-start | bytes 196616 | tf_op jit(solution)/shard_map/ppermute | solution.py:46
  6.5 2.8 %fusion.71 = bf16[8,4096]{1,0:T(8,128)(2,1)S(1)} fusion(bf16[512,4096]{1,0:T(8,128)(2,1)} %up.3), kind=kOutput, calls=%fused_computation.129 | convolution fusion | flops 33554432 | bytes 4259840 | tf_op jit(solution)/shard_map/dot_general | solution.py:70
  12.9 2.8 %queries.1.later = bf16[128,4,1792]{2,1,0:T(4,128)(2,1)} custom-call(s32[4]{0:T(128)S(1)} %pad_add_fusion.place, bf16[512,512]{1,0:T(8,128)(2,1)S(1)} %get-tuple-element.29.rows, bf16[512,1024]{1,0:T(8,128)(2,1)S(1)} %copy-done.5, bf16[512,64]{1,0:T(8,128)(2,1)S(1)} %copy.19.keyval, bf16[8,4,640]{2,1,0:T(4,128)(2,1)S(1)} %pad_maximum_fusion.7.riders, ...), custom_call_target="tpu_custom_call" | custom-call | tf_op jit(solution)/shard_map/queries/pallas_call | solution.py:152
  15.7 9.9 %all-to-all-start = ((bf16[128,4,1792]{2,1,0:T(4,128)(2,1)}), bf16[128,4,1792]{2,1,0:T(4,128)(2,1)S(1)}, u32[]{:S(2)}, u32[]{:S(2)}) async-start(bf16[128,4,1792]{2,1,0:T(4,128)(2,1)} %queries.1.later), calls=%async_computation | async-start | bytes 3670016 | tf_op jit(solution)/shard_map/all_to_all | solution.py:402
  25.7 6.0 %products.2 = (bf16[2,128,2048]{2,1,0:T(8,128)(2,1)}, bf16[2,128,2048]{2,1,0:T(8,128)(2,1)}, bf16[128,2048]{1,0:T(8,128)(2,1)}, bf16[128,2048]{1,0:T(8,128)(2,1)}, bf16[2,128,2048]{2,1,0:T(8,128)(2,1)}) custom-call(bf16[512,512]{1,0:T(8,128)(2,1)} %copy-done.6, bf16[512,4096]{1,0:T(8,128)(2,1)} %gate.3, bf16[512,4096]{1,0:T(8,128)(2,1)} %up.3, ...), custom_call_target="tpu_custom_call" | custom-call | tf_op jit(solution)/shard_map/products/pallas_call | solution.py:181
  32.9 2.2 %collective-permute-start.5 = (bf16[2,128,2048]{2,1,0:T(8,128)(2,1)}, bf16[2,128,2048]{2,1,0:T(8,128)(2,1)}, u32[]{:S(2)}, u32[]{:S(2)}) collective-permute-start(bf16[2,128,2048]{2,1,0:T(8,128)(2,1)} %get-tuple-element.33), channel_id=1, source_target_pairs={{0,96},{8,104},{16,112},{24,120},{32,0},{40,8},{48,16},{56,24},{64... | collective-permute-start | bytes 3145736 | tf_op jit(solution)/shard_map/ppermute | solution.py:46
  35.0 6.3 %products.3 = (bf16[2,128,2048]{2,1,0:T(8,128)(2,1)}, bf16[2,128,2048]{2,1,0:T(8,128)(2,1)}, bf16[128,2048]{1,0:T(8,128)(2,1)}, bf16[128,2048]{1,0:T(8,128)(2,1)}, bf16[2,128,2048]{2,1,0:T(8,128)(2,1)}) custom-call(bf16[512,512]{1,0:T(8,128)(2,1)} %copy-done.11, bf16[512,4096]{1,0:T(8,128)(2,1)} %gate.3, bf16[512,4096]{1,0:T(8,128)(2,1)} %up.3, ...), custom_call_target="tpu_custom_call" | custom-call | tf_op jit(solution)/shard_map/products/pallas_call | solution.py:181
  42.6 2.0 %collective-permute-start.19 = (bf16[2,128,2048]{2,1,0:T(8,128)(2,1)}, bf16[2,128,2048]{2,1,0:T(8,128)(2,1)}, u32[]{:S(2)}, u32[]{:S(2)}) collective-permute-start(bf16[2,128,2048]{2,1,0:T(8,128)(2,1)} %get-tuple-element.46), channel_id=1, source_target_pairs={{0,24},{8,0},{16,8},{24,16},{32,56},{40,32},{48,40},{56,48},{64,88... | collective-permute-start | bytes 3145736 | tf_op jit(solution)/shard_map/ppermute | solution.py:46
  44.7 8.6 %all-to-all-done.come = bf16[128,4,1792]{2,1,0:T(4,128)(2,1)S(1)} async-done(((bf16[128,4,1792]{2,1,0:T(4,128)(2,1)}), bf16[128,4,1792]{2,1,0:T(4,128)(2,1)S(1)}, u32[]{:S(2)}, u32[]{:S(2)}) %all-to-all-start) | async-done | bytes 1835040 | tf_op jit(solution)/shard_map/all_to_all | solution.py:402
  53.3 2.2 %copy-done = bf16[4,2048,256]{2,1,0:T(8,128)(2,1)S(1)} copy-done((bf16[4,2048,256]{2,1,0:T(8,128)(2,1)S(1)}, bf16[4,2048,256]{2,1,0:T(8,128)(2,1)}, u32[]{:S(2)}) %copy-start) | copy-done | bytes 4194328
  55.4 2.2 %copy-done.1 = bf16[4,2048,256]{2,1,0:T(8,128)(2,1)S(1)} copy-done((bf16[4,2048,256]{2,1,0:T(8,128)(2,1)S(1)}, bf16[4,2048,256]{2,1,0:T(8,128)(2,1)}, u32[]{:S(2)}) %copy-start.1) | copy-done | bytes 4194328
  58.9 7.0 %attend.1 = (bf16[8,24,1024]{2,1,0:T(8,128)(2,1)}, bf16[4,1,512]{2,1,0:T(2,128)(2,1)S(1)}) custom-call(bf16[128,4,1792]{2,1,0:T(4,128)(2,1)S(1)} %all-to-all-done.come, f32[2,128]{1,0:T(2,128)S(1)} %pad_maximum_fusion.8.turn, bf16[4,2048,256]{2,1,0:T(8,128)(2,1)S(1)} %copy-done, bf16[4,2048,256]{2,1,0:T(8,128)(2,1)S(1)} %copy-done.1, ...), custom_call_target="tpu_custom_call" | custom-call | tf_op jit(solution)/shard_map/attend/pallas_call | solution.py:359
  65.9 3.6 %all-to-all-start.1 = ((bf16[8,24,1024]{2,1,0:T(8,128)(2,1)}), bf16[8,24,1024]{2,1,0:T(8,128)(2,1)S(1)}, u32[]{:S(2)}, u32[]{:S(2)}) async-start(bf16[8,24,1024]{2,1,0:T(8,128)(2,1)} %get-tuple-element.38.later), calls=%async_computation.1 | async-start | bytes 786432 | tf_op jit(solution)/shard_map/all_to_all | solution.py:414
  69.5 2.4 %collective-permute-done.4.left = bf16[2,128,2048]{2,1,0:T(8,128)(2,1)} collective-permute-done((bf16[2,128,2048]{2,1,0:T(8,128)(2,1)}, bf16[2,128,2048]{2,1,0:T(8,128)(2,1)}, u32[]{:S(2)}, u32[]{:S(2)}) %collective-permute-start.4) | collective-permute-done | bytes 1048608 | tf_op jit(solution)/shard_map/ppermute | solution.py:46
  73.0 2.3 %second.2 = (bf16[128,2048]{1,0:T(8,128)(2,1)}, bf16[128,2048]{1,0:T(8,128)(2,1)}) custom-call(bf16[2,128,2048]{2,1,0:T(8,128)(2,1)} %collective-permute-done.4.left, bf16[2,128,2048]{2,1,0:T(8,128)(2,1)} %collective-permute-done.5.right, bf16[128,2048]{1,0:T(8,128)(2,1)S(1)} %copy-done.9, bf16[128,2048]{1,0:T(8,128)(2,1)S(1)} %copy-done.10, ...), custom_call_target="tpu_custom_call" | custom-call | tf_op jit(solution)/shard_map/second/pallas_call | solution.py:209
  75.7 2.8 %collective-permute-start.7 = (bf16[128,2048]{1,0:T(8,128)(2,1)}, bf16[128,2048]{1,0:T(8,128)(2,1)}, u32[]{:S(2)}, u32[]{:S(2)}) collective-permute-start(bf16[128,2048]{1,0:T(8,128)(2,1)} %get-tuple-element.40), channel_id=1, source_target_pairs={{0,96},{8,104},{16,112},{24,120},{32,0},{40,8},{48,16},{56,24},{64... | collective-permute-start | bytes 1572872 | tf_op jit(solution)/shard_map/ppermute | solution.py:46
  78.6 2.1 %second.3 = (bf16[128,2048]{1,0:T(8,128)(2,1)}, bf16[128,2048]{1,0:T(8,128)(2,1)}) custom-call(bf16[2,128,2048]{2,1,0:T(8,128)(2,1)S(1)} %collective-permute-done.18.left, bf16[2,128,2048]{2,1,0:T(8,128)(2,1)} %collective-permute-done.19.right, bf16[128,2048]{1,0:T(8,128)(2,1)S(1)} %copy-done.7, bf16[128,2048]{1,0:T(8,128)(2,1)S(1)} %copy-done.8, ...), custom_call_target="tpu_custom_call" | custom-call | tf_op jit(solution)/shard_map/second/pallas_call | solution.py:209
  81.4 2.6 %collective-permute-start.21 = (bf16[128,2048]{1,0:T(8,128)(2,1)}, bf16[128,2048]{1,0:T(8,128)(2,1)}, u32[]{:S(2)}, u32[]{:S(2)}) collective-permute-start(bf16[128,2048]{1,0:T(8,128)(2,1)} %get-tuple-element.50), channel_id=1, source_target_pairs={{0,24},{8,0},{16,8},{24,16},{32,56},{40,32},{48,40},{56,48},{64,88... | collective-permute-start | bytes 1572872 | tf_op jit(solution)/shard_map/ppermute | solution.py:46
  84.7 6.0 %collective-permute-done.6.gate = bf16[128,2048]{1,0:T(8,128)(2,1)} collective-permute-done((bf16[128,2048]{1,0:T(8,128)(2,1)}, bf16[128,2048]{1,0:T(8,128)(2,1)}, u32[]{:S(2)}, u32[]{:S(2)}) %collective-permute-start.6) | collective-permute-done | bytes 524320 | tf_op jit(solution)/shard_map/ppermute | solution.py:46
  92.0 2.3 %total.2 = (bf16[2,32,2048]{2,1,0:T(8,128)(2,1)S(1)}, bf16[2,32,2048]{2,1,0:T(8,128)(2,1)}, bf16[2,32,2048]{2,1,0:T(8,128)(2,1)S(1)}, bf16[2,32,2048]{2,1,0:T(8,128)(2,1)S(1)}) custom-call(bf16[2,128,2048]{2,1,0:T(8,128)(2,1)S(1)} %copy-done.4, bf16[2,128,2048]{2,1,0:T(8,128)(2,1)} %collective-permute-done.4.left, ...), custom_call_target="tpu_custom_call" | custom-call | tf_op jit(solution)/shard_map/total/pallas_call | solution.py:230
  97.2 2.6 %collective-permute-start.9 = (bf16[2,32,2048]{2,1,0:T(8,128)(2,1)}, bf16[2,32,2048]{2,1,0:T(8,128)(2,1)}, u32[]{:S(2)}, u32[]{:S(2)}) collective-permute-start(bf16[2,32,2048]{2,1,0:T(8,128)(2,1)} %copy-done.16), channel_id=1, source_target_pairs={{0,24},{8,0},{16,8},{24,16},{32,56},{40,32},{48,40},{56,48},{64,88... | collective-permute-start | bytes 786440 | tf_op jit(solution)/shard_map/ppermute | solution.py:46
  104.5 3.3 %collective-permute-start.23 = (bf16[2,32,2048]{2,1,0:T(8,128)(2,1)}, bf16[2,32,2048]{2,1,0:T(8,128)(2,1)S(1)}, u32[]{:S(2)}, u32[]{:S(2)}) collective-permute-start(bf16[2,32,2048]{2,1,0:T(8,128)(2,1)} %copy-done.17), channel_id=1, source_target_pairs={{0,96},{8,104},{16,112},{24,120},{32,0},{40,8},{48,16},{56,24},{64... | collective-permute-start | bytes 786440 | tf_op jit(solution)/shard_map/ppermute | solution.py:46
  115.0 3.2 %collective-permute-start.12 = (bf16[2,32,1280]{2,1,0:T(8,128)(2,1)S(1)}, bf16[2,32,1280]{2,1,0:T(8,128)(2,1)S(1)}, u32[]{:S(2)}, u32[]{:S(2)}) collective-permute-start(bf16[2,32,1280]{2,1,0:T(8,128)(2,1)S(1)} %hidden.2), channel_id=1, source_target_pairs={{0,16},{8,24},{16,0},{24,8},{32,48},{40,56},{48,32},{56,40},{64,80... | collective-permute-start | bytes 491528 | tf_op jit(solution)/shard_map/ppermute | solution.py:46
  120.5 3.0 %collective-permute-start.26 = (bf16[2,32,1280]{2,1,0:T(8,128)(2,1)S(1)}, bf16[2,32,1280]{2,1,0:T(8,128)(2,1)S(1)}, u32[]{:S(2)}, u32[]{:S(2)}) collective-permute-start(bf16[2,32,1280]{2,1,0:T(8,128)(2,1)S(1)} %hidden.3), channel_id=1, source_target_pairs={{0,64},{8,72},{16,80},{24,88},{32,96},{40,104},{48,112},{56,120},{... | collective-permute-start | bytes 491528 | tf_op jit(solution)/shard_map/ppermute | solution.py:46
  123.6 2.1 %collective-permute-start.15 = (bf16[2,128,1280]{2,1,0:T(8,128)(2,1)S(1)}, bf16[2,128,1280]{2,1,0:T(8,128)(2,1)S(1)}, u32[]{:S(2)}, u32[]{:S(2)}) collective-permute-start(bf16[2,128,1280]{2,1,0:T(8,128)(2,1)S(1)} %pad_maximum_fusion.2), channel_id=1, source_target_pairs={{0,32},{8,40},{16,48},{24,56},{32,64},{40,72},{48,80},{56,88},{64,... | collective-permute-start | bytes 1966088 | tf_op jit(solution)/shard_map/ppermute | solution.py:46
  127.2 4.8 %collective-permute-done.26 = bf16[2,32,1280]{2,1,0:T(8,128)(2,1)S(1)} collective-permute-done((bf16[2,32,1280]{2,1,0:T(8,128)(2,1)S(1)}, bf16[2,32,1280]{2,1,0:T(8,128)(2,1)S(1)}, u32[]{:S(2)}, u32[]{:S(2)}) %collective-permute-start.26) | collective-permute-done | bytes 163872 | tf_op jit(solution)/shard_map/ppermute | solution.py:46
  132.2 2.1 %collective-permute-start.29 = (bf16[2,128,1280]{2,1,0:T(8,128)(2,1)S(1)}, bf16[2,128,1280]{2,1,0:T(8,128)(2,1)S(1)}, u32[]{:S(2)}, u32[]{:S(2)}) collective-permute-start(bf16[2,128,1280]{2,1,0:T(8,128)(2,1)S(1)} %pad_maximum_fusion.3), channel_id=1, source_target_pairs={{0,8},{8,16},{16,24},{24,0},{32,40},{40,48},{48,56},{56,32},{64,72... | collective-permute-start | bytes 1966088 | tf_op jit(solution)/shard_map/ppermute | solution.py:46
  137.3 4.7 %collective-permute-done.14 = bf16[2,128,1280]{2,1,0:T(8,128)(2,1)S(1)} collective-permute-done((bf16[2,128,1280]{2,1,0:T(8,128)(2,1)S(1)}, bf16[2,128,1280]{2,1,0:T(8,128)(2,1)S(1)}, u32[]{:S(2)}, u32[]{:S(2)}) %collective-permute-start.14) | collective-permute-done | bytes 655392 | tf_op jit(solution)/shard_map/ppermute | solution.py:46
  142.0 3.6 %collective-permute-start.17 = (bf16[128,1280]{1,0:T(8,128)(2,1)S(1)}, bf16[128,1280]{1,0:T(8,128)(2,1)S(1)}, u32[]{:S(2)}, u32[]{:S(2)}) collective-permute-start(bf16[128,1280]{1,0:T(8,128)(2,1)S(1)} %slice_bitcast_fusion.10), channel_id=1, source_target_pairs={{0,96},{8,104},{16,112},{24,120},{32,0},{40,8},{48,16},{56,24},{64... | collective-permute-start | bytes 983048 | tf_op jit(solution)/shard_map/ppermute | solution.py:46
  151.9 3.0 %collective-permute-done.31 = bf16[128,1280]{1,0:T(8,128)(2,1)S(1)} collective-permute-done((bf16[128,1280]{1,0:T(8,128)(2,1)S(1)}, bf16[128,1280]{1,0:T(8,128)(2,1)S(1)}, u32[]{:S(2)}, u32[]{:S(2)}) %collective-permute-start.31) | collective-permute-done | bytes 327712 | tf_op jit(solution)/shard_map/ppermute | solution.py:46
  161.1 3.4 %collective-permute-start.35 = (bf16[64,512]{1,0:T(8,128)(2,1)S(1)}, bf16[64,512]{1,0:T(8,128)(2,1)S(1)}, u32[]{:S(2)}, u32[]{:S(2)}) collective-permute-start(bf16[64,512]{1,0:T(8,128)(2,1)S(1)} %get-tuple-element.62), channel_id=1, source_target_pairs={{0,4},{1,5},{2,6},{3,7},{4,0},{5,1},{6,2},{7,3},{8,12},{9,13},{10,... | collective-permute-start | bytes 196616 | tf_op jit(solution)/shard_map/ppermute | solution.py:46
  168.8 3.1 %collective-permute-done.33 = bf16[64,512]{1,0:T(8,128)(2,1)S(1)} collective-permute-done((bf16[64,512]{1,0:T(8,128)(2,1)S(1)}, bf16[64,512]{1,0:T(8,128)(2,1)S(1)}, u32[]{:S(2)}, u32[]{:S(2)}) %collective-permute-start.33) | collective-permute-done | bytes 65568 | tf_op jit(solution)/shard_map/ppermute | solution.py:46
  (182 shorter events, 53.2 us)
Async XLA Ops:
  0.7 9.6 %collective-permute-start.2 = (bf16[64,512]{1,0:T(8,128)(2,1)}, bf16[64,512]{1,0:T(8,128)(2,1)S(1)}, u32[]{:S(2)}, u32[]{:S(2)}) collective-permute-start(bf16[64,512]{1,0:T(8,128)(2,1)} %param.9), channel_id=1, source_target_pairs={{0,2},{1,3},{2,4},{3,5},{4,6},{5,7},{6,0},{7,1},{8,10},{9,11},{10,... | collective-permute-start | bytes 196616 | tf_op jit(solution)/shard_map/ppermute | solution.py:46
  2.3 7.9 %collective-permute-start.1 = (bf16[64,512]{1,0:T(8,128)(2,1)}, bf16[64,512]{1,0:T(8,128)(2,1)S(1)}, u32[]{:S(2)}, u32[]{:S(2)}) collective-permute-start(bf16[64,512]{1,0:T(8,128)(2,1)} %param.9), channel_id=1, source_target_pairs={{0,4},{1,5},{2,6},{3,7},{4,0},{5,1},{6,2},{7,3},{8,12},{9,13},{10,... | collective-permute-start | bytes 196616 | tf_op jit(solution)/shard_map/ppermute | solution.py:46
  15.7 37.5 %all-to-all-start = ((bf16[128,4,1792]{2,1,0:T(4,128)(2,1)}), bf16[128,4,1792]{2,1,0:T(4,128)(2,1)S(1)}, u32[]{:S(2)}, u32[]{:S(2)}) async-start(bf16[128,4,1792]{2,1,0:T(4,128)(2,1)} %queries.1.later), calls=%async_computation | async-start | bytes 3670016 | tf_op jit(solution)/shard_map/all_to_all | solution.py:402
  31.7 40.3 %collective-permute-start.4 = (bf16[2,128,2048]{2,1,0:T(8,128)(2,1)}, bf16[2,128,2048]{2,1,0:T(8,128)(2,1)}, u32[]{:S(2)}, u32[]{:S(2)}) collective-permute-start(bf16[2,128,2048]{2,1,0:T(8,128)(2,1)} %get-tuple-element.32), channel_id=1, source_target_pairs={{0,32},{8,40},{16,48},{24,56},{32,64},{40,72},{48,80},{56,88},{64,... | collective-permute-start | bytes 3145736 | tf_op jit(solution)/shard_map/ppermute | solution.py:46
  32.9 39.1 %collective-permute-start.5 = (bf16[2,128,2048]{2,1,0:T(8,128)(2,1)}, bf16[2,128,2048]{2,1,0:T(8,128)(2,1)}, u32[]{:S(2)}, u32[]{:S(2)}) collective-permute-start(bf16[2,128,2048]{2,1,0:T(8,128)(2,1)} %get-tuple-element.33), channel_id=1, source_target_pairs={{0,96},{8,104},{16,112},{24,120},{32,0},{40,8},{48,16},{56,24},{64... | collective-permute-start | bytes 3145736 | tf_op jit(solution)/shard_map/ppermute | solution.py:46
  41.3 37.3 %collective-permute-start.18 = (bf16[2,128,2048]{2,1,0:T(8,128)(2,1)}, bf16[2,128,2048]{2,1,0:T(8,128)(2,1)S(1)}, u32[]{:S(2)}, u32[]{:S(2)}) collective-permute-start(bf16[2,128,2048]{2,1,0:T(8,128)(2,1)} %get-tuple-element.45), channel_id=1, source_target_pairs={{0,8},{8,16},{16,24},{24,0},{32,40},{40,48},{48,56},{56,32},{64,72... | collective-permute-start | bytes 3145736 | tf_op jit(solution)/shard_map/ppermute | solution.py:46
  42.6 36.0 %collective-permute-start.19 = (bf16[2,128,2048]{2,1,0:T(8,128)(2,1)}, bf16[2,128,2048]{2,1,0:T(8,128)(2,1)}, u32[]{:S(2)}, u32[]{:S(2)}) collective-permute-start(bf16[2,128,2048]{2,1,0:T(8,128)(2,1)} %get-tuple-element.46), channel_id=1, source_target_pairs={{0,24},{8,0},{16,8},{24,16},{32,56},{40,32},{48,40},{56,48},{64,88... | collective-permute-start | bytes 3145736 | tf_op jit(solution)/shard_map/ppermute | solution.py:46
  65.9 18.1 %all-to-all-start.1 = ((bf16[8,24,1024]{2,1,0:T(8,128)(2,1)}), bf16[8,24,1024]{2,1,0:T(8,128)(2,1)S(1)}, u32[]{:S(2)}, u32[]{:S(2)}) async-start(bf16[8,24,1024]{2,1,0:T(8,128)(2,1)} %get-tuple-element.38.later), calls=%async_computation.1 | async-start | bytes 786432 | tf_op jit(solution)/shard_map/all_to_all | solution.py:414
  75.3 15.4 %collective-permute-start.6 = (bf16[128,2048]{1,0:T(8,128)(2,1)}, bf16[128,2048]{1,0:T(8,128)(2,1)}, u32[]{:S(2)}, u32[]{:S(2)}) collective-permute-start(bf16[128,2048]{1,0:T(8,128)(2,1)} %get-tuple-element.39.later), channel_id=1, source_target_pairs={{0,32},{8,40},{16,48},{24,56},{32,64},{40,72},{48,80},{56,88},{64,... | collective-permute-start | bytes 1572872 | tf_op jit(solution)/shard_map/ppermute | solution.py:46
  75.7 15.0 %collective-permute-start.7 = (bf16[128,2048]{1,0:T(8,128)(2,1)}, bf16[128,2048]{1,0:T(8,128)(2,1)}, u32[]{:S(2)}, u32[]{:S(2)}) collective-permute-start(bf16[128,2048]{1,0:T(8,128)(2,1)} %get-tuple-element.40), channel_id=1, source_target_pairs={{0,96},{8,104},{16,112},{24,120},{32,0},{40,8},{48,16},{56,24},{64... | collective-permute-start | bytes 1572872 | tf_op jit(solution)/shard_map/ppermute | solution.py:46
  80.7 20.0 %collective-permute-start.20 = (bf16[128,2048]{1,0:T(8,128)(2,1)}, bf16[128,2048]{1,0:T(8,128)(2,1)S(1)}, u32[]{:S(2)}, u32[]{:S(2)}) collective-permute-start(bf16[128,2048]{1,0:T(8,128)(2,1)} %get-tuple-element.49), channel_id=1, source_target_pairs={{0,8},{8,16},{16,24},{24,0},{32,40},{40,48},{48,56},{56,32},{64,72... | collective-permute-start | bytes 1572872 | tf_op jit(solution)/shard_map/ppermute | solution.py:46
  81.4 19.4 %collective-permute-start.21 = (bf16[128,2048]{1,0:T(8,128)(2,1)}, bf16[128,2048]{1,0:T(8,128)(2,1)}, u32[]{:S(2)}, u32[]{:S(2)}) collective-permute-start(bf16[128,2048]{1,0:T(8,128)(2,1)} %get-tuple-element.50), channel_id=1, source_target_pairs={{0,24},{8,0},{16,8},{24,16},{32,56},{40,32},{48,40},{56,48},{64,88... | collective-permute-start | bytes 1572872 | tf_op jit(solution)/shard_map/ppermute | solution.py:46
  96.4 11.4 %collective-permute-start.8 = (bf16[2,32,2048]{2,1,0:T(8,128)(2,1)}, bf16[2,32,2048]{2,1,0:T(8,128)(2,1)}, u32[]{:S(2)}, u32[]{:S(2)}) collective-permute-start(bf16[2,32,2048]{2,1,0:T(8,128)(2,1)} %get-tuple-element.42), channel_id=1, source_target_pairs={{0,8},{8,16},{16,24},{24,0},{32,40},{40,48},{48,56},{56,32},{64,72... | collective-permute-start | bytes 786440 | tf_op jit(solution)/shard_map/ppermute | solution.py:46
  97.2 13.2 %collective-permute-start.9 = (bf16[2,32,2048]{2,1,0:T(8,128)(2,1)}, bf16[2,32,2048]{2,1,0:T(8,128)(2,1)}, u32[]{:S(2)}, u32[]{:S(2)}) collective-permute-start(bf16[2,32,2048]{2,1,0:T(8,128)(2,1)} %copy-done.16), channel_id=1, source_target_pairs={{0,24},{8,0},{16,8},{24,16},{32,56},{40,32},{48,40},{56,48},{64,88... | collective-permute-start | bytes 786440 | tf_op jit(solution)/shard_map/ppermute | solution.py:46
  99.8 11.3 %collective-permute-start.10 = (bf16[2,32,2048]{2,1,0:T(8,128)(2,1)}, bf16[2,32,2048]{2,1,0:T(8,128)(2,1)}, u32[]{:S(2)}, u32[]{:S(2)}) collective-permute-start(bf16[2,32,2048]{2,1,0:T(8,128)(2,1)} %copy-done.14), channel_id=1, source_target_pairs={{0,16},{8,24},{16,0},{24,8},{32,48},{40,56},{48,32},{56,40},{64,80... | collective-permute-start | bytes 786440 | tf_op jit(solution)/shard_map/ppermute | solution.py:46
  104.2 13.9 %collective-permute-start.22 = (bf16[2,32,2048]{2,1,0:T(8,128)(2,1)}, bf16[2,32,2048]{2,1,0:T(8,128)(2,1)S(1)}, u32[]{:S(2)}, u32[]{:S(2)}) collective-permute-start(bf16[2,32,2048]{2,1,0:T(8,128)(2,1)} %get-tuple-element.52), channel_id=1, source_target_pairs={{0,32},{8,40},{16,48},{24,56},{32,64},{40,72},{48,80},{56,88},{64,... | collective-permute-start | bytes 786440 | tf_op jit(solution)/shard_map/ppermute | solution.py:46
  104.5 14.6 %collective-permute-start.23 = (bf16[2,32,2048]{2,1,0:T(8,128)(2,1)}, bf16[2,32,2048]{2,1,0:T(8,128)(2,1)S(1)}, u32[]{:S(2)}, u32[]{:S(2)}) collective-permute-start(bf16[2,32,2048]{2,1,0:T(8,128)(2,1)} %copy-done.17), channel_id=1, source_target_pairs={{0,96},{8,104},{16,112},{24,120},{32,0},{40,8},{48,16},{56,24},{64... | collective-permute-start | bytes 786440 | tf_op jit(solution)/shard_map/ppermute | solution.py:46
  107.8 11.3 %collective-permute-start.24 = (bf16[2,32,2048]{2,1,0:T(8,128)(2,1)}, bf16[2,32,2048]{2,1,0:T(8,128)(2,1)S(1)}, u32[]{:S(2)}, u32[]{:S(2)}) collective-permute-start(bf16[2,32,2048]{2,1,0:T(8,128)(2,1)} %copy-done.15), channel_id=1, source_target_pairs={{0,64},{8,72},{16,80},{24,88},{32,96},{40,104},{48,112},{56,120},{... | collective-permute-start | bytes 786440 | tf_op jit(solution)/shard_map/ppermute | solution.py:46
  113.6 9.9 %collective-permute-start.13 = (bf16[2,32,1280]{2,1,0:T(8,128)(2,1)S(1)}, bf16[2,32,1280]{2,1,0:T(8,128)(2,1)S(1)}, u32[]{:S(2)}, u32[]{:S(2)}) collective-permute-start(bf16[2,32,1280]{2,1,0:T(8,128)(2,1)S(1)} %hidden.2), channel_id=1, source_target_pairs={{0,8},{8,16},{16,24},{24,0},{32,40},{40,48},{48,56},{56,32},{64,72... | collective-permute-start | bytes 491528 | tf_op jit(solution)/shard_map/ppermute | solution.py:46
  115.0 8.6 %collective-permute-start.12 = (bf16[2,32,1280]{2,1,0:T(8,128)(2,1)S(1)}, bf16[2,32,1280]{2,1,0:T(8,128)(2,1)S(1)}, u32[]{:S(2)}, u32[]{:S(2)}) collective-permute-start(bf16[2,32,1280]{2,1,0:T(8,128)(2,1)S(1)} %hidden.2), channel_id=1, source_target_pairs={{0,16},{8,24},{16,0},{24,8},{32,48},{40,56},{48,32},{56,40},{64,80... | collective-permute-start | bytes 491528 | tf_op jit(solution)/shard_map/ppermute | solution.py:46
  119.4 7.8 %collective-permute-start.27 = (bf16[2,32,1280]{2,1,0:T(8,128)(2,1)S(1)}, bf16[2,32,1280]{2,1,0:T(8,128)(2,1)S(1)}, u32[]{:S(2)}, u32[]{:S(2)}) collective-permute-start(bf16[2,32,1280]{2,1,0:T(8,128)(2,1)S(1)} %hidden.3), channel_id=1, source_target_pairs={{0,32},{8,40},{16,48},{24,56},{32,64},{40,72},{48,80},{56,88},{64,... | collective-permute-start | bytes 491528 | tf_op jit(solution)/shard_map/ppermute | solution.py:46
  120.5 11.5 %collective-permute-start.26 = (bf16[2,32,1280]{2,1,0:T(8,128)(2,1)S(1)}, bf16[2,32,1280]{2,1,0:T(8,128)(2,1)S(1)}, u32[]{:S(2)}, u32[]{:S(2)}) collective-permute-start(bf16[2,32,1280]{2,1,0:T(8,128)(2,1)S(1)} %hidden.3), channel_id=1, source_target_pairs={{0,64},{8,72},{16,80},{24,88},{32,96},{40,104},{48,112},{56,120},{... | collective-permute-start | bytes 491528 | tf_op jit(solution)/shard_map/ppermute | solution.py:46
  123.5 8.6 %collective-permute-start.25 = (bf16[2,32,1280]{2,1,0:T(8,128)(2,1)S(1)}, bf16[2,32,1280]{2,1,0:T(8,128)(2,1)S(1)}, u32[]{:S(2)}, u32[]{:S(2)}) collective-permute-start(bf16[2,32,1280]{2,1,0:T(8,128)(2,1)S(1)} %hidden.3), channel_id=1, source_target_pairs={{0,96},{8,104},{16,112},{24,120},{32,0},{40,8},{48,16},{56,24},{64... | collective-permute-start | bytes 491528 | tf_op jit(solution)/shard_map/ppermute | solution.py:46
  123.6 22.0 %collective-permute-start.15 = (bf16[2,128,1280]{2,1,0:T(8,128)(2,1)S(1)}, bf16[2,128,1280]{2,1,0:T(8,128)(2,1)S(1)}, u32[]{:S(2)}, u32[]{:S(2)}) collective-permute-start(bf16[2,128,1280]{2,1,0:T(8,128)(2,1)S(1)} %pad_maximum_fusion.2), channel_id=1, source_target_pairs={{0,32},{8,40},{16,48},{24,56},{32,64},{40,72},{48,80},{56,88},{64,... | collective-permute-start | bytes 1966088 | tf_op jit(solution)/shard_map/ppermute | solution.py:46
  125.7 16.3 %collective-permute-start.14 = (bf16[2,128,1280]{2,1,0:T(8,128)(2,1)S(1)}, bf16[2,128,1280]{2,1,0:T(8,128)(2,1)S(1)}, u32[]{:S(2)}, u32[]{:S(2)}) collective-permute-start(bf16[2,128,1280]{2,1,0:T(8,128)(2,1)S(1)} %pad_maximum_fusion.2), channel_id=1, source_target_pairs={{0,96},{8,104},{16,112},{24,120},{32,0},{40,8},{48,16},{56,24},{64... | collective-permute-start | bytes 1966088 | tf_op jit(solution)/shard_map/ppermute | solution.py:46
  132.2 14.2 %collective-permute-start.29 = (bf16[2,128,1280]{2,1,0:T(8,128)(2,1)S(1)}, bf16[2,128,1280]{2,1,0:T(8,128)(2,1)S(1)}, u32[]{:S(2)}, u32[]{:S(2)}) collective-permute-start(bf16[2,128,1280]{2,1,0:T(8,128)(2,1)S(1)} %pad_maximum_fusion.3), channel_id=1, source_target_pairs={{0,8},{8,16},{16,24},{24,0},{32,40},{40,48},{48,56},{56,32},{64,72... | collective-permute-start | bytes 1966088 | tf_op jit(solution)/shard_map/ppermute | solution.py:46
  134.3 12.9 %collective-permute-start.28 = (bf16[2,128,1280]{2,1,0:T(8,128)(2,1)S(1)}, bf16[2,128,1280]{2,1,0:T(8,128)(2,1)S(1)}, u32[]{:S(2)}, u32[]{:S(2)}) collective-permute-start(bf16[2,128,1280]{2,1,0:T(8,128)(2,1)S(1)} %pad_maximum_fusion.3), channel_id=1, source_target_pairs={{0,24},{8,0},{16,8},{24,16},{32,56},{40,32},{48,40},{56,48},{64,88... | collective-permute-start | bytes 1966088 | tf_op jit(solution)/shard_map/ppermute | solution.py:46
  142.0 9.7 %collective-permute-start.17 = (bf16[128,1280]{1,0:T(8,128)(2,1)S(1)}, bf16[128,1280]{1,0:T(8,128)(2,1)S(1)}, u32[]{:S(2)}, u32[]{:S(2)}) collective-permute-start(bf16[128,1280]{1,0:T(8,128)(2,1)S(1)} %slice_bitcast_fusion.10), channel_id=1, source_target_pairs={{0,96},{8,104},{16,112},{24,120},{32,0},{40,8},{48,16},{56,24},{64... | collective-permute-start | bytes 983048 | tf_op jit(solution)/shard_map/ppermute | solution.py:46
  147.3 7.6 %collective-permute-start.31 = (bf16[128,1280]{1,0:T(8,128)(2,1)S(1)}, bf16[128,1280]{1,0:T(8,128)(2,1)S(1)}, u32[]{:S(2)}, u32[]{:S(2)}) collective-permute-start(bf16[128,1280]{1,0:T(8,128)(2,1)S(1)} %slice_bitcast_fusion.2), channel_id=1, source_target_pairs={{0,24},{8,0},{16,8},{24,16},{32,56},{40,32},{48,40},{56,48},{64,88... | collective-permute-start | bytes 983048 | tf_op jit(solution)/shard_map/ppermute | solution.py:46
  148.7 8.7 %collective-permute-start.16 = (bf16[128,1280]{1,0:T(8,128)(2,1)S(1)}, bf16[128,1280]{1,0:T(8,128)(2,1)S(1)}, u32[]{:S(2)}, u32[]{:S(2)}) collective-permute-start(bf16[128,1280]{1,0:T(8,128)(2,1)S(1)} %get-tuple-element.58), channel_id=1, source_target_pairs={{0,32},{8,40},{16,48},{24,56},{32,64},{40,72},{48,80},{56,88},{64,... | collective-permute-start | bytes 983048 | tf_op jit(solution)/shard_map/ppermute | solution.py:46
  148.8 9.3 %collective-permute-start.30 = (bf16[128,1280]{1,0:T(8,128)(2,1)S(1)}, bf16[128,1280]{1,0:T(8,128)(2,1)S(1)}, u32[]{:S(2)}, u32[]{:S(2)}) collective-permute-start(bf16[128,1280]{1,0:T(8,128)(2,1)S(1)} %get-tuple-element.56), channel_id=1, source_target_pairs={{0,8},{8,16},{16,24},{24,0},{32,40},{40,48},{48,56},{56,32},{64,72... | collective-permute-start | bytes 983048 | tf_op jit(solution)/shard_map/ppermute | solution.py:46
  161.1 6.0 %collective-permute-start.35 = (bf16[64,512]{1,0:T(8,128)(2,1)S(1)}, bf16[64,512]{1,0:T(8,128)(2,1)S(1)}, u32[]{:S(2)}, u32[]{:S(2)}) collective-permute-start(bf16[64,512]{1,0:T(8,128)(2,1)S(1)} %get-tuple-element.62), channel_id=1, source_target_pairs={{0,4},{1,5},{2,6},{3,7},{4,0},{5,1},{6,2},{7,3},{8,12},{9,13},{10,... | collective-permute-start | bytes 196616 | tf_op jit(solution)/shard_map/ppermute | solution.py:46
  (29 other events, 188.0 us)

commit v4 on v3

--- a/solution.py
+++ b/solution.py
@@ -234,7 +234,7 @@
         + [pl.BlockSpec(memory_space=pl.ANY)],
         out_specs=[whole(out) for out in outs],
         out_shape=outs,
-        compiler_params=params(),
+        compiler_params=params(56),
         name="total",
     )(own, left, right, gate, up, later)
 

time: 174 us -> 171 us (0.983)
    unnamed x50 -> x44, local copies, waits for them, and re-layouts: 13.2 us -> 10.2 us
  transfers between devices with their start and end apart: 38 -> 38, of which waited for: 15 -> 15; matrix products, arithmetic and copies ran while one was open for 8% -> 9% of each run, Pallas kernels for 17% -> 18%
where the time goes in v4:
time: 171 us; the launch traced here: 170 us
  starting transfers between devices  67.7 us (40%)
  waiting for transfers between devices  40.5 us (24%)
  Pallas kernels  34.2 us (20%)
  local copies, waits for them, and re-layouts  13.6 us (8%)
  matrix products  10.6 us (6%)
  other arithmetic  2.14 us (1%)
    ppermute x36, starting transfers between devices, send(): return lax.ppermute(value, axis, pairs)  53.5 us
    ppermute x36, waiting for transfers between devices, send(): return lax.ppermute(value, axis, pairs)  31.9 us
    pallas_call x2, Pallas kernels, products(): pl.pallas_call(products_kernel, grid=(cols // BLOCK,), in_specs=[pl.Block...  12.3 us
    dot_general x28, matrix products, dot(): return jnp.dot(a, b, preferred_element_type=F32)  10.6 us
    unnamed x44, local copies, waits for them, and re-layouts  10.2 us
    all_to_all x1, starting transfers between devices, local(): att = lax.all_to_all(att, ('gx', 'gy'), 0, 0)  9.93 us
    all_to_all x1, waiting for transfers between devices, local(): att = lax.all_to_all(att, ('gx', 'gy'), 0, 0)  8.63 us
    pallas_call x1, Pallas kernels, attend(): pl.pallas_call(functools.partial(attend_kernel, width=width, q_cols=q_col...  7.03 us
  transfers between devices with their start and end apart: 38, of which 15 were waited for; matrix products, arithmetic and copies ran while one was open for 9% of the time, Pallas kernels for 18%

profile of v4, /device:TPU:0, one launch (start us, length us, event | category | flops | bytes accessed | tf_op | source)
XLA Modules:
  0.0 170.1 jit_solution(9788315635723765365)
XLA Ops:
  2.3 2.7 %collective-permute-start.1 = (bf16[64,512]{1,0:T(8,128)(2,1)}, bf16[64,512]{1,0:T(8,128)(2,1)S(1)}, u32[]{:S(2)}, u32[]{:S(2)}) collective-permute-start(bf16[64,512]{1,0:T(8,128)(2,1)} %param.9), channel_id=1, source_target_pairs={{0,4},{1,5},{2,6},{3,7},{4,0},{5,1},{6,2},{7,3},{8,12},{9,13},{10,... | collective-permute-start | bytes 196616 | tf_op jit(solution)/shard_map/ppermute | solution.py:46
  6.5 2.8 %fusion.71 = bf16[8,4096]{1,0:T(8,128)(2,1)S(1)} fusion(bf16[512,4096]{1,0:T(8,128)(2,1)} %up.3), kind=kOutput, calls=%fused_computation.129 | convolution fusion | flops 33554432 | bytes 4259840 | tf_op jit(solution)/shard_map/dot_general | solution.py:70
  12.9 2.8 %queries.1.later = bf16[128,4,1792]{2,1,0:T(4,128)(2,1)} custom-call(s32[4]{0:T(128)S(1)} %pad_add_fusion.place, bf16[512,512]{1,0:T(8,128)(2,1)S(1)} %get-tuple-element.29.rows, bf16[512,1024]{1,0:T(8,128)(2,1)S(1)} %copy-done.4, bf16[512,64]{1,0:T(8,128)(2,1)S(1)} %copy.19.keyval, bf16[8,4,640]{2,1,0:T(4,128)(2,1)S(1)} %pad_maximum_fusion.7.riders, ...), custom_call_target="tpu_custom_call" | custom-call | tf_op jit(solution)/shard_map/queries/pallas_call | solution.py:152
  15.7 9.9 %all-to-all-start = ((bf16[128,4,1792]{2,1,0:T(4,128)(2,1)}), bf16[128,4,1792]{2,1,0:T(4,128)(2,1)S(1)}, u32[]{:S(2)}, u32[]{:S(2)}) async-start(bf16[128,4,1792]{2,1,0:T(4,128)(2,1)} %queries.1.later), calls=%async_computation | async-start | bytes 3670016 | tf_op jit(solution)/shard_map/all_to_all | solution.py:402
  25.7 6.1 %products.2 = (bf16[2,128,2048]{2,1,0:T(8,128)(2,1)}, bf16[2,128,2048]{2,1,0:T(8,128)(2,1)}, bf16[128,2048]{1,0:T(8,128)(2,1)}, bf16[128,2048]{1,0:T(8,128)(2,1)}, bf16[2,128,2048]{2,1,0:T(8,128)(2,1)}) custom-call(bf16[512,512]{1,0:T(8,128)(2,1)} %copy-done.5, bf16[512,4096]{1,0:T(8,128)(2,1)} %gate.3, bf16[512,4096]{1,0:T(8,128)(2,1)} %up.3, ...), custom_call_target="tpu_custom_call" | custom-call | tf_op jit(solution)/shard_map/products/pallas_call | solution.py:181
  32.9 2.2 %collective-permute-start.5 = (bf16[2,128,2048]{2,1,0:T(8,128)(2,1)}, bf16[2,128,2048]{2,1,0:T(8,128)(2,1)}, u32[]{:S(2)}, u32[]{:S(2)}) collective-permute-start(bf16[2,128,2048]{2,1,0:T(8,128)(2,1)} %get-tuple-element.33), channel_id=1, source_target_pairs={{0,96},{8,104},{16,112},{24,120},{32,0},{40,8},{48,16},{56,24},{64... | collective-permute-start | bytes 3145736 | tf_op jit(solution)/shard_map/ppermute | solution.py:46
  35.1 6.2 %products.3 = (bf16[2,128,2048]{2,1,0:T(8,128)(2,1)}, bf16[2,128,2048]{2,1,0:T(8,128)(2,1)}, bf16[128,2048]{1,0:T(8,128)(2,1)}, bf16[128,2048]{1,0:T(8,128)(2,1)}, bf16[2,128,2048]{2,1,0:T(8,128)(2,1)}) custom-call(bf16[512,512]{1,0:T(8,128)(2,1)} %copy-done.10, bf16[512,4096]{1,0:T(8,128)(2,1)} %gate.3, bf16[512,4096]{1,0:T(8,128)(2,1)} %up.3, ...), custom_call_target="tpu_custom_call" | custom-call | tf_op jit(solution)/shard_map/products/pallas_call | solution.py:181
  42.5 2.0 %collective-permute-start.19 = (bf16[2,128,2048]{2,1,0:T(8,128)(2,1)}, bf16[2,128,2048]{2,1,0:T(8,128)(2,1)}, u32[]{:S(2)}, u32[]{:S(2)}) collective-permute-start(bf16[2,128,2048]{2,1,0:T(8,128)(2,1)} %get-tuple-element.46), channel_id=1, source_target_pairs={{0,24},{8,0},{16,8},{24,16},{32,56},{40,32},{48,40},{56,48},{64,88... | collective-permute-start | bytes 3145736 | tf_op jit(solution)/shard_map/ppermute | solution.py:46
  44.6 8.6 %all-to-all-done.come = bf16[128,4,1792]{2,1,0:T(4,128)(2,1)S(1)} async-done(((bf16[128,4,1792]{2,1,0:T(4,128)(2,1)}), bf16[128,4,1792]{2,1,0:T(4,128)(2,1)S(1)}, u32[]{:S(2)}, u32[]{:S(2)}) %all-to-all-start) | async-done | bytes 1835040 | tf_op jit(solution)/shard_map/all_to_all | solution.py:402
  53.3 2.2 %copy-done = bf16[4,2048,256]{2,1,0:T(8,128)(2,1)S(1)} copy-done((bf16[4,2048,256]{2,1,0:T(8,128)(2,1)S(1)}, bf16[4,2048,256]{2,1,0:T(8,128)(2,1)}, u32[]{:S(2)}) %copy-start) | copy-done | bytes 4194328
  55.4 2.2 %copy-done.1 = bf16[4,2048,256]{2,1,0:T(8,128)(2,1)S(1)} copy-done((bf16[4,2048,256]{2,1,0:T(8,128)(2,1)S(1)}, bf16[4,2048,256]{2,1,0:T(8,128)(2,1)}, u32[]{:S(2)}) %copy-start.1) | copy-done | bytes 4194328
  58.9 7.0 %attend.1 = (bf16[8,24,1024]{2,1,0:T(8,128)(2,1)}, bf16[4,1,512]{2,1,0:T(2,128)(2,1)S(1)}) custom-call(bf16[128,4,1792]{2,1,0:T(4,128)(2,1)S(1)} %all-to-all-done.come, f32[2,128]{1,0:T(2,128)S(1)} %pad_maximum_fusion.8.turn, bf16[4,2048,256]{2,1,0:T(8,128)(2,1)S(1)} %copy-done, bf16[4,2048,256]{2,1,0:T(8,128)(2,1)S(1)} %copy-done.1, ...), custom_call_target="tpu_custom_call" | custom-call | tf_op jit(solution)/shard_map/attend/pallas_call | solution.py:359
  65.9 4.2 %all-to-all-start.1 = ((bf16[8,24,1024]{2,1,0:T(8,128)(2,1)}), bf16[8,24,1024]{2,1,0:T(8,128)(2,1)}, u32[]{:S(2)}, u32[]{:S(2)}) async-start(bf16[8,24,1024]{2,1,0:T(8,128)(2,1)} %get-tuple-element.38.later), calls=%async_computation.1 | async-start | bytes 786432 | tf_op jit(solution)/shard_map/all_to_all | solution.py:414
  73.0 2.3 %second.2 = (bf16[128,2048]{1,0:T(8,128)(2,1)}, bf16[128,2048]{1,0:T(8,128)(2,1)}) custom-call(bf16[2,128,2048]{2,1,0:T(8,128)(2,1)} %collective-permute-done.4.left, bf16[2,128,2048]{2,1,0:T(8,128)(2,1)} %collective-permute-done.5.right, bf16[128,2048]{1,0:T(8,128)(2,1)S(1)} %copy-done.8, bf16[128,2048]{1,0:T(8,128)(2,1)S(1)} %copy-done.9, ...), custom_call_target="tpu_custom_call" | custom-call | tf_op jit(solution)/shard_map/second/pallas_call | solution.py:209
  75.7 2.8 %collective-permute-start.7 = (bf16[128,2048]{1,0:T(8,128)(2,1)}, bf16[128,2048]{1,0:T(8,128)(2,1)}, u32[]{:S(2)}, u32[]{:S(2)}) collective-permute-start(bf16[128,2048]{1,0:T(8,128)(2,1)} %get-tuple-element.40), channel_id=1, source_target_pairs={{0,96},{8,104},{16,112},{24,120},{32,0},{40,8},{48,16},{56,24},{64... | collective-permute-start | bytes 1572872 | tf_op jit(solution)/shard_map/ppermute | solution.py:46
  78.6 2.4 %second.3 = (bf16[128,2048]{1,0:T(8,128)(2,1)}, bf16[128,2048]{1,0:T(8,128)(2,1)S(1)}) custom-call(bf16[2,128,2048]{2,1,0:T(8,128)(2,1)S(1)} %collective-permute-done.18.left, bf16[2,128,2048]{2,1,0:T(8,128)(2,1)} %collective-permute-done.19.right, bf16[128,2048]{1,0:T(8,128)(2,1)S(1)} %copy-done.6, bf16[128,2048]{1,0:T(8,128)(2,1)S(1)} %copy-done.7, ...), custom_call_target="tpu_custom_call" | custom-call | tf_op jit(solution)/shard_map/second/pallas_call | solution.py:209
  81.6 2.6 %collective-permute-start.21 = (bf16[128,2048]{1,0:T(8,128)(2,1)S(1)}, bf16[128,2048]{1,0:T(8,128)(2,1)}, u32[]{:S(2)}, u32[]{:S(2)}) collective-permute-start(bf16[128,2048]{1,0:T(8,128)(2,1)S(1)} %get-tuple-element.50), channel_id=1, source_target_pairs={{0,24},{8,0},{16,8},{24,16},{32,56},{40,32},{48,40},{56,48},{64,88... | collective-permute-start | bytes 1572872 | tf_op jit(solution)/shard_map/ppermute | solution.py:46
  85.8 4.8 %collective-permute-done.6.gate = bf16[128,2048]{1,0:T(8,128)(2,1)S(1)} collective-permute-done((bf16[128,2048]{1,0:T(8,128)(2,1)}, bf16[128,2048]{1,0:T(8,128)(2,1)S(1)}, u32[]{:S(2)}, u32[]{:S(2)}) %collective-permute-start.6) | collective-permute-done | bytes 524320 | tf_op jit(solution)/shard_map/ppermute | solution.py:46
  91.5 2.9 %total.2 = (bf16[2,32,2048]{2,1,0:T(8,128)(2,1)}, bf16[2,32,2048]{2,1,0:T(8,128)(2,1)}, bf16[2,32,2048]{2,1,0:T(8,128)(2,1)}, bf16[2,32,2048]{2,1,0:T(8,128)(2,1)}) custom-call(bf16[2,128,2048]{2,1,0:T(8,128)(2,1)} %get-tuple-element.31.later.own, bf16[2,128,2048]{2,1,0:T(8,128)(2,1)} %collective-permute-done.4.left, ...), custom_call_target="tpu_custom_call" | custom-call | tf_op jit(solution)/shard_map/total/pallas_call | solution.py:230
  96.1 2.6 %collective-permute-start.9 = (bf16[2,32,2048]{2,1,0:T(8,128)(2,1)}, bf16[2,32,2048]{2,1,0:T(8,128)(2,1)S(1)}, u32[]{:S(2)}, u32[]{:S(2)}) collective-permute-start(bf16[2,32,2048]{2,1,0:T(8,128)(2,1)} %get-tuple-element.43), channel_id=1, source_target_pairs={{0,24},{8,0},{16,8},{24,16},{32,56},{40,32},{48,40},{56,48},{64,88... | collective-permute-start | bytes 786440 | tf_op jit(solution)/shard_map/ppermute | solution.py:46
  99.7 3.0 %total.3 = (bf16[2,32,2048]{2,1,0:T(8,128)(2,1)}, bf16[2,32,2048]{2,1,0:T(8,128)(2,1)}, bf16[2,32,2048]{2,1,0:T(8,128)(2,1)}, bf16[2,32,2048]{2,1,0:T(8,128)(2,1)}) custom-call(bf16[2,128,2048]{2,1,0:T(8,128)(2,1)} %get-tuple-element.37.later.own, bf16[2,128,2048]{2,1,0:T(8,128)(2,1)} %copy-done.3, bf16[2,128,2048]{2,1,0:T(8,128)(2,1)} %collective-permute-done.19.right, ...), custom_call_target="tpu_custom_call" | custom-call | tf_op jit(solution)/shard_map/total/pallas_call | solution.py:230
  103.9 3.3 %collective-permute-start.23 = (bf16[2,32,2048]{2,1,0:T(8,128)(2,1)}, bf16[2,32,2048]{2,1,0:T(8,128)(2,1)S(1)}, u32[]{:S(2)}, u32[]{:S(2)}) collective-permute-start(bf16[2,32,2048]{2,1,0:T(8,128)(2,1)} %get-tuple-element.53), channel_id=1, source_target_pairs={{0,96},{8,104},{16,112},{24,120},{32,0},{40,8},{48,16},{56,24},{64... | collective-permute-start | bytes 786440 | tf_op jit(solution)/shard_map/ppermute | solution.py:46
  111.7 3.2 %collective-permute-start.12 = (bf16[2,32,1280]{2,1,0:T(8,128)(2,1)S(1)}, bf16[2,32,1280]{2,1,0:T(8,128)(2,1)S(1)}, u32[]{:S(2)}, u32[]{:S(2)}) collective-permute-start(bf16[2,32,1280]{2,1,0:T(8,128)(2,1)S(1)} %hidden.2), channel_id=1, source_target_pairs={{0,16},{8,24},{16,0},{24,8},{32,48},{40,56},{48,32},{56,40},{64,80... | collective-permute-start | bytes 491528 | tf_op jit(solution)/shard_map/ppermute | solution.py:46
  120.1 3.1 %collective-permute-start.26 = (bf16[2,32,1280]{2,1,0:T(8,128)(2,1)S(1)}, bf16[2,32,1280]{2,1,0:T(8,128)(2,1)S(1)}, u32[]{:S(2)}, u32[]{:S(2)}) collective-permute-start(bf16[2,32,1280]{2,1,0:T(8,128)(2,1)S(1)} %hidden.3), channel_id=1, source_target_pairs={{0,64},{8,72},{16,80},{24,88},{32,96},{40,104},{48,112},{56,120},{... | collective-permute-start | bytes 491528 | tf_op jit(solution)/shard_map/ppermute | solution.py:46
  123.3 2.1 %collective-permute-start.15 = (bf16[2,128,1280]{2,1,0:T(8,128)(2,1)S(1)}, bf16[2,128,1280]{2,1,0:T(8,128)(2,1)S(1)}, u32[]{:S(2)}, u32[]{:S(2)}) collective-permute-start(bf16[2,128,1280]{2,1,0:T(8,128)(2,1)S(1)} %pad_maximum_fusion.2), channel_id=1, source_target_pairs={{0,32},{8,40},{16,48},{24,56},{32,64},{40,72},{48,80},{56,88},{64,... | collective-permute-start | bytes 1966088 | tf_op jit(solution)/shard_map/ppermute | solution.py:46
  126.9 5.0 %collective-permute-done.26 = bf16[2,32,1280]{2,1,0:T(8,128)(2,1)S(1)} collective-permute-done((bf16[2,32,1280]{2,1,0:T(8,128)(2,1)S(1)}, bf16[2,32,1280]{2,1,0:T(8,128)(2,1)S(1)}, u32[]{:S(2)}, u32[]{:S(2)}) %collective-permute-start.26) | collective-permute-done | bytes 163872 | tf_op jit(solution)/shard_map/ppermute | solution.py:46
  132.7 2.5 %collective-permute-start.28 = (bf16[2,128,1280]{2,1,0:T(8,128)(2,1)S(1)}, bf16[2,128,1280]{2,1,0:T(8,128)(2,1)S(1)}, u32[]{:S(2)}, u32[]{:S(2)}) collective-permute-start(bf16[2,128,1280]{2,1,0:T(8,128)(2,1)S(1)} %pad_maximum_fusion.3), channel_id=1, source_target_pairs={{0,24},{8,0},{16,8},{24,16},{32,56},{40,32},{48,40},{56,48},{64,88... | collective-permute-start | bytes 1966088 | tf_op jit(solution)/shard_map/ppermute | solution.py:46
  137.0 5.5 %collective-permute-done.14 = bf16[2,128,1280]{2,1,0:T(8,128)(2,1)S(1)} collective-permute-done((bf16[2,128,1280]{2,1,0:T(8,128)(2,1)S(1)}, bf16[2,128,1280]{2,1,0:T(8,128)(2,1)S(1)}, u32[]{:S(2)}, u32[]{:S(2)}) %collective-permute-start.14) | collective-permute-done | bytes 655392 | tf_op jit(solution)/shard_map/ppermute | solution.py:46
  150.7 2.5 %collective-permute-done.31 = bf16[128,1280]{1,0:T(8,128)(2,1)S(1)} collective-permute-done((bf16[128,1280]{1,0:T(8,128)(2,1)S(1)}, bf16[128,1280]{1,0:T(8,128)(2,1)S(1)}, u32[]{:S(2)}, u32[]{:S(2)}) %collective-permute-start.31) | collective-permute-done | bytes 327712 | tf_op jit(solution)/shard_map/ppermute | solution.py:46
  153.7 2.2 %collective-permute-done.16 = bf16[128,1280]{1,0:T(8,128)(2,1)S(1)} collective-permute-done((bf16[128,1280]{1,0:T(8,128)(2,1)S(1)}, bf16[128,1280]{1,0:T(8,128)(2,1)S(1)}, u32[]{:S(2)}, u32[]{:S(2)}) %collective-permute-start.16) | collective-permute-done | bytes 327712 | tf_op jit(solution)/shard_map/ppermute | solution.py:46
  159.6 3.1 %collective-permute-start.35 = (bf16[64,512]{1,0:T(8,128)(2,1)S(1)}, bf16[64,512]{1,0:T(8,128)(2,1)S(1)}, u32[]{:S(2)}, u32[]{:S(2)}) collective-permute-start(bf16[64,512]{1,0:T(8,128)(2,1)S(1)} %get-tuple-element.62), channel_id=1, source_target_pairs={{0,4},{1,5},{2,6},{3,7},{4,0},{5,1},{6,2},{7,3},{8,12},{9,13},{10,... | collective-permute-start | bytes 196616 | tf_op jit(solution)/shard_map/ppermute | solution.py:46
  167.0 2.4 %collective-permute-done.33 = bf16[64,512]{1,0:T(8,128)(2,1)S(1)} collective-permute-done((bf16[64,512]{1,0:T(8,128)(2,1)S(1)}, bf16[64,512]{1,0:T(8,128)(2,1)S(1)}, u32[]{:S(2)}, u32[]{:S(2)}) %collective-permute-start.33) | collective-permute-done | bytes 65568 | tf_op jit(solution)/shard_map/ppermute | solution.py:46
  (176 shorter events, 51.3 us)
Async XLA Ops:
  0.7 9.6 %collective-permute-start.2 = (bf16[64,512]{1,0:T(8,128)(2,1)}, bf16[64,512]{1,0:T(8,128)(2,1)S(1)}, u32[]{:S(2)}, u32[]{:S(2)}) collective-permute-start(bf16[64,512]{1,0:T(8,128)(2,1)} %param.9), channel_id=1, source_target_pairs={{0,2},{1,3},{2,4},{3,5},{4,6},{5,7},{6,0},{7,1},{8,10},{9,11},{10,... | collective-permute-start | bytes 196616 | tf_op jit(solution)/shard_map/ppermute | solution.py:46
  2.3 7.9 %collective-permute-start.1 = (bf16[64,512]{1,0:T(8,128)(2,1)}, bf16[64,512]{1,0:T(8,128)(2,1)S(1)}, u32[]{:S(2)}, u32[]{:S(2)}) collective-permute-start(bf16[64,512]{1,0:T(8,128)(2,1)} %param.9), channel_id=1, source_target_pairs={{0,4},{1,5},{2,6},{3,7},{4,0},{5,1},{6,2},{7,3},{8,12},{9,13},{10,... | collective-permute-start | bytes 196616 | tf_op jit(solution)/shard_map/ppermute | solution.py:46
  15.7 37.5 %all-to-all-start = ((bf16[128,4,1792]{2,1,0:T(4,128)(2,1)}), bf16[128,4,1792]{2,1,0:T(4,128)(2,1)S(1)}, u32[]{:S(2)}, u32[]{:S(2)}) async-start(bf16[128,4,1792]{2,1,0:T(4,128)(2,1)} %queries.1.later), calls=%async_computation | async-start | bytes 3670016 | tf_op jit(solution)/shard_map/all_to_all | solution.py:402
  31.7 40.2 %collective-permute-start.4 = (bf16[2,128,2048]{2,1,0:T(8,128)(2,1)}, bf16[2,128,2048]{2,1,0:T(8,128)(2,1)}, u32[]{:S(2)}, u32[]{:S(2)}) collective-permute-start(bf16[2,128,2048]{2,1,0:T(8,128)(2,1)} %get-tuple-element.32), channel_id=1, source_target_pairs={{0,32},{8,40},{16,48},{24,56},{32,64},{40,72},{48,80},{56,88},{64,... | collective-permute-start | bytes 3145736 | tf_op jit(solution)/shard_map/ppermute | solution.py:46
  32.9 39.1 %collective-permute-start.5 = (bf16[2,128,2048]{2,1,0:T(8,128)(2,1)}, bf16[2,128,2048]{2,1,0:T(8,128)(2,1)}, u32[]{:S(2)}, u32[]{:S(2)}) collective-permute-start(bf16[2,128,2048]{2,1,0:T(8,128)(2,1)} %get-tuple-element.33), channel_id=1, source_target_pairs={{0,96},{8,104},{16,112},{24,120},{32,0},{40,8},{48,16},{56,24},{64... | collective-permute-start | bytes 3145736 | tf_op jit(solution)/shard_map/ppermute | solution.py:46
  41.2 37.3 %collective-permute-start.18 = (bf16[2,128,2048]{2,1,0:T(8,128)(2,1)}, bf16[2,128,2048]{2,1,0:T(8,128)(2,1)S(1)}, u32[]{:S(2)}, u32[]{:S(2)}) collective-permute-start(bf16[2,128,2048]{2,1,0:T(8,128)(2,1)} %get-tuple-element.45), channel_id=1, source_target_pairs={{0,8},{8,16},{16,24},{24,0},{32,40},{40,48},{48,56},{56,32},{64,72... | collective-permute-start | bytes 3145736 | tf_op jit(solution)/shard_map/ppermute | solution.py:46
  42.5 36.1 %collective-permute-start.19 = (bf16[2,128,2048]{2,1,0:T(8,128)(2,1)}, bf16[2,128,2048]{2,1,0:T(8,128)(2,1)}, u32[]{:S(2)}, u32[]{:S(2)}) collective-permute-start(bf16[2,128,2048]{2,1,0:T(8,128)(2,1)} %get-tuple-element.46), channel_id=1, source_target_pairs={{0,24},{8,0},{16,8},{24,16},{32,56},{40,32},{48,40},{56,48},{64,88... | collective-permute-start | bytes 3145736 | tf_op jit(solution)/shard_map/ppermute | solution.py:46
  65.9 18.3 %all-to-all-start.1 = ((bf16[8,24,1024]{2,1,0:T(8,128)(2,1)}), bf16[8,24,1024]{2,1,0:T(8,128)(2,1)}, u32[]{:S(2)}, u32[]{:S(2)}) async-start(bf16[8,24,1024]{2,1,0:T(8,128)(2,1)} %get-tuple-element.38.later), calls=%async_computation.1 | async-start | bytes 786432 | tf_op jit(solution)/shard_map/all_to_all | solution.py:414
  75.3 15.3 %collective-permute-start.6 = (bf16[128,2048]{1,0:T(8,128)(2,1)}, bf16[128,2048]{1,0:T(8,128)(2,1)S(1)}, u32[]{:S(2)}, u32[]{:S(2)}) collective-permute-start(bf16[128,2048]{1,0:T(8,128)(2,1)} %get-tuple-element.39.later), channel_id=1, source_target_pairs={{0,32},{8,40},{16,48},{24,56},{32,64},{40,72},{48,80},{56,88},{64,... | collective-permute-start | bytes 1572872 | tf_op jit(solution)/shard_map/ppermute | solution.py:46
  75.7 14.9 %collective-permute-start.7 = (bf16[128,2048]{1,0:T(8,128)(2,1)}, bf16[128,2048]{1,0:T(8,128)(2,1)}, u32[]{:S(2)}, u32[]{:S(2)}) collective-permute-start(bf16[128,2048]{1,0:T(8,128)(2,1)} %get-tuple-element.40), channel_id=1, source_target_pairs={{0,96},{8,104},{16,112},{24,120},{32,0},{40,8},{48,16},{56,24},{64... | collective-permute-start | bytes 1572872 | tf_op jit(solution)/shard_map/ppermute | solution.py:46
  80.9 18.8 %collective-permute-start.20 = (bf16[128,2048]{1,0:T(8,128)(2,1)}, bf16[128,2048]{1,0:T(8,128)(2,1)}, u32[]{:S(2)}, u32[]{:S(2)}) collective-permute-start(bf16[128,2048]{1,0:T(8,128)(2,1)} %get-tuple-element.49), channel_id=1, source_target_pairs={{0,8},{8,16},{16,24},{24,0},{32,40},{40,48},{48,56},{56,32},{64,72... | collective-permute-start | bytes 1572872 | tf_op jit(solution)/shard_map/ppermute | solution.py:46
  81.6 18.1 %collective-permute-start.21 = (bf16[128,2048]{1,0:T(8,128)(2,1)S(1)}, bf16[128,2048]{1,0:T(8,128)(2,1)}, u32[]{:S(2)}, u32[]{:S(2)}) collective-permute-start(bf16[128,2048]{1,0:T(8,128)(2,1)S(1)} %get-tuple-element.50), channel_id=1, source_target_pairs={{0,24},{8,0},{16,8},{24,16},{32,56},{40,32},{48,40},{56,48},{64,88... | collective-permute-start | bytes 1572872 | tf_op jit(solution)/shard_map/ppermute | solution.py:46
  94.4 12.8 %collective-permute-start.8 = (bf16[2,32,2048]{2,1,0:T(8,128)(2,1)}, bf16[2,32,2048]{2,1,0:T(8,128)(2,1)S(1)}, u32[]{:S(2)}, u32[]{:S(2)}) collective-permute-start(bf16[2,32,2048]{2,1,0:T(8,128)(2,1)} %get-tuple-element.42), channel_id=1, source_target_pairs={{0,8},{8,16},{16,24},{24,0},{32,40},{40,48},{48,56},{56,32},{64,72... | collective-permute-start | bytes 786440 | tf_op jit(solution)/shard_map/ppermute | solution.py:46
  96.1 13.4 %collective-permute-start.9 = (bf16[2,32,2048]{2,1,0:T(8,128)(2,1)}, bf16[2,32,2048]{2,1,0:T(8,128)(2,1)S(1)}, u32[]{:S(2)}, u32[]{:S(2)}) collective-permute-start(bf16[2,32,2048]{2,1,0:T(8,128)(2,1)} %get-tuple-element.43), channel_id=1, source_target_pairs={{0,24},{8,0},{16,8},{24,16},{32,56},{40,32},{48,40},{56,48},{64,88... | collective-permute-start | bytes 786440 | tf_op jit(solution)/shard_map/ppermute | solution.py:46
  98.8 10.8 %collective-permute-start.10 = (bf16[2,32,2048]{2,1,0:T(8,128)(2,1)}, bf16[2,32,2048]{2,1,0:T(8,128)(2,1)S(1)}, u32[]{:S(2)}, u32[]{:S(2)}) collective-permute-start(bf16[2,32,2048]{2,1,0:T(8,128)(2,1)} %get-tuple-element.44), channel_id=1, source_target_pairs={{0,16},{8,24},{16,0},{24,8},{32,48},{40,56},{48,32},{56,40},{64,80... | collective-permute-start | bytes 786440 | tf_op jit(solution)/shard_map/ppermute | solution.py:46
  102.7 12.2 %collective-permute-start.22 = (bf16[2,32,2048]{2,1,0:T(8,128)(2,1)}, bf16[2,32,2048]{2,1,0:T(8,128)(2,1)S(1)}, u32[]{:S(2)}, u32[]{:S(2)}) collective-permute-start(bf16[2,32,2048]{2,1,0:T(8,128)(2,1)} %get-tuple-element.52), channel_id=1, source_target_pairs={{0,32},{8,40},{16,48},{24,56},{32,64},{40,72},{48,80},{56,88},{64,... | collective-permute-start | bytes 786440 | tf_op jit(solution)/shard_map/ppermute | solution.py:46
  103.9 13.0 %collective-permute-start.23 = (bf16[2,32,2048]{2,1,0:T(8,128)(2,1)}, bf16[2,32,2048]{2,1,0:T(8,128)(2,1)S(1)}, u32[]{:S(2)}, u32[]{:S(2)}) collective-permute-start(bf16[2,32,2048]{2,1,0:T(8,128)(2,1)} %get-tuple-element.53), channel_id=1, source_target_pairs={{0,96},{8,104},{16,112},{24,120},{32,0},{40,8},{48,16},{56,24},{64... | collective-permute-start | bytes 786440 | tf_op jit(solution)/shard_map/ppermute | solution.py:46
  107.2 9.7 %collective-permute-start.24 = (bf16[2,32,2048]{2,1,0:T(8,128)(2,1)}, bf16[2,32,2048]{2,1,0:T(8,128)(2,1)S(1)}, u32[]{:S(2)}, u32[]{:S(2)}) collective-permute-start(bf16[2,32,2048]{2,1,0:T(8,128)(2,1)} %get-tuple-element.54), channel_id=1, source_target_pairs={{0,64},{8,72},{16,80},{24,88},{32,96},{40,104},{48,112},{56,120},{... | collective-permute-start | bytes 786440 | tf_op jit(solution)/shard_map/ppermute | solution.py:46
  109.8 13.4 %collective-permute-start.13 = (bf16[2,32,1280]{2,1,0:T(8,128)(2,1)S(1)}, bf16[2,32,1280]{2,1,0:T(8,128)(2,1)S(1)}, u32[]{:S(2)}, u32[]{:S(2)}) collective-permute-start(bf16[2,32,1280]{2,1,0:T(8,128)(2,1)S(1)} %hidden.2), channel_id=1, source_target_pairs={{0,8},{8,16},{16,24},{24,0},{32,40},{40,48},{48,56},{56,32},{64,72... | collective-permute-start | bytes 491528 | tf_op jit(solution)/shard_map/ppermute | solution.py:46
  111.7 11.5 %collective-permute-start.12 = (bf16[2,32,1280]{2,1,0:T(8,128)(2,1)S(1)}, bf16[2,32,1280]{2,1,0:T(8,128)(2,1)S(1)}, u32[]{:S(2)}, u32[]{:S(2)}) collective-permute-start(bf16[2,32,1280]{2,1,0:T(8,128)(2,1)S(1)} %hidden.2), channel_id=1, source_target_pairs={{0,16},{8,24},{16,0},{24,8},{32,48},{40,56},{48,32},{56,40},{64,80... | collective-permute-start | bytes 491528 | tf_op jit(solution)/shard_map/ppermute | solution.py:46
  114.9 8.4 %collective-permute-start.11 = (bf16[2,32,1280]{2,1,0:T(8,128)(2,1)S(1)}, bf16[2,32,1280]{2,1,0:T(8,128)(2,1)S(1)}, u32[]{:S(2)}, u32[]{:S(2)}) collective-permute-start(bf16[2,32,1280]{2,1,0:T(8,128)(2,1)S(1)} %hidden.2), channel_id=1, source_target_pairs={{0,24},{8,0},{16,8},{24,16},{32,56},{40,32},{48,40},{56,48},{64,88... | collective-permute-start | bytes 491528 | tf_op jit(solution)/shard_map/ppermute | solution.py:46
  118.1 8.8 %collective-permute-start.27 = (bf16[2,32,1280]{2,1,0:T(8,128)(2,1)S(1)}, bf16[2,32,1280]{2,1,0:T(8,128)(2,1)S(1)}, u32[]{:S(2)}, u32[]{:S(2)}) collective-permute-start(bf16[2,32,1280]{2,1,0:T(8,128)(2,1)S(1)} %hidden.3), channel_id=1, source_target_pairs={{0,32},{8,40},{16,48},{24,56},{32,64},{40,72},{48,80},{56,88},{64,... | collective-permute-start | bytes 491528 | tf_op jit(solution)/shard_map/ppermute | solution.py:46
  120.1 11.8 %collective-permute-start.26 = (bf16[2,32,1280]{2,1,0:T(8,128)(2,1)S(1)}, bf16[2,32,1280]{2,1,0:T(8,128)(2,1)S(1)}, u32[]{:S(2)}, u32[]{:S(2)}) collective-permute-start(bf16[2,32,1280]{2,1,0:T(8,128)(2,1)S(1)} %hidden.3), channel_id=1, source_target_pairs={{0,64},{8,72},{16,80},{24,88},{32,96},{40,104},{48,112},{56,120},{... | collective-permute-start | bytes 491528 | tf_op jit(solution)/shard_map/ppermute | solution.py:46
  123.3 8.6 %collective-permute-start.25 = (bf16[2,32,1280]{2,1,0:T(8,128)(2,1)S(1)}, bf16[2,32,1280]{2,1,0:T(8,128)(2,1)S(1)}, u32[]{:S(2)}, u32[]{:S(2)}) collective-permute-start(bf16[2,32,1280]{2,1,0:T(8,128)(2,1)S(1)} %hidden.3), channel_id=1, source_target_pairs={{0,96},{8,104},{16,112},{24,120},{32,0},{40,8},{48,16},{56,24},{64... | collective-permute-start | bytes 491528 | tf_op jit(solution)/shard_map/ppermute | solution.py:46
  123.3 21.0 %collective-permute-start.15 = (bf16[2,128,1280]{2,1,0:T(8,128)(2,1)S(1)}, bf16[2,128,1280]{2,1,0:T(8,128)(2,1)S(1)}, u32[]{:S(2)}, u32[]{:S(2)}) collective-permute-start(bf16[2,128,1280]{2,1,0:T(8,128)(2,1)S(1)} %pad_maximum_fusion.2), channel_id=1, source_target_pairs={{0,32},{8,40},{16,48},{24,56},{32,64},{40,72},{48,80},{56,88},{64,... | collective-permute-start | bytes 1966088 | tf_op jit(solution)/shard_map/ppermute | solution.py:46
  125.4 17.1 %collective-permute-start.14 = (bf16[2,128,1280]{2,1,0:T(8,128)(2,1)S(1)}, bf16[2,128,1280]{2,1,0:T(8,128)(2,1)S(1)}, u32[]{:S(2)}, u32[]{:S(2)}) collective-permute-start(bf16[2,128,1280]{2,1,0:T(8,128)(2,1)S(1)} %pad_maximum_fusion.2), channel_id=1, source_target_pairs={{0,96},{8,104},{16,112},{24,120},{32,0},{40,8},{48,16},{56,24},{64... | collective-permute-start | bytes 1966088 | tf_op jit(solution)/shard_map/ppermute | solution.py:46
  131.9 13.2 %collective-permute-start.29 = (bf16[2,128,1280]{2,1,0:T(8,128)(2,1)S(1)}, bf16[2,128,1280]{2,1,0:T(8,128)(2,1)S(1)}, u32[]{:S(2)}, u32[]{:S(2)}) collective-permute-start(bf16[2,128,1280]{2,1,0:T(8,128)(2,1)S(1)} %pad_maximum_fusion.3), channel_id=1, source_target_pairs={{0,8},{8,16},{16,24},{24,0},{32,40},{40,48},{48,56},{56,32},{64,72... | collective-permute-start | bytes 1966088 | tf_op jit(solution)/shard_map/ppermute | solution.py:46
  132.7 13.3 %collective-permute-start.28 = (bf16[2,128,1280]{2,1,0:T(8,128)(2,1)S(1)}, bf16[2,128,1280]{2,1,0:T(8,128)(2,1)S(1)}, u32[]{:S(2)}, u32[]{:S(2)}) collective-permute-start(bf16[2,128,1280]{2,1,0:T(8,128)(2,1)S(1)} %pad_maximum_fusion.3), channel_id=1, source_target_pairs={{0,24},{8,0},{16,8},{24,16},{32,56},{40,32},{48,40},{56,48},{64,88... | collective-permute-start | bytes 1966088 | tf_op jit(solution)/shard_map/ppermute | solution.py:46
  142.6 7.9 %collective-permute-start.17 = (bf16[128,1280]{1,0:T(8,128)(2,1)S(1)}, bf16[128,1280]{1,0:T(8,128)(2,1)S(1)}, u32[]{:S(2)}, u32[]{:S(2)}) collective-permute-start(bf16[128,1280]{1,0:T(8,128)(2,1)S(1)} %slice_bitcast_fusion.10), channel_id=1, source_target_pairs={{0,96},{8,104},{16,112},{24,120},{32,0},{40,8},{48,16},{56,24},{64... | collective-permute-start | bytes 983048 | tf_op jit(solution)/shard_map/ppermute | solution.py:46
  146.0 7.1 %collective-permute-start.31 = (bf16[128,1280]{1,0:T(8,128)(2,1)S(1)}, bf16[128,1280]{1,0:T(8,128)(2,1)S(1)}, u32[]{:S(2)}, u32[]{:S(2)}) collective-permute-start(bf16[128,1280]{1,0:T(8,128)(2,1)S(1)} %slice_bitcast_fusion.2), channel_id=1, source_target_pairs={{0,24},{8,0},{16,8},{24,16},{32,56},{40,32},{48,40},{56,48},{64,88... | collective-permute-start | bytes 983048 | tf_op jit(solution)/shard_map/ppermute | solution.py:46
  147.5 8.4 %collective-permute-start.16 = (bf16[128,1280]{1,0:T(8,128)(2,1)S(1)}, bf16[128,1280]{1,0:T(8,128)(2,1)S(1)}, u32[]{:S(2)}, u32[]{:S(2)}) collective-permute-start(bf16[128,1280]{1,0:T(8,128)(2,1)S(1)} %get-tuple-element.58), channel_id=1, source_target_pairs={{0,32},{8,40},{16,48},{24,56},{32,64},{40,72},{48,80},{56,88},{64,... | collective-permute-start | bytes 983048 | tf_op jit(solution)/shard_map/ppermute | solution.py:46
  148.0 8.6 %collective-permute-start.30 = (bf16[128,1280]{1,0:T(8,128)(2,1)S(1)}, bf16[128,1280]{1,0:T(8,128)(2,1)S(1)}, u32[]{:S(2)}, u32[]{:S(2)}) collective-permute-start(bf16[128,1280]{1,0:T(8,128)(2,1)S(1)} %get-tuple-element.56), channel_id=1, source_target_pairs={{0,8},{8,16},{16,24},{24,0},{32,40},{40,48},{48,56},{56,32},{64,72... | collective-permute-start | bytes 983048 | tf_op jit(solution)/shard_map/ppermute | solution.py:46
  (26 other events, 210.8 us)

commit v5 on v4

--- a/solution.py
+++ b/solution.py
@@ -124,7 +124,7 @@
         in_specs=[pl.BlockSpec(memory_space=pltpu.SMEM), VMEM, VMEM],
         out_specs=[VMEM] * 3,
         out_shape=[shape((rows, width))] * 2 + [shape((rows // 4, 4, 128))],
-        compiler_params=params(),
+        compiler_params=params(56),
         name="prepare",
     )(place, strip, other)
 

time: 171 us -> 176 us (1.029)
  local copies, waits for them, and re-layouts: 13.6 us -> 16.8 us
    unnamed x44 -> x50, local copies, waits for them, and re-layouts: 10.2 us -> 13.4 us
  transfers between devices with their start and end apart: 38 -> 38, of which waited for: 15 -> 15; matrix products, arithmetic and copies ran while one was open for 9% -> 9% of each run, Pallas kernels for 18% -> 17%
where the time goes in v5:
time: 176 us; the launch traced here: 175 us
  starting transfers between devices  67.7 us (38%)
  waiting for transfers between devices  40.1 us (23%)
  Pallas kernels  35.6 us (20%)
  local copies, waits for them, and re-layouts  16.8 us (10%)
  matrix products  10.6 us (6%)
  other arithmetic  2.66 us (2%)
    ppermute x36, starting transfers between devices, send(): return lax.ppermute(value, axis, pairs)  53.5 us
    ppermute x36, waiting for transfers between devices, send(): return lax.ppermute(value, axis, pairs)  31.4 us
    unnamed x50, local copies, waits for them, and re-layouts  13.4 us
    pallas_call x2, Pallas kernels, products(): pl.pallas_call(products_kernel, grid=(cols // BLOCK,), in_specs=[pl.Block...  12.2 us
    dot_general x28, matrix products, dot(): return jnp.dot(a, b, preferred_element_type=F32)  10.6 us
    all_to_all x1, starting transfers between devices, local(): att = lax.all_to_all(att, ('gx', 'gy'), 0, 0)  9.93 us
    all_to_all x1, waiting for transfers between devices, local(): att = lax.all_to_all(att, ('gx', 'gy'), 0, 0)  8.7 us
    pallas_call x1, Pallas kernels, attend(): pl.pallas_call(functools.partial(attend_kernel, width=width, q_cols=q_col...  7.01 us
  transfers between devices with their start and end apart: 38, of which 15 were waited for; matrix products, arithmetic and copies ran while one was open for 9% of the time, Pallas kernels for 17%

profile of v5, /device:TPU:0, one launch (start us, length us, event | category | flops | bytes accessed | tf_op | source)
XLA Modules:
  0.0 174.8 jit_solution(2983079049416638122)
XLA Ops:
  2.3 2.7 %collective-permute-start.1 = (bf16[64,512]{1,0:T(8,128)(2,1)}, bf16[64,512]{1,0:T(8,128)(2,1)S(1)}, u32[]{:S(2)}, u32[]{:S(2)}) collective-permute-start(bf16[64,512]{1,0:T(8,128)(2,1)} %param.9), channel_id=1, source_target_pairs={{0,4},{1,5},{2,6},{3,7},{4,0},{5,1},{6,2},{7,3},{8,12},{9,13},{10,... | collective-permute-start | bytes 196616 | tf_op jit(solution)/shard_map/ppermute | solution.py:46
  6.5 2.8 %fusion.71 = bf16[8,4096]{1,0:T(8,128)(2,1)S(1)} fusion(bf16[512,4096]{1,0:T(8,128)(2,1)} %up.3), kind=kOutput, calls=%fused_computation.129 | convolution fusion | flops 33554432 | bytes 4259840 | tf_op jit(solution)/shard_map/dot_general | solution.py:70
  12.6 2.5 %prepare.1 = (bf16[512,512]{1,0:T(8,128)(2,1)}, bf16[512,512]{1,0:T(8,128)(2,1)}, bf16[128,4,128]{2,1,0:T(4,128)(2,1)}) custom-call(s32[4]{0:T(128)} %pad_add_fusion.place, bf16[4,64,512]{2,1,0:T(8,128)(2,1)} %copy-done.17, bf16[4,64,512]{2,1,0:T(8,128)(2,1)} %copy-done.19), custom_call_target="tpu_custom_call" | custom-call | tf_op jit(solution)/shard_map/prepare/pallas_call | solution.py:122
  17.6 2.8 %queries.1.later = bf16[128,4,1792]{2,1,0:T(4,128)(2,1)} custom-call(s32[4]{0:T(128)S(1)} %copy-done.13, bf16[512,512]{1,0:T(8,128)(2,1)S(1)} %copy-done.5, bf16[512,1024]{1,0:T(8,128)(2,1)S(1)} %copy-done.4, bf16[512,64]{1,0:T(8,128)(2,1)S(1)} %copy.19.keyval, bf16[8,4,640]{2,1,0:T(4,128)(2,1)S(1)} %pad_maximum_fusion.7.riders, ...), custom_call_target="tpu_custom_call" | custom-call | tf_op jit(solution)/shard_map/queries/pallas_call | solution.py:152
  20.4 9.9 %all-to-all-start = ((bf16[128,4,1792]{2,1,0:T(4,128)(2,1)}), bf16[128,4,1792]{2,1,0:T(4,128)(2,1)S(1)}, u32[]{:S(2)}, u32[]{:S(2)}) async-start(bf16[128,4,1792]{2,1,0:T(4,128)(2,1)} %queries.1.later), calls=%async_computation | async-start | bytes 3670016 | tf_op jit(solution)/shard_map/all_to_all | solution.py:402
  30.4 6.0 %products.2 = (bf16[2,128,2048]{2,1,0:T(8,128)(2,1)}, bf16[2,128,2048]{2,1,0:T(8,128)(2,1)}, bf16[128,2048]{1,0:T(8,128)(2,1)}, bf16[128,2048]{1,0:T(8,128)(2,1)}, bf16[2,128,2048]{2,1,0:T(8,128)(2,1)}) custom-call(bf16[512,512]{1,0:T(8,128)(2,1)} %get-tuple-element.29.rows, bf16[512,4096]{1,0:T(8,128)(2,1)} %gate.3, bf16[512,4096]{1,0:T(8,128)(2,1)} %up.3, ...), custom_call_target="tpu_custom_call" | custom-call | tf_op jit(solution)/shard_map/products/pallas_call | solution.py:181
  37.6 2.2 %collective-permute-start.5 = (bf16[2,128,2048]{2,1,0:T(8,128)(2,1)}, bf16[2,128,2048]{2,1,0:T(8,128)(2,1)}, u32[]{:S(2)}, u32[]{:S(2)}) collective-permute-start(bf16[2,128,2048]{2,1,0:T(8,128)(2,1)} %get-tuple-element.33), channel_id=1, source_target_pairs={{0,96},{8,104},{16,112},{24,120},{32,0},{40,8},{48,16},{56,24},{64... | collective-permute-start | bytes 3145736 | tf_op jit(solution)/shard_map/ppermute | solution.py:46
  39.7 6.2 %products.3 = (bf16[2,128,2048]{2,1,0:T(8,128)(2,1)}, bf16[2,128,2048]{2,1,0:T(8,128)(2,1)}, bf16[128,2048]{1,0:T(8,128)(2,1)}, bf16[128,2048]{1,0:T(8,128)(2,1)}, bf16[2,128,2048]{2,1,0:T(8,128)(2,1)}) custom-call(bf16[512,512]{1,0:T(8,128)(2,1)} %get-tuple-element.36.rows, bf16[512,4096]{1,0:T(8,128)(2,1)} %gate.3, bf16[512,4096]{1,0:T(8,128)(2,1)} %up.3, ...), custom_call_target="tpu_custom_call" | custom-call | tf_op jit(solution)/shard_map/products/pallas_call | solution.py:181
  49.3 8.7 %all-to-all-done.come = bf16[128,4,1792]{2,1,0:T(4,128)(2,1)S(1)} async-done(((bf16[128,4,1792]{2,1,0:T(4,128)(2,1)}), bf16[128,4,1792]{2,1,0:T(4,128)(2,1)S(1)}, u32[]{:S(2)}, u32[]{:S(2)}) %all-to-all-start) | async-done | bytes 1835040 | tf_op jit(solution)/shard_map/all_to_all | solution.py:402
  58.0 2.2 %copy-done = bf16[4,2048,256]{2,1,0:T(8,128)(2,1)S(1)} copy-done((bf16[4,2048,256]{2,1,0:T(8,128)(2,1)S(1)}, bf16[4,2048,256]{2,1,0:T(8,128)(2,1)}, u32[]{:S(2)}) %copy-start) | copy-done | bytes 4194328
  60.2 2.2 %copy-done.1 = bf16[4,2048,256]{2,1,0:T(8,128)(2,1)S(1)} copy-done((bf16[4,2048,256]{2,1,0:T(8,128)(2,1)S(1)}, bf16[4,2048,256]{2,1,0:T(8,128)(2,1)}, u32[]{:S(2)}) %copy-start.1) | copy-done | bytes 4194328
  63.6 7.0 %attend.1 = (bf16[8,24,1024]{2,1,0:T(8,128)(2,1)}, bf16[4,1,512]{2,1,0:T(2,128)(2,1)S(1)}) custom-call(bf16[128,4,1792]{2,1,0:T(4,128)(2,1)S(1)} %all-to-all-done.come, f32[2,128]{1,0:T(2,128)S(1)} %pad_maximum_fusion.8.turn, bf16[4,2048,256]{2,1,0:T(8,128)(2,1)S(1)} %copy-done, bf16[4,2048,256]{2,1,0:T(8,128)(2,1)S(1)} %copy-done.1, ...), custom_call_target="tpu_custom_call" | custom-call | tf_op jit(solution)/shard_map/attend/pallas_call | solution.py:359
  70.6 4.2 %all-to-all-start.1 = ((bf16[8,24,1024]{2,1,0:T(8,128)(2,1)}), bf16[8,24,1024]{2,1,0:T(8,128)(2,1)}, u32[]{:S(2)}, u32[]{:S(2)}) async-start(bf16[8,24,1024]{2,1,0:T(8,128)(2,1)} %get-tuple-element.38.later), calls=%async_computation.1 | async-start | bytes 786432 | tf_op jit(solution)/shard_map/all_to_all | solution.py:414
  77.7 2.3 %second.2 = (bf16[128,2048]{1,0:T(8,128)(2,1)}, bf16[128,2048]{1,0:T(8,128)(2,1)}) custom-call(bf16[2,128,2048]{2,1,0:T(8,128)(2,1)} %collective-permute-done.4.left, bf16[2,128,2048]{2,1,0:T(8,128)(2,1)} %collective-permute-done.5.right, bf16[128,2048]{1,0:T(8,128)(2,1)S(1)} %copy-done.8, bf16[128,2048]{1,0:T(8,128)(2,1)S(1)} %copy-done.9, ...), custom_call_target="tpu_custom_call" | custom-call | tf_op jit(solution)/shard_map/second/pallas_call | solution.py:209
  80.5 2.8 %collective-permute-start.7 = (bf16[128,2048]{1,0:T(8,128)(2,1)}, bf16[128,2048]{1,0:T(8,128)(2,1)}, u32[]{:S(2)}, u32[]{:S(2)}) collective-permute-start(bf16[128,2048]{1,0:T(8,128)(2,1)} %get-tuple-element.40), channel_id=1, source_target_pairs={{0,96},{8,104},{16,112},{24,120},{32,0},{40,8},{48,16},{56,24},{64... | collective-permute-start | bytes 1572872 | tf_op jit(solution)/shard_map/ppermute | solution.py:46
  83.3 2.3 %second.3 = (bf16[128,2048]{1,0:T(8,128)(2,1)}, bf16[128,2048]{1,0:T(8,128)(2,1)S(1)}) custom-call(bf16[2,128,2048]{2,1,0:T(8,128)(2,1)S(1)} %collective-permute-done.18.left, bf16[2,128,2048]{2,1,0:T(8,128)(2,1)} %collective-permute-done.19.right, bf16[128,2048]{1,0:T(8,128)(2,1)S(1)} %copy-done.6, bf16[128,2048]{1,0:T(8,128)(2,1)S(1)} %copy-done.7, ...), custom_call_target="tpu_custom_call" | custom-call | tf_op jit(solution)/shard_map/second/pallas_call | solution.py:209
  86.3 2.6 %collective-permute-start.21 = (bf16[128,2048]{1,0:T(8,128)(2,1)S(1)}, bf16[128,2048]{1,0:T(8,128)(2,1)}, u32[]{:S(2)}, u32[]{:S(2)}) collective-permute-start(bf16[128,2048]{1,0:T(8,128)(2,1)S(1)} %get-tuple-element.50), channel_id=1, source_target_pairs={{0,24},{8,0},{16,8},{24,16},{32,56},{40,32},{48,40},{56,48},{64,88... | collective-permute-start | bytes 1572872 | tf_op jit(solution)/shard_map/ppermute | solution.py:46
  90.5 4.8 %collective-permute-done.6.gate = bf16[128,2048]{1,0:T(8,128)(2,1)S(1)} collective-permute-done((bf16[128,2048]{1,0:T(8,128)(2,1)}, bf16[128,2048]{1,0:T(8,128)(2,1)S(1)}, u32[]{:S(2)}, u32[]{:S(2)}) %collective-permute-start.6) | collective-permute-done | bytes 524320 | tf_op jit(solution)/shard_map/ppermute | solution.py:46
  96.2 2.9 %total.2 = (bf16[2,32,2048]{2,1,0:T(8,128)(2,1)}, bf16[2,32,2048]{2,1,0:T(8,128)(2,1)}, bf16[2,32,2048]{2,1,0:T(8,128)(2,1)}, bf16[2,32,2048]{2,1,0:T(8,128)(2,1)}) custom-call(bf16[2,128,2048]{2,1,0:T(8,128)(2,1)} %get-tuple-element.31.later.own, bf16[2,128,2048]{2,1,0:T(8,128)(2,1)} %collective-permute-done.4.left, ...), custom_call_target="tpu_custom_call" | custom-call | tf_op jit(solution)/shard_map/total/pallas_call | solution.py:230
  100.8 2.6 %collective-permute-start.9 = (bf16[2,32,2048]{2,1,0:T(8,128)(2,1)}, bf16[2,32,2048]{2,1,0:T(8,128)(2,1)S(1)}, u32[]{:S(2)}, u32[]{:S(2)}) collective-permute-start(bf16[2,32,2048]{2,1,0:T(8,128)(2,1)} %get-tuple-element.43), channel_id=1, source_target_pairs={{0,24},{8,0},{16,8},{24,16},{32,56},{40,32},{48,40},{56,48},{64,88... | collective-permute-start | bytes 786440 | tf_op jit(solution)/shard_map/ppermute | solution.py:46
  104.4 3.0 %total.3 = (bf16[2,32,2048]{2,1,0:T(8,128)(2,1)}, bf16[2,32,2048]{2,1,0:T(8,128)(2,1)}, bf16[2,32,2048]{2,1,0:T(8,128)(2,1)}, bf16[2,32,2048]{2,1,0:T(8,128)(2,1)}) custom-call(bf16[2,128,2048]{2,1,0:T(8,128)(2,1)} %get-tuple-element.37.later.own, bf16[2,128,2048]{2,1,0:T(8,128)(2,1)} %copy-done.3, bf16[2,128,2048]{2,1,0:T(8,128)(2,1)} %collective-permute-done.19.right, ...), custom_call_target="tpu_custom_call" | custom-call | tf_op jit(solution)/shard_map/total/pallas_call | solution.py:230
  108.6 3.3 %collective-permute-start.23 = (bf16[2,32,2048]{2,1,0:T(8,128)(2,1)}, bf16[2,32,2048]{2,1,0:T(8,128)(2,1)S(1)}, u32[]{:S(2)}, u32[]{:S(2)}) collective-permute-start(bf16[2,32,2048]{2,1,0:T(8,128)(2,1)} %get-tuple-element.53), channel_id=1, source_target_pairs={{0,96},{8,104},{16,112},{24,120},{32,0},{40,8},{48,16},{56,24},{64... | collective-permute-start | bytes 786440 | tf_op jit(solution)/shard_map/ppermute | solution.py:46
  116.4 3.2 %collective-permute-start.12 = (bf16[2,32,1280]{2,1,0:T(8,128)(2,1)S(1)}, bf16[2,32,1280]{2,1,0:T(8,128)(2,1)S(1)}, u32[]{:S(2)}, u32[]{:S(2)}) collective-permute-start(bf16[2,32,1280]{2,1,0:T(8,128)(2,1)S(1)} %hidden.2), channel_id=1, source_target_pairs={{0,16},{8,24},{16,0},{24,8},{32,48},{40,56},{48,32},{56,40},{64,80... | collective-permute-start | bytes 491528 | tf_op jit(solution)/shard_map/ppermute | solution.py:46
  124.8 3.1 %collective-permute-start.26 = (bf16[2,32,1280]{2,1,0:T(8,128)(2,1)S(1)}, bf16[2,32,1280]{2,1,0:T(8,128)(2,1)S(1)}, u32[]{:S(2)}, u32[]{:S(2)}) collective-permute-start(bf16[2,32,1280]{2,1,0:T(8,128)(2,1)S(1)} %hidden.3), channel_id=1, source_target_pairs={{0,64},{8,72},{16,80},{24,88},{32,96},{40,104},{48,112},{56,120},{... | collective-permute-start | bytes 491528 | tf_op jit(solution)/shard_map/ppermute | solution.py:46
  128.0 2.1 %collective-permute-start.15 = (bf16[2,128,1280]{2,1,0:T(8,128)(2,1)S(1)}, bf16[2,128,1280]{2,1,0:T(8,128)(2,1)S(1)}, u32[]{:S(2)}, u32[]{:S(2)}) collective-permute-start(bf16[2,128,1280]{2,1,0:T(8,128)(2,1)S(1)} %pad_maximum_fusion.2), channel_id=1, source_target_pairs={{0,32},{8,40},{16,48},{24,56},{32,64},{40,72},{48,80},{56,88},{64,... | collective-permute-start | bytes 1966088 | tf_op jit(solution)/shard_map/ppermute | solution.py:46
  131.6 5.0 %collective-permute-done.26 = bf16[2,32,1280]{2,1,0:T(8,128)(2,1)S(1)} collective-permute-done((bf16[2,32,1280]{2,1,0:T(8,128)(2,1)S(1)}, bf16[2,32,1280]{2,1,0:T(8,128)(2,1)S(1)}, u32[]{:S(2)}, u32[]{:S(2)}) %collective-permute-start.26) | collective-permute-done | bytes 163872 | tf_op jit(solution)/shard_map/ppermute | solution.py:46
  137.4 2.5 %collective-permute-start.28 = (bf16[2,128,1280]{2,1,0:T(8,128)(2,1)S(1)}, bf16[2,128,1280]{2,1,0:T(8,128)(2,1)S(1)}, u32[]{:S(2)}, u32[]{:S(2)}) collective-permute-start(bf16[2,128,1280]{2,1,0:T(8,128)(2,1)S(1)} %pad_maximum_fusion.3), channel_id=1, source_target_pairs={{0,24},{8,0},{16,8},{24,16},{32,56},{40,32},{48,40},{56,48},{64,88... | collective-permute-start | bytes 1966088 | tf_op jit(solution)/shard_map/ppermute | solution.py:46
  141.7 5.5 %collective-permute-done.14 = bf16[2,128,1280]{2,1,0:T(8,128)(2,1)S(1)} collective-permute-done((bf16[2,128,1280]{2,1,0:T(8,128)(2,1)S(1)}, bf16[2,128,1280]{2,1,0:T(8,128)(2,1)S(1)}, u32[]{:S(2)}, u32[]{:S(2)}) %collective-permute-start.14) | collective-permute-done | bytes 655392 | tf_op jit(solution)/shard_map/ppermute | solution.py:46
  155.3 2.5 %collective-permute-done.31 = bf16[128,1280]{1,0:T(8,128)(2,1)S(1)} collective-permute-done((bf16[128,1280]{1,0:T(8,128)(2,1)S(1)}, bf16[128,1280]{1,0:T(8,128)(2,1)S(1)}, u32[]{:S(2)}, u32[]{:S(2)}) %collective-permute-start.31) | collective-permute-done | bytes 327712 | tf_op jit(solution)/shard_map/ppermute | solution.py:46
  158.4 2.2 %collective-permute-done.16 = bf16[128,1280]{1,0:T(8,128)(2,1)S(1)} collective-permute-done((bf16[128,1280]{1,0:T(8,128)(2,1)S(1)}, bf16[128,1280]{1,0:T(8,128)(2,1)S(1)}, u32[]{:S(2)}, u32[]{:S(2)}) %collective-permute-start.16) | collective-permute-done | bytes 327712 | tf_op jit(solution)/shard_map/ppermute | solution.py:46
  164.3 3.1 %collective-permute-start.35 = (bf16[64,512]{1,0:T(8,128)(2,1)S(1)}, bf16[64,512]{1,0:T(8,128)(2,1)S(1)}, u32[]{:S(2)}, u32[]{:S(2)}) collective-permute-start(bf16[64,512]{1,0:T(8,128)(2,1)S(1)} %get-tuple-element.62), channel_id=1, source_target_pairs={{0,4},{1,5},{2,6},{3,7},{4,0},{5,1},{6,2},{7,3},{8,12},{9,13},{10,... | collective-permute-start | bytes 196616 | tf_op jit(solution)/shard_map/ppermute | solution.py:46
  171.7 2.4 %collective-permute-done.33 = bf16[64,512]{1,0:T(8,128)(2,1)S(1)} collective-permute-done((bf16[64,512]{1,0:T(8,128)(2,1)S(1)}, bf16[64,512]{1,0:T(8,128)(2,1)S(1)}, u32[]{:S(2)}, u32[]{:S(2)}) %collective-permute-start.33) | collective-permute-done | bytes 65568 | tf_op jit(solution)/shard_map/ppermute | solution.py:46
  (182 shorter events, 55.7 us)
Async XLA Ops:
  0.7 9.6 %collective-permute-start.2 = (bf16[64,512]{1,0:T(8,128)(2,1)}, bf16[64,512]{1,0:T(8,128)(2,1)S(1)}, u32[]{:S(2)}, u32[]{:S(2)}) collective-permute-start(bf16[64,512]{1,0:T(8,128)(2,1)} %param.9), channel_id=1, source_target_pairs={{0,2},{1,3},{2,4},{3,5},{4,6},{5,7},{6,0},{7,1},{8,10},{9,11},{10,... | collective-permute-start | bytes 196616 | tf_op jit(solution)/shard_map/ppermute | solution.py:46
  2.3 7.9 %collective-permute-start.1 = (bf16[64,512]{1,0:T(8,128)(2,1)}, bf16[64,512]{1,0:T(8,128)(2,1)S(1)}, u32[]{:S(2)}, u32[]{:S(2)}) collective-permute-start(bf16[64,512]{1,0:T(8,128)(2,1)} %param.9), channel_id=1, source_target_pairs={{0,4},{1,5},{2,6},{3,7},{4,0},{5,1},{6,2},{7,3},{8,12},{9,13},{10,... | collective-permute-start | bytes 196616 | tf_op jit(solution)/shard_map/ppermute | solution.py:46
  20.4 37.5 %all-to-all-start = ((bf16[128,4,1792]{2,1,0:T(4,128)(2,1)}), bf16[128,4,1792]{2,1,0:T(4,128)(2,1)S(1)}, u32[]{:S(2)}, u32[]{:S(2)}) async-start(bf16[128,4,1792]{2,1,0:T(4,128)(2,1)} %queries.1.later), calls=%async_computation | async-start | bytes 3670016 | tf_op jit(solution)/shard_map/all_to_all | solution.py:402
  36.4 40.3 %collective-permute-start.4 = (bf16[2,128,2048]{2,1,0:T(8,128)(2,1)}, bf16[2,128,2048]{2,1,0:T(8,128)(2,1)}, u32[]{:S(2)}, u32[]{:S(2)}) collective-permute-start(bf16[2,128,2048]{2,1,0:T(8,128)(2,1)} %get-tuple-element.32), channel_id=1, source_target_pairs={{0,32},{8,40},{16,48},{24,56},{32,64},{40,72},{48,80},{56,88},{64,... | collective-permute-start | bytes 3145736 | tf_op jit(solution)/shard_map/ppermute | solution.py:46
  37.6 39.1 %collective-permute-start.5 = (bf16[2,128,2048]{2,1,0:T(8,128)(2,1)}, bf16[2,128,2048]{2,1,0:T(8,128)(2,1)}, u32[]{:S(2)}, u32[]{:S(2)}) collective-permute-start(bf16[2,128,2048]{2,1,0:T(8,128)(2,1)} %get-tuple-element.33), channel_id=1, source_target_pairs={{0,96},{8,104},{16,112},{24,120},{32,0},{40,8},{48,16},{56,24},{64... | collective-permute-start | bytes 3145736 | tf_op jit(solution)/shard_map/ppermute | solution.py:46
  45.9 37.4 %collective-permute-start.18 = (bf16[2,128,2048]{2,1,0:T(8,128)(2,1)}, bf16[2,128,2048]{2,1,0:T(8,128)(2,1)S(1)}, u32[]{:S(2)}, u32[]{:S(2)}) collective-permute-start(bf16[2,128,2048]{2,1,0:T(8,128)(2,1)} %get-tuple-element.45), channel_id=1, source_target_pairs={{0,8},{8,16},{16,24},{24,0},{32,40},{40,48},{48,56},{56,32},{64,72... | collective-permute-start | bytes 3145736 | tf_op jit(solution)/shard_map/ppermute | solution.py:46
  47.2 36.1 %collective-permute-start.19 = (bf16[2,128,2048]{2,1,0:T(8,128)(2,1)}, bf16[2,128,2048]{2,1,0:T(8,128)(2,1)}, u32[]{:S(2)}, u32[]{:S(2)}) collective-permute-start(bf16[2,128,2048]{2,1,0:T(8,128)(2,1)} %get-tuple-element.46), channel_id=1, source_target_pairs={{0,24},{8,0},{16,8},{24,16},{32,56},{40,32},{48,40},{56,48},{64,88... | collective-permute-start | bytes 3145736 | tf_op jit(solution)/shard_map/ppermute | solution.py:46
  70.6 18.3 %all-to-all-start.1 = ((bf16[8,24,1024]{2,1,0:T(8,128)(2,1)}), bf16[8,24,1024]{2,1,0:T(8,128)(2,1)}, u32[]{:S(2)}, u32[]{:S(2)}) async-start(bf16[8,24,1024]{2,1,0:T(8,128)(2,1)} %get-tuple-element.38.later), calls=%async_computation.1 | async-start | bytes 786432 | tf_op jit(solution)/shard_map/all_to_all | solution.py:414
  80.0 15.3 %collective-permute-start.6 = (bf16[128,2048]{1,0:T(8,128)(2,1)}, bf16[128,2048]{1,0:T(8,128)(2,1)S(1)}, u32[]{:S(2)}, u32[]{:S(2)}) collective-permute-start(bf16[128,2048]{1,0:T(8,128)(2,1)} %get-tuple-element.39.later), channel_id=1, source_target_pairs={{0,32},{8,40},{16,48},{24,56},{32,64},{40,72},{48,80},{56,88},{64,... | collective-permute-start | bytes 1572872 | tf_op jit(solution)/shard_map/ppermute | solution.py:46
  80.5 14.9 %collective-permute-start.7 = (bf16[128,2048]{1,0:T(8,128)(2,1)}, bf16[128,2048]{1,0:T(8,128)(2,1)}, u32[]{:S(2)}, u32[]{:S(2)}) collective-permute-start(bf16[128,2048]{1,0:T(8,128)(2,1)} %get-tuple-element.40), channel_id=1, source_target_pairs={{0,96},{8,104},{16,112},{24,120},{32,0},{40,8},{48,16},{56,24},{64... | collective-permute-start | bytes 1572872 | tf_op jit(solution)/shard_map/ppermute | solution.py:46
  85.6 18.8 %collective-permute-start.20 = (bf16[128,2048]{1,0:T(8,128)(2,1)}, bf16[128,2048]{1,0:T(8,128)(2,1)}, u32[]{:S(2)}, u32[]{:S(2)}) collective-permute-start(bf16[128,2048]{1,0:T(8,128)(2,1)} %get-tuple-element.49), channel_id=1, source_target_pairs={{0,8},{8,16},{16,24},{24,0},{32,40},{40,48},{48,56},{56,32},{64,72... | collective-permute-start | bytes 1572872 | tf_op jit(solution)/shard_map/ppermute | solution.py:46
  86.3 18.1 %collective-permute-start.21 = (bf16[128,2048]{1,0:T(8,128)(2,1)S(1)}, bf16[128,2048]{1,0:T(8,128)(2,1)}, u32[]{:S(2)}, u32[]{:S(2)}) collective-permute-start(bf16[128,2048]{1,0:T(8,128)(2,1)S(1)} %get-tuple-element.50), channel_id=1, source_target_pairs={{0,24},{8,0},{16,8},{24,16},{32,56},{40,32},{48,40},{56,48},{64,88... | collective-permute-start | bytes 1572872 | tf_op jit(solution)/shard_map/ppermute | solution.py:46
  99.1 12.8 %collective-permute-start.8 = (bf16[2,32,2048]{2,1,0:T(8,128)(2,1)}, bf16[2,32,2048]{2,1,0:T(8,128)(2,1)S(1)}, u32[]{:S(2)}, u32[]{:S(2)}) collective-permute-start(bf16[2,32,2048]{2,1,0:T(8,128)(2,1)} %get-tuple-element.42), channel_id=1, source_target_pairs={{0,8},{8,16},{16,24},{24,0},{32,40},{40,48},{48,56},{56,32},{64,72... | collective-permute-start | bytes 786440 | tf_op jit(solution)/shard_map/ppermute | solution.py:46
  100.8 13.4 %collective-permute-start.9 = (bf16[2,32,2048]{2,1,0:T(8,128)(2,1)}, bf16[2,32,2048]{2,1,0:T(8,128)(2,1)S(1)}, u32[]{:S(2)}, u32[]{:S(2)}) collective-permute-start(bf16[2,32,2048]{2,1,0:T(8,128)(2,1)} %get-tuple-element.43), channel_id=1, source_target_pairs={{0,24},{8,0},{16,8},{24,16},{32,56},{40,32},{48,40},{56,48},{64,88... | collective-permute-start | bytes 786440 | tf_op jit(solution)/shard_map/ppermute | solution.py:46
  103.5 10.7 %collective-permute-start.10 = (bf16[2,32,2048]{2,1,0:T(8,128)(2,1)}, bf16[2,32,2048]{2,1,0:T(8,128)(2,1)S(1)}, u32[]{:S(2)}, u32[]{:S(2)}) collective-permute-start(bf16[2,32,2048]{2,1,0:T(8,128)(2,1)} %get-tuple-element.44), channel_id=1, source_target_pairs={{0,16},{8,24},{16,0},{24,8},{32,48},{40,56},{48,32},{56,40},{64,80... | collective-permute-start | bytes 786440 | tf_op jit(solution)/shard_map/ppermute | solution.py:46
  107.4 12.2 %collective-permute-start.22 = (bf16[2,32,2048]{2,1,0:T(8,128)(2,1)}, bf16[2,32,2048]{2,1,0:T(8,128)(2,1)S(1)}, u32[]{:S(2)}, u32[]{:S(2)}) collective-permute-start(bf16[2,32,2048]{2,1,0:T(8,128)(2,1)} %get-tuple-element.52), channel_id=1, source_target_pairs={{0,32},{8,40},{16,48},{24,56},{32,64},{40,72},{48,80},{56,88},{64,... | collective-permute-start | bytes 786440 | tf_op jit(solution)/shard_map/ppermute | solution.py:46
  108.6 13.0 %collective-permute-start.23 = (bf16[2,32,2048]{2,1,0:T(8,128)(2,1)}, bf16[2,32,2048]{2,1,0:T(8,128)(2,1)S(1)}, u32[]{:S(2)}, u32[]{:S(2)}) collective-permute-start(bf16[2,32,2048]{2,1,0:T(8,128)(2,1)} %get-tuple-element.53), channel_id=1, source_target_pairs={{0,96},{8,104},{16,112},{24,120},{32,0},{40,8},{48,16},{56,24},{64... | collective-permute-start | bytes 786440 | tf_op jit(solution)/shard_map/ppermute | solution.py:46
  111.9 9.7 %collective-permute-start.24 = (bf16[2,32,2048]{2,1,0:T(8,128)(2,1)}, bf16[2,32,2048]{2,1,0:T(8,128)(2,1)S(1)}, u32[]{:S(2)}, u32[]{:S(2)}) collective-permute-start(bf16[2,32,2048]{2,1,0:T(8,128)(2,1)} %get-tuple-element.54), channel_id=1, source_target_pairs={{0,64},{8,72},{16,80},{24,88},{32,96},{40,104},{48,112},{56,120},{... | collective-permute-start | bytes 786440 | tf_op jit(solution)/shard_map/ppermute | solution.py:46
  114.5 13.4 %collective-permute-start.13 = (bf16[2,32,1280]{2,1,0:T(8,128)(2,1)S(1)}, bf16[2,32,1280]{2,1,0:T(8,128)(2,1)S(1)}, u32[]{:S(2)}, u32[]{:S(2)}) collective-permute-start(bf16[2,32,1280]{2,1,0:T(8,128)(2,1)S(1)} %hidden.2), channel_id=1, source_target_pairs={{0,8},{8,16},{16,24},{24,0},{32,40},{40,48},{48,56},{56,32},{64,72... | collective-permute-start | bytes 491528 | tf_op jit(solution)/shard_map/ppermute | solution.py:46
  116.4 11.5 %collective-permute-start.12 = (bf16[2,32,1280]{2,1,0:T(8,128)(2,1)S(1)}, bf16[2,32,1280]{2,1,0:T(8,128)(2,1)S(1)}, u32[]{:S(2)}, u32[]{:S(2)}) collective-permute-start(bf16[2,32,1280]{2,1,0:T(8,128)(2,1)S(1)} %hidden.2), channel_id=1, source_target_pairs={{0,16},{8,24},{16,0},{24,8},{32,48},{40,56},{48,32},{56,40},{64,80... | collective-permute-start | bytes 491528 | tf_op jit(solution)/shard_map/ppermute | solution.py:46
  119.6 8.4 %collective-permute-start.11 = (bf16[2,32,1280]{2,1,0:T(8,128)(2,1)S(1)}, bf16[2,32,1280]{2,1,0:T(8,128)(2,1)S(1)}, u32[]{:S(2)}, u32[]{:S(2)}) collective-permute-start(bf16[2,32,1280]{2,1,0:T(8,128)(2,1)S(1)} %hidden.2), channel_id=1, source_target_pairs={{0,24},{8,0},{16,8},{24,16},{32,56},{40,32},{48,40},{56,48},{64,88... | collective-permute-start | bytes 491528 | tf_op jit(solution)/shard_map/ppermute | solution.py:46
  122.8 8.8 %collective-permute-start.27 = (bf16[2,32,1280]{2,1,0:T(8,128)(2,1)S(1)}, bf16[2,32,1280]{2,1,0:T(8,128)(2,1)S(1)}, u32[]{:S(2)}, u32[]{:S(2)}) collective-permute-start(bf16[2,32,1280]{2,1,0:T(8,128)(2,1)S(1)} %hidden.3), channel_id=1, source_target_pairs={{0,32},{8,40},{16,48},{24,56},{32,64},{40,72},{48,80},{56,88},{64,... | collective-permute-start | bytes 491528 | tf_op jit(solution)/shard_map/ppermute | solution.py:46
  124.8 11.8 %collective-permute-start.26 = (bf16[2,32,1280]{2,1,0:T(8,128)(2,1)S(1)}, bf16[2,32,1280]{2,1,0:T(8,128)(2,1)S(1)}, u32[]{:S(2)}, u32[]{:S(2)}) collective-permute-start(bf16[2,32,1280]{2,1,0:T(8,128)(2,1)S(1)} %hidden.3), channel_id=1, source_target_pairs={{0,64},{8,72},{16,80},{24,88},{32,96},{40,104},{48,112},{56,120},{... | collective-permute-start | bytes 491528 | tf_op jit(solution)/shard_map/ppermute | solution.py:46
  127.9 8.6 %collective-permute-start.25 = (bf16[2,32,1280]{2,1,0:T(8,128)(2,1)S(1)}, bf16[2,32,1280]{2,1,0:T(8,128)(2,1)S(1)}, u32[]{:S(2)}, u32[]{:S(2)}) collective-permute-start(bf16[2,32,1280]{2,1,0:T(8,128)(2,1)S(1)} %hidden.3), channel_id=1, source_target_pairs={{0,96},{8,104},{16,112},{24,120},{32,0},{40,8},{48,16},{56,24},{64... | collective-permute-start | bytes 491528 | tf_op jit(solution)/shard_map/ppermute | solution.py:46
  128.0 21.0 %collective-permute-start.15 = (bf16[2,128,1280]{2,1,0:T(8,128)(2,1)S(1)}, bf16[2,128,1280]{2,1,0:T(8,128)(2,1)S(1)}, u32[]{:S(2)}, u32[]{:S(2)}) collective-permute-start(bf16[2,128,1280]{2,1,0:T(8,128)(2,1)S(1)} %pad_maximum_fusion.2), channel_id=1, source_target_pairs={{0,32},{8,40},{16,48},{24,56},{32,64},{40,72},{48,80},{56,88},{64,... | collective-permute-start | bytes 1966088 | tf_op jit(solution)/shard_map/ppermute | solution.py:46
  130.1 17.1 %collective-permute-start.14 = (bf16[2,128,1280]{2,1,0:T(8,128)(2,1)S(1)}, bf16[2,128,1280]{2,1,0:T(8,128)(2,1)S(1)}, u32[]{:S(2)}, u32[]{:S(2)}) collective-permute-start(bf16[2,128,1280]{2,1,0:T(8,128)(2,1)S(1)} %pad_maximum_fusion.2), channel_id=1, source_target_pairs={{0,96},{8,104},{16,112},{24,120},{32,0},{40,8},{48,16},{56,24},{64... | collective-permute-start | bytes 1966088 | tf_op jit(solution)/shard_map/ppermute | solution.py:46
  136.6 13.2 %collective-permute-start.29 = (bf16[2,128,1280]{2,1,0:T(8,128)(2,1)S(1)}, bf16[2,128,1280]{2,1,0:T(8,128)(2,1)S(1)}, u32[]{:S(2)}, u32[]{:S(2)}) collective-permute-start(bf16[2,128,1280]{2,1,0:T(8,128)(2,1)S(1)} %pad_maximum_fusion.3), channel_id=1, source_target_pairs={{0,8},{8,16},{16,24},{24,0},{32,40},{40,48},{48,56},{56,32},{64,72... | collective-permute-start | bytes 1966088 | tf_op jit(solution)/shard_map/ppermute | solution.py:46
  137.4 13.2 %collective-permute-start.28 = (bf16[2,128,1280]{2,1,0:T(8,128)(2,1)S(1)}, bf16[2,128,1280]{2,1,0:T(8,128)(2,1)S(1)}, u32[]{:S(2)}, u32[]{:S(2)}) collective-permute-start(bf16[2,128,1280]{2,1,0:T(8,128)(2,1)S(1)} %pad_maximum_fusion.3), channel_id=1, source_target_pairs={{0,24},{8,0},{16,8},{24,16},{32,56},{40,32},{48,40},{56,48},{64,88... | collective-permute-start | bytes 1966088 | tf_op jit(solution)/shard_map/ppermute | solution.py:46
  147.2 7.9 %collective-permute-start.17 = (bf16[128,1280]{1,0:T(8,128)(2,1)S(1)}, bf16[128,1280]{1,0:T(8,128)(2,1)S(1)}, u32[]{:S(2)}, u32[]{:S(2)}) collective-permute-start(bf16[128,1280]{1,0:T(8,128)(2,1)S(1)} %slice_bitcast_fusion.10), channel_id=1, source_target_pairs={{0,96},{8,104},{16,112},{24,120},{32,0},{40,8},{48,16},{56,24},{64... | collective-permute-start | bytes 983048 | tf_op jit(solution)/shard_map/ppermute | solution.py:46
  150.7 7.1 %collective-permute-start.31 = (bf16[128,1280]{1,0:T(8,128)(2,1)S(1)}, bf16[128,1280]{1,0:T(8,128)(2,1)S(1)}, u32[]{:S(2)}, u32[]{:S(2)}) collective-permute-start(bf16[128,1280]{1,0:T(8,128)(2,1)S(1)} %slice_bitcast_fusion.2), channel_id=1, source_target_pairs={{0,24},{8,0},{16,8},{24,16},{32,56},{40,32},{48,40},{56,48},{64,88... | collective-permute-start | bytes 983048 | tf_op jit(solution)/shard_map/ppermute | solution.py:46
  152.2 8.4 %collective-permute-start.16 = (bf16[128,1280]{1,0:T(8,128)(2,1)S(1)}, bf16[128,1280]{1,0:T(8,128)(2,1)S(1)}, u32[]{:S(2)}, u32[]{:S(2)}) collective-permute-start(bf16[128,1280]{1,0:T(8,128)(2,1)S(1)} %get-tuple-element.58), channel_id=1, source_target_pairs={{0,32},{8,40},{16,48},{24,56},{32,64},{40,72},{48,80},{56,88},{64,... | collective-permute-start | bytes 983048 | tf_op jit(solution)/shard_map/ppermute | solution.py:46
  152.7 8.6 %collective-permute-start.30 = (bf16[128,1280]{1,0:T(8,128)(2,1)S(1)}, bf16[128,1280]{1,0:T(8,128)(2,1)S(1)}, u32[]{:S(2)}, u32[]{:S(2)}) collective-permute-start(bf16[128,1280]{1,0:T(8,128)(2,1)S(1)} %get-tuple-element.56), channel_id=1, source_target_pairs={{0,8},{8,16},{16,24},{24,0},{32,40},{40,48},{48,56},{56,32},{64,72... | collective-permute-start | bytes 983048 | tf_op jit(solution)/shard_map/ppermute | solution.py:46
  (29 other events, 200.2 us)
